TPU v7x, 512 devices: a whole 4x8x8 slice. The times are simulated.
512 devices in a mesh: tm: 128 (over y, x, z_lo), chan: 4 (over z_hi, core).
Axes of the slice: x: 4, y: 8, z: 8 (z_hi: 2, z_lo: 4; z = z_hi * 4 + z_lo), core: 2. Of those that a mesh axis runs over, the one named last changes fastest.
Arguments:
- voltages: bfloat16 [32, 2, 2, 512, 16384], P('chan', None, None, 'tm'), parts along dimension 0, may hold values from -6 to 6
- taps: float32 [4, 16384], replicated, may hold values from -3 to 3
Outputs:
- drift_power: float32 [8, 16, 131072], P('chan', None, 'tm'), parts along dimension 0
There are 4 independent parts, one for each index of `chan`. A program takes and returns all parts, laid end to end along the dimension named above; an argument that names none is the same for every part. Nothing has to cross between parts.
All inputs are finite; a program needn't handle non-finite values.
Results may differ from a plain program's by a relative error of at most 0.0017.
The roundings to bfloat16 on the way count: a program that leaves them out, or rounds other values in their place, can miss the bound.
Values may be sent and summed in bfloat16 or wider, within the bound.
No kernel may reach another device: no remote copies, remote signals or barrier semaphores. Data moves between devices by JAX's collectives and lax.ppermute only.
A program may use at most 64 MiB of HBM per device.

v0:
```python
import math

import jax
import jax.numpy as jnp
from jax import lax
from jax.sharding import PartitionSpec as P

NT = 16


def shifted(value, axis, by):
    peers = lax.axis_size(axis)
    pairs = [(i, i + by) for i in range(peers) if 0 <= i + by < peers]
    return lax.ppermute(value, axis, pairs)


def with_halo(value, sides, width):
    for axis, dim in sides:
        peers, length = (lax.axis_size(axis), value.shape[dim])
        up = [(i, (i + 1) % peers) for i in range(peers - 1)]
        down = [(j, i) for i, j in up]
        last = lax.slice_in_dim(value, length - width, length, axis=dim)
        first = lax.slice_in_dim(value, 0, width, axis=dim)
        before = lax.ppermute(last, axis, up)
        after = lax.ppermute(first, axis, down)
        value = jnp.concatenate([before, value, after], axis=dim)
    return value


def section_table(size):
    index = jnp.arange(size, dtype=jnp.int32)
    product = index[:, None] * index[None, :] % size
    angle = -2.0 * math.pi / size * product.astype(jnp.float32)
    scale = 1.0 / math.sqrt(size)
    real_part = jnp.cos(angle) * scale
    imag_part = jnp.sin(angle) * scale
    top = jnp.stack([real_part, -imag_part], axis=1)
    low = jnp.stack([imag_part, real_part], axis=1)
    return jnp.stack([top, low], axis=0).astype(jnp.bfloat16)


def twiddle_table(size):
    index = jnp.arange(size, dtype=jnp.int32)
    product = index[:, None] * index[None, :]
    angle = -2.0 * math.pi / (size * size) * product.astype(jnp.float32)
    return (jnp.cos(angle), jnp.sin(angle))


def spectra(extended, taps, frames):
    count = taps.shape[0]
    length = taps.shape[1]
    side = math.isqrt(length)
    sample = jnp.arange(length, dtype=jnp.int32)
    shaped = taps * (1.0 - 2.0 * (sample % 2).astype(jnp.float32))
    filtered = shaped[0] * extended[:, :, :, count - 1 : count - 1 + frames, :].astype(jnp.float32)
    for k in range(1, count):
        filtered = filtered + shaped[k] * extended[
            :, :, :, count - 1 - k : count - 1 - k + frames, :
        ].astype(jnp.float32)
    filtered = filtered.astype(jnp.bfloat16)
    shape = filtered.shape
    filtered = filtered.reshape(shape[0], shape[1], shape[2], frames, side, side)
    table = section_table(side)
    first = jnp.einsum("ukvn,abvfnm->abfukm", table, filtered, preferred_element_type=jnp.float32)
    cos_part, sin_part = twiddle_table(side)
    real_part = first[:, :, :, 0]
    imag_part = first[:, :, :, 1]
    turned = jnp.stack(
        [real_part * cos_part - imag_part * sin_part, real_part * sin_part + imag_part * cos_part],
        axis=3,
    ).astype(jnp.bfloat16)
    spectrum = jnp.einsum("ujvm,abfvkm->fabujk", table, turned, preferred_element_type=jnp.float32)
    power = jnp.sum(spectrum * spectrum, axis=(2, 3))
    return power.reshape(frames, shape[0] * length)


def taylor(padded, sense):
    level = padded[:, None, :]
    length = 1
    while level.shape[0] > 1:
        earlier = level[0::2]
        later = level[1::2]
        rows = []
        for drift in range(2 * length):
            half = drift // 2
            move = drift - half
            rows.append(earlier[:, half] + jnp.roll(later[:, half], -sense * move, axis=-1))
        level = jnp.stack(rows, axis=1)
        length = length * 2
    return level[0]


def per_device(voltages, taps):
    count = taps.shape[0]
    frames = voltages.shape[3]
    near = shifted(voltages[:, :, :, frames - (count - 1) :, :], "tm", 1)
    extended = jnp.concatenate([near, voltages], axis=3)
    power = spectra(extended, taps, frames)
    per_step = frames * lax.axis_size("tm") // NT
    owned = lax.all_to_all(
        power.astype(jnp.bfloat16), "tm", split_axis=1, concat_axis=0, tiled=True
    ).astype(power.dtype)
    steps_power = owned.reshape(NT, -1, owned.shape[1]).sum(axis=1) / per_step
    widened = with_halo(steps_power, (("tm", 1),), NT)
    owned_width = steps_power.shape[1]
    rising = taylor(widened, 1)[:, NT : NT + owned_width]
    falling = taylor(widened, -1)[:, NT : NT + owned_width]
    return jnp.stack([rising, falling], axis=0) / NT


def solution(mesh):
    placed = (P("chan", None, None, "tm", None), P())
    return jax.shard_map(
        per_device, mesh=mesh, in_specs=placed, out_specs=P("chan", None, "tm"), check_vma=False
    )
```

profile of v0, /device:TPU:8, one launch (start us, length us, event | category | flops | bytes accessed | tf_op | source)
XLA Modules:
  0.0 188.6 jit_solution(14183298165297724550)
XLA Ops:
  0.0 4.7 %slice.744 = bf16[8,2,2,3,16384]{4,3,2,1,0:T(4,128)(2,1)S(1)} slice(bf16[8,2,2,4,16384]{4,3,2,1,0:T(4,128)(2,1)} %param.2), slice={[0:8], [0:2], [0:2], [1:4], [0:16384]} | slice | bytes 6291456 | tf_op jit(solution)/shard_map/slice | solution.py:96
  4.7 2.3 %copy.247 = bf16[8,2,2,3,16384]{4,0,3,2,1:T(8,128)(2,1)S(1)} copy(bf16[8,2,2,3,16384]{4,3,2,1,0:T(4,128)(2,1)S(1)} %slice.744) | data formatting | bytes 6291456
  7.0 4.5 %collective-permute-start = (bf16[8,2,2,3,16384]{4,0,3,2,1:T(8,128)(2,1)S(1)}, bf16[8,2,2,3,16384]{4,0,3,2,1:T(8,128)(2,1)S(1)}, u32[]{:S(2)}, u32[]{:S(2)}) collective-permute-start(bf16[8,2,2,3,16384]{4,0,3,2,1:T(8,128)(2,1)S(1)} %copy.247), channel_id=1, source_target_pairs={{0,4},{4,8},{8,12},{12,16},{16,20},{20,24},{24,28},{28,32},{32,36}... | collective-permute-start | bytes 9437192 | tf_op jit(solution)/shard_map/ppermute | solution.py:14
  11.5 0.3 fusion.25
  11.8 0.3 negate_convert_fusion
  12.1 0.3 fusion.17
  12.5 0.2 fusion.41
  12.7 72.5 %collective-permute-done = bf16[8,2,2,3,16384]{4,0,3,2,1:T(8,128)(2,1)S(1)} collective-permute-done((bf16[8,2,2,3,16384]{4,0,3,2,1:T(8,128)(2,1)S(1)}, bf16[8,2,2,3,16384]{4,0,3,2,1:T(8,128)(2,1)S(1)}, u32[]{:S(2)}, u32[]{:S(2)}) %collective-permute-start) | collective-permute-done | bytes 3145760 | tf_op jit(solution)/shard_map/ppermute | solution.py:14
  85.1 2.7 %copy.176 = bf16[8,2,2,3,16384]{4,3,2,1,0:T(4,128)(2,1)S(1)} copy(bf16[8,2,2,3,16384]{4,0,3,2,1:T(8,128)(2,1)S(1)} %collective-permute-done) | data formatting | bytes 6291456 | tf_op jit(solution)/shard_map/ppermute | solution.py:14
  87.8 14.5 %add_convert_fusion = bf16[8,2,2,4,16384]{4,3,2,1,0:T(4,128)(2,1)} fusion(bf16[8,2,2,4,16384]{4,3,2,1,0:T(4,128)(2,1)S(1)} %copy-done, bf16[8,2,2,3,16384]{4,3,2,1,0:T(4,128)(2,1)S(1)} %copy.176, f32[16384]{0:T(1024)S(1)} %bitcast.395, f32[16384]{0:T(1024)S(1)} %bitcast.396, f32[16384]{0:T(1024)S(1)} %bitcast.397, f32[16384]{0:T(1024)S(1)} %bitcast.394), kind=kLoop, calls=%fused_computation.6 | loop fusion | flops 44040192 | bytes 11796480 | tf_op jit(solution)/shard_map/convert_element_type | solution.py:60
  102.3 8.5 %reshape.578 = bf16[8,2,2,4,128,128]{5,4,3,2,1,0:T(8,128)(2,1)} reshape(bf16[8,2,2,4,16384]{4,3,2,1,0:T(4,128)(2,1)} %add_convert_fusion) | data formatting | bytes 8388608 | tf_op jit(solution)/shard_map/reshape | solution.py:62
  110.8 3.5 %fusion.8 = f32[8,2,4,2,128,128]{4,5,3,2,1,0:T(8,128)S(1)} fusion(bf16[1,128,2,128]{3,1,2,0:T(8,128)(2,1)S(1)} %get-tuple-element.58, bf16[1,128,2,128]{3,1,2,0:T(8,128)(2,1)S(1)} %get-tuple-element.57, bf16[8,2,2,4,128,128]{5,4,3,2,1,0:T(8,128)(2,1)} %reshape.578), kind=kOutput, calls=%fused_computation.18 | convolution fusion | flops 1074003968 | bytes 12713984 | tf_op jit(solution)/shard_map/ukvn,abvfnm->abfukm/dot_general | solution.py:64
  114.3 1.2 subtract_convert_fusion
  115.5 1.3 fusion
  116.8 0.7 copy.179
  117.5 0.5 convert_element_type.90
  118.0 0.8 copy.180
  118.8 40.4 %all_to_all.10 = bf16[4,128,1024]{2,0,1:T(4,128)(2,1)S(1)} all-to-all(bf16[4,128,1024]{2,0,1:T(4,128)(2,1)S(1)} %copy.180), channel_id=1, replica_groups=mesh['tm'=128,'chan'=4] {'tm'}, dimensions={1} | all-to-all | bytes 2097152 | tf_op jit(solution)/shard_map/all_to_all | solution.py:100
  159.2 1.5 convert_reduce_fusion
  160.7 0.1 bitcast_reduce_fusion
  160.9 3.8 %collective-permute-start.2 = (f32[16,16]{1,0:T(8,128)S(1)}, f32[16,16]{1,0:T(8,128)S(1)}, u32[]{:S(2)}, u32[]{:S(2)}) collective-permute-start(f32[16,16]{1,0:T(8,128)S(1)} %get-tuple-element.11), channel_id=1, source_target_pairs={{4,0},{8,4},{12,8},{16,12},{20,16},{24,20},{28,24},{32,28},{36,32}... | collective-permute-start | bytes 3080 | tf_op jit(solution)/shard_map/ppermute | solution.py:25
  164.7 2.0 %collective-permute-start.1 = (f32[16,16]{1,0:T(8,128)S(1)}, f32[16,16]{1,0:T(8,128)S(1)}, u32[]{:S(2)}, u32[]{:S(2)}) collective-permute-start(f32[16,16]{1,0:T(8,128)S(1)} %get-tuple-element.12), channel_id=1, source_target_pairs={{0,4},{4,8},{8,12},{12,16},{16,20},{20,24},{24,28},{28,32},{32,36}... | collective-permute-start | bytes 3080 | tf_op jit(solution)/shard_map/ppermute | solution.py:24
  166.8 8.3 %collective-permute-done.1 = f32[16,16]{1,0:T(8,128)S(1)} collective-permute-done((f32[16,16]{1,0:T(8,128)S(1)}, f32[16,16]{1,0:T(8,128)S(1)}, u32[]{:S(2)}, u32[]{:S(2)}) %collective-permute-start.1) | collective-permute-done | bytes 1056 | tf_op jit(solution)/shard_map/ppermute | solution.py:24
  175.1 0.1 concatenate.513
  175.4 0.1 maximum_add_fusion
  175.8 0.1 slice_add_fusion
  176.9 0.1 maximum_add_fusion.21
  177.2 0.6 slice.1041
  178.9 0.1 slice_add_fusion.1
  179.3 0.5 slice.955
  180.4 0.1 fusion.43
  180.5 0.1 maximum_add_fusion.14
  180.6 0.6 slice.961
  182.5 0.6 slice.1035
  183.1 0.7 fusion.26
  184.1 0.8 fusion.28
  185.0 0.1 stack.44
  185.2 0.7 constant_dynamic-update-slice_fusion.14
  185.9 0.7 constant_dynamic-update-slice_fusion.13
  186.7 0.1 constant_dynamic-update-slice_fusion.12
  186.7 0.1 constant_dynamic-update-slice_fusion.11
  186.9 0.1 constant_dynamic-update-slice_fusion.9
  187.0 0.1 constant_dynamic-update-slice_fusion.8
  187.3 0.1 constant_dynamic-update-slice_fusion.5
  187.4 0.1 constant_dynamic-update-slice_fusion.4
  187.6 0.1 constant_dynamic-update-slice_fusion.1
  187.7 0.1 constant_dynamic-update-slice_fusion
  187.9 0.7 maximum_multiply_fusion
  (157 shorter events, 5.8 us)
Async XLA Ops:
  4.7 7.6 %copy-start.1 = (f32[4,16384]{1,0:T(4,128)S(1)}, f32[4,16384]{1,0:T(4,128)}, u32[]{:S(2)}) copy-start(f32[4,16384]{1,0:T(4,128)} %param.3) | copy-start | bytes 786436
  7.0 78.1 %collective-permute-start = (bf16[8,2,2,3,16384]{4,0,3,2,1:T(8,128)(2,1)S(1)}, bf16[8,2,2,3,16384]{4,0,3,2,1:T(8,128)(2,1)S(1)}, u32[]{:S(2)}, u32[]{:S(2)}) collective-permute-start(bf16[8,2,2,3,16384]{4,0,3,2,1:T(8,128)(2,1)S(1)} %copy.247), channel_id=1, source_target_pairs={{0,4},{4,8},{8,12},{12,16},{16,20},{20,24},{24,28},{28,32},{32,36}... | collective-permute-start | bytes 9437192 | tf_op jit(solution)/shard_map/ppermute | solution.py:14
  12.4 75.4 %copy-start = (bf16[8,2,2,4,16384]{4,3,2,1,0:T(4,128)(2,1)S(1)}, bf16[8,2,2,4,16384]{4,3,2,1,0:T(4,128)(2,1)}, u32[]{:S(2)}) copy-start(bf16[8,2,2,4,16384]{4,3,2,1,0:T(4,128)(2,1)} %param.2) | copy-start | bytes 12582916
  160.9 5.9 %collective-permute-start.2 = (f32[16,16]{1,0:T(8,128)S(1)}, f32[16,16]{1,0:T(8,128)S(1)}, u32[]{:S(2)}, u32[]{:S(2)}) collective-permute-start(f32[16,16]{1,0:T(8,128)S(1)} %get-tuple-element.11), channel_id=1, source_target_pairs={{4,0},{8,4},{12,8},{16,12},{20,16},{24,20},{28,24},{32,28},{36,32}... | collective-permute-start | bytes 3080 | tf_op jit(solution)/shard_map/ppermute | solution.py:25
  164.7 10.4 %collective-permute-start.1 = (f32[16,16]{1,0:T(8,128)S(1)}, f32[16,16]{1,0:T(8,128)S(1)}, u32[]{:S(2)}, u32[]{:S(2)}) collective-permute-start(f32[16,16]{1,0:T(8,128)S(1)} %get-tuple-element.12), channel_id=1, source_target_pairs={{0,4},{4,8},{8,12},{12,16},{16,20},{20,24},{24,28},{28,32},{32,36}... | collective-permute-start | bytes 3080 | tf_op jit(solution)/shard_map/ppermute | solution.py:24
where the time goes:
time: 189 us
  waiting for transfers between devices  80.8 us (43%)
  blocking collectives  40.4 us (21%)
  local copies, waits for them, and re-layouts  27.5 us (15%)
  other arithmetic  24.1 us (13%)
  starting transfers between devices  10.3 us (5%)
  matrix products  4.8 us (3%)
    ppermute x1, waiting for transfers between devices, shifted(): return lax.ppermute(value, axis, pairs)  72.5 us
    all_to_all x1, blocking collectives, per_device(): lax.all_to_all(power.astype(jnp.bfloat16), 'tm', split_axis=1, concat_axi...  40.4 us
    convert_element_type x1, other arithmetic, spectra(): filtered = filtered.astype(jnp.bfloat16)  14.5 us
    reshape x1, local copies, waits for them, and re-layouts, spectra(): filtered.reshape(shape[0], shape[1], shape[2], frames, side, side)  8.48 us
    ppermute x1, waiting for transfers between devices, with_halo(): before = lax.ppermute(last, axis, up)  8.31 us
    slice x1, local copies, waits for them, and re-layouts, per_device(): near = shifted(voltages[:, :, :, frames - (count - 1):, :], 'tm', 1)  4.7 us
    ppermute x1, starting transfers between devices, shifted(): return lax.ppermute(value, axis, pairs)  4.46 us
    concatenate x97, local copies, waits for them, and re-layouts, taylor(): jnp.roll(later[:, half], -sense * move, axis=-1)  3.82 us
  transfers between devices with their start and end apart: 3, of which 2 were waited for; matrix products, arithmetic and copies ran while one was open for 1% of the time, Pallas kernels for 0%

commit v1 on v0

v1 whole, which is shorter than its diff:
```python
import math

import jax
import jax.numpy as jnp
import ml_dtypes
import numpy as np
from jax import lax
from jax.experimental import pallas as pl
from jax.experimental.pallas import tpu as pltpu
from jax.sharding import PartitionSpec as P

NT = 16
SIDE = 128
BLOCK = 16


def tables(side):
    index = np.arange(side, dtype=np.int64)
    angle = -2.0 * math.pi / side * ((index[:, None] * index[None, :]) % side)
    re = (np.cos(angle) / math.sqrt(side)).astype(ml_dtypes.bfloat16)
    im = (np.sin(angle) / math.sqrt(side)).astype(ml_dtypes.bfloat16)
    fourier = np.block([[re, -im], [im, re]])
    turn = -2.0 * math.pi / (side * side) * (index[:, None] * index[None, :])
    return fourier, np.cos(turn).astype(np.float32), np.sin(turn).astype(np.float32)


def pack_kernel(v_ref, out_ref, rows):
    frames = v_ref.shape[3] // SIDE
    for p in range(2):
        for r in range(2):
            rows[...] = v_ref[0, p, r].astype(jnp.float32)
            for t in range(1, frames):
                out_ref[p, r, t - 1] = rows[pl.ds(t, SIDE, stride=frames), :].astype(jnp.bfloat16)


def chunk_power(v_ref, h_ref, taps_ref, fourier_ref, back_ref, cos_ref, sin_ref, rows, wide, tall):
    frames = v_ref.shape[3] // SIDE
    count = taps_ref.shape[0] // SIDE
    lane = lax.broadcasted_iota(jnp.int32, (BLOCK, SIDE), 1)
    sign = 1.0 - 2.0 * (lane % 2).astype(jnp.float32)
    total = None
    for p in range(2):
        for r in range(2):
            rows[r] = v_ref[0, p, r].astype(jnp.float32)
        for n in range(0, SIDE, BLOCK):
            shaped = [
                taps_ref[pl.ds(count * n + k, BLOCK, stride=count), :] * sign for k in range(count)
            ]
            for r in range(2):
                frame = [h_ref[p, r, t, pl.ds(n, BLOCK), :].astype(jnp.float32) for t in range(count - 1)]
                frame += [rows[r, pl.ds(frames * n + t, BLOCK, stride=frames), :] for t in range(frames)]
                for t in range(frames):
                    value = shaped[0] * frame[t + count - 1]
                    for k in range(1, count):
                        value = value + shaped[k] * frame[t + count - 1 - k]
                    wide[pl.ds(r * SIDE + n, BLOCK), pl.ds(t * SIDE, SIDE)] = value.astype(jnp.bfloat16)
        first = jnp.dot(fourier_ref[...], wide[...], preferred_element_type=jnp.float32)
        cos, sin = cos_ref[...], sin_ref[...]
        for t in range(frames):
            re = first[:SIDE, t * SIDE : (t + 1) * SIDE]
            im = first[SIDE:, t * SIDE : (t + 1) * SIDE]
            tall[pl.ds(t * SIDE, SIDE), pl.ds(0, SIDE)] = (re * cos - im * sin).astype(jnp.bfloat16)
            tall[pl.ds(t * SIDE, SIDE), pl.ds(SIDE, SIDE)] = (re * sin + im * cos).astype(jnp.bfloat16)
        spectrum = jnp.dot(tall[...], back_ref[...], preferred_element_type=jnp.float32)
        square = spectrum * spectrum
        for t in range(frames):
            part = square[t * SIDE : (t + 1) * SIDE]
            part = part[:, :SIDE] + part[:, SIDE:]
            total = part if total is None else total + part
    return total.T


def chunk_kernel(*refs):
    ins, (out_ref,), scratch = refs[:7], refs[7:8], refs[8:]
    out_ref[...] = chunk_power(*ins, *scratch)


def last_kernel(*refs):
    ins, before, out_ref, scratch = refs[:7], refs[7:-4], refs[-4], refs[-3:]
    last = chunk_power(*ins, *scratch)
    each = SIDE // 8
    tiles = []
    for ref in before:
        tiles += [ref[pl.ds(8 * i, 8), :] for i in range(each)]
    tiles += [last[8 * i : 8 * i + 8] for i in range(each)]
    zero = jnp.zeros((8, SIDE), jnp.float32)
    row = lax.broadcasted_iota(jnp.int32, (8, SIDE), 0)
    for d in range(len(tiles)):
        after = tiles[d + 1] if d + 1 < len(tiles) else zero
        prior = tiles[d - 1] if d else zero
        edge = jnp.where(row == 0, after, jnp.where(row == 7, prior, 0.0))
        out_ref[d] = jnp.concatenate([tiles[d], edge], axis=0).astype(jnp.bfloat16)


def tree_kernel(in_ref, out_ref, flat):
    sources = in_ref.shape[0]
    per = sources // NT
    lane = lax.broadcasted_iota(jnp.int32, (16, SIDE), 1)
    steps = []
    for s in range(NT):
        value = in_ref[s * per].astype(jnp.float32)
        for i in range(1, per):
            value = value + in_ref[s * per + i].astype(jnp.float32)
        steps.append(value)

    def moved(value, move, sense):
        if move == 0:
            return value
        if sense > 0:
            here = pltpu.roll(value, SIDE - move, 1)
            return jnp.where(lane < SIDE - move, here, pltpu.roll(here, 15, 0))
        here = pltpu.roll(value, move, 1)
        return jnp.where(lane >= move, here, pltpu.roll(here, 1, 0))

    for which, sense in enumerate((1, -1)):
        level = [[value] for value in steps]
        length = 1
        while len(level) > 1:
            level = [
                [
                    level[j][d // 2] + moved(level[j + 1][d // 2], d - d // 2, sense)
                    for d in range(2 * length)
                ]
                for j in range(0, len(level), 2)
            ]
            length *= 2
        for d in range(NT):
            flat[pl.ds(8 * d, 8), :] = level[0][d][:8]
        for r in range(8):
            out_ref[which, :, pl.ds(r * SIDE, SIDE)] = flat[pl.ds(r, NT, stride=8), :] * (1.0 / (4 * per * NT))


def per_device(voltages, taps):
    channels, _, _, frames, length = voltages.shape
    count = taps.shape[0]
    peers = lax.axis_size("tm")
    fourier, cos, sin = tables(SIDE)
    back = jnp.asarray(np.ascontiguousarray(fourier.T))
    fourier, cos, sin = jnp.asarray(fourier), jnp.asarray(cos), jnp.asarray(sin)
    rows = voltages.reshape(channels, 2, 2, frames, SIDE, SIDE).transpose(0, 1, 2, 4, 3, 5)
    rows = rows.reshape(channels, 2, 2, SIDE * frames, SIDE)
    coefficients = taps.reshape(count, SIDE, SIDE).transpose(1, 0, 2).reshape(SIDE * count, SIDE)
    pairs = [(i, i + 1) for i in range(peers - 1)]

    def block_of(c):
        return pl.BlockSpec((1, 2, 2, SIDE * frames, SIDE), lambda i: (c, 0, 0, 0, 0))

    def whole(shape):
        return pl.BlockSpec(shape, lambda i: (0,) * len(shape))

    halo = (2, 2, count - 1, SIDE, SIDE)
    near = []
    for c in range(channels):
        packed = pl.pallas_call(
            pack_kernel,
            grid=(1,),
            in_specs=[block_of(c)],
            out_specs=whole(halo),
            out_shape=jax.ShapeDtypeStruct(halo, jnp.bfloat16),
            scratch_shapes=[pltpu.VMEM((SIDE * frames, SIDE), jnp.float32)],
            cost_estimate=pl.CostEstimate(flops=1 << 20, bytes_accessed=1 << 20, transcendentals=0),
            name="pack",
        )(rows)
        near.append(lax.ppermute(packed, "tm", pairs))

    constants = [coefficients, fourier, back, cos, sin]
    specs = [whole(value.shape) for value in constants]
    scratch = [
        pltpu.VMEM((2, SIDE * frames, SIDE), jnp.float32),
        pltpu.VMEM((2 * SIDE, frames * SIDE), jnp.bfloat16),
        pltpu.VMEM((frames * SIDE, 2 * SIDE), jnp.bfloat16),
    ]
    cost = pl.CostEstimate(flops=300 << 20, bytes_accessed=2 << 20, transcendentals=0)
    tile = (SIDE, SIDE)
    powers = []
    for c in range(channels - 1):
        powers.append(
            pl.pallas_call(
                chunk_kernel,
                grid=(1,),
                in_specs=[block_of(c), whole(halo)] + specs,
                out_specs=whole(tile),
                out_shape=jax.ShapeDtypeStruct(tile, jnp.float32),
                scratch_shapes=scratch,
                cost_estimate=cost,
                name="chunk",
            )(rows, near[c], *constants)
        )
    sent = (peers, 16, SIDE)
    out = pl.pallas_call(
        last_kernel,
        grid=(1,),
        in_specs=[block_of(channels - 1), whole(halo)] + specs + [whole(tile)] * (channels - 1),
        out_specs=whole(sent),
        out_shape=jax.ShapeDtypeStruct(sent, jnp.bfloat16),
        scratch_shapes=scratch,
        cost_estimate=cost,
        name="last",
    )(rows, near[channels - 1], *constants, *powers)
    owned = lax.all_to_all(out, "tm", split_axis=0, concat_axis=0, tiled=True)
    result = (2, NT, channels * length // peers)
    return pl.pallas_call(
        tree_kernel,
        grid=(1,),
        in_specs=[whole(sent)],
        out_specs=whole(result),
        out_shape=jax.ShapeDtypeStruct(result, jnp.float32),
        scratch_shapes=[pltpu.VMEM((8 * NT, SIDE), jnp.float32)],
        cost_estimate=pl.CostEstimate(flops=1 << 22, bytes_accessed=1 << 20, transcendentals=0),
        name="tree",
    )(owned)


def solution(mesh):
    placed = (P("chan", None, None, "tm", None), P())
    return jax.shard_map(
        per_device, mesh=mesh, in_specs=placed, out_specs=P("chan", None, "tm"), check_vma=False
    )
```

time: 189 us -> 117 us (0.62)
  waiting for transfers between devices: 80.8 us -> 12.5 us
  Pallas kernels: 0 us -> 41.8 us
  other arithmetic: 24.1 us -> 0 us
  local copies, waits for them, and re-layouts: 27.5 us -> 3.76 us
  starting transfers between devices: 10.3 us -> 28.2 us
  blocking collectives: 40.4 us -> 30 us
  matrix products: 4.8 us -> 0 us
    ppermute x3 -> x8, waiting for transfers between devices: 80.8 us -> 12.5 us  [per_device(): near.append(lax.ppermute(packed, 'tm', pairs))]
    pallas_call x0 -> x17, Pallas kernels: none -> 41.8 us  [the longest x7 21.1 us: per_device(): pl.pallas_call(chunk_kernel, grid=(1,), in_specs=[block_of(c), whole(halo...]
    ppermute x3 -> x8, starting transfers between devices: 10.3 us -> 28.2 us  [per_device(): near.append(lax.ppermute(packed, 'tm', pairs))]
    convert_element_type x1 -> x0, other arithmetic: 14.5 us -> none  [spectra(): filtered = filtered.astype(jnp.bfloat16)]
    all_to_all x1, blocking collectives: 40.4 us -> 30 us  [per_device(): owned = lax.all_to_all(out, 'tm', split_axis=0, concat_axis=0, tiled=True)]
    reshape x1 -> x0, local copies, waits for them, and re-layouts: 8.48 us -> none  [spectra(): filtered.reshape(shape[0], shape[1], shape[2], frames, side, side)]
    slice x19 -> x0, local copies, waits for them, and re-layouts: 7.75 us -> none  [the longest x1 4.7 us: per_device(): near = shifted(voltages[:, :, :, frames - (count - 1):, :], 'tm', 1)]
    dot_general x2 -> x0, matrix products: 4.8 us -> none  [the longest x1 3.49 us: spectra(): jnp.einsum('ukvn,abvfnm->abfukm', table, filtered, preferred_element_type...]
  transfers between devices with their start and end apart: 3 -> 8, of which waited for: 2 -> 3; matrix products, arithmetic and copies ran while one was open for 1% -> 0% of each run, Pallas kernels for 0% -> 30%
where the time goes in v1:
time: 117 us; the launch traced here: 116 us
  Pallas kernels  41.8 us (36%)
  blocking collectives  30 us (26%)
  starting transfers between devices  28.2 us (24%)
  waiting for transfers between devices  12.5 us (11%)
  local copies, waits for them, and re-layouts  3.76 us (3%)
    all_to_all x1, blocking collectives, per_device(): owned = lax.all_to_all(out, 'tm', split_axis=0, concat_axis=0, tiled=True)  30 us
    ppermute x8, starting transfers between devices, per_device(): near.append(lax.ppermute(packed, 'tm', pairs))  28.2 us
    pallas_call x7, Pallas kernels, per_device(): pl.pallas_call(chunk_kernel, grid=(1,), in_specs=[block_of(c), whole(halo...  21.1 us
    pallas_call x8, Pallas kernels, per_device(): pl.pallas_call(pack_kernel, grid=(1,), in_specs=[block_of(c)], out_specs=...  15.3 us
    ppermute x8, waiting for transfers between devices, per_device(): near.append(lax.ppermute(packed, 'tm', pairs))  12.5 us
    unnamed x16, local copies, waits for them, and re-layouts  3.76 us
    pallas_call x1, Pallas kernels, per_device(): pl.pallas_call(last_kernel, grid=(1,), in_specs=[block_of(channels - 1),...  3.3 us
  transfers between devices with their start and end apart: 8, of which 3 were waited for; matrix products, arithmetic and copies ran while one was open for 0% of the time, Pallas kernels for 30%

profile of v1, /device:TPU:8, one launch (start us, length us, event | category | flops | bytes accessed | tf_op | source)
XLA Modules:
  0.0 116.4 jit_solution(11952650078761768892)
XLA Ops:
  0.0 1.9 %pack.9 = bf16[2,2,3,128,128]{4,3,2,1,0:T(8,128)(2,1)} custom-call(bf16[8,2,2,512,128]{4,3,2,1,0:T(8,128)(2,1)} %bitcast.10), custom_call_target="tpu_custom_call" | custom-call | flops 1048576 | bytes 1048576 | tf_op jit(solution)/shard_map/pack/pallas_call | solution.py:154
  1.9 4.3 %collective-permute-start.1 = (bf16[2,2,3,128,128]{4,3,2,1,0:T(8,128)(2,1)}, bf16[2,2,3,128,128]{4,3,2,1,0:T(8,128)(2,1)S(1)}, u32[]{:S(2)}, u32[]{:S(2)}) collective-permute-start(bf16[2,2,3,128,128]{4,3,2,1,0:T(8,128)(2,1)} %pack.9), channel_id=1, source_target_pairs={{0,4},{4,8},{8,12},{12,16},{16,20},{20,24},{24,28},{28,32},{32,36}... | collective-permute-start | bytes 1179656 | tf_op jit(solution)/shard_map/ppermute | solution.py:164
  6.2 1.9 %pack.10 = bf16[2,2,3,128,128]{4,3,2,1,0:T(8,128)(2,1)} custom-call(bf16[8,2,2,512,128]{4,3,2,1,0:T(8,128)(2,1)} %bitcast.11), custom_call_target="tpu_custom_call" | custom-call | flops 1048576 | bytes 1048576 | tf_op jit(solution)/shard_map/pack/pallas_call | solution.py:154
  8.1 4.3 %collective-permute-start.2 = (bf16[2,2,3,128,128]{4,3,2,1,0:T(8,128)(2,1)}, bf16[2,2,3,128,128]{4,3,2,1,0:T(8,128)(2,1)S(1)}, u32[]{:S(2)}, u32[]{:S(2)}) collective-permute-start(bf16[2,2,3,128,128]{4,3,2,1,0:T(8,128)(2,1)} %pack.10), channel_id=1, source_target_pairs={{0,4},{4,8},{8,12},{12,16},{16,20},{20,24},{24,28},{28,32},{32,36}... | collective-permute-start | bytes 1179656 | tf_op jit(solution)/shard_map/ppermute | solution.py:164
  12.4 1.9 %pack.11 = bf16[2,2,3,128,128]{4,3,2,1,0:T(8,128)(2,1)} custom-call(bf16[8,2,2,512,128]{4,3,2,1,0:T(8,128)(2,1)} %bitcast.12), custom_call_target="tpu_custom_call" | custom-call | flops 1048576 | bytes 1048576 | tf_op jit(solution)/shard_map/pack/pallas_call | solution.py:154
  14.3 4.3 %collective-permute-start.3 = (bf16[2,2,3,128,128]{4,3,2,1,0:T(8,128)(2,1)}, bf16[2,2,3,128,128]{4,3,2,1,0:T(8,128)(2,1)S(1)}, u32[]{:S(2)}, u32[]{:S(2)}) collective-permute-start(bf16[2,2,3,128,128]{4,3,2,1,0:T(8,128)(2,1)} %pack.11), channel_id=1, source_target_pairs={{0,4},{4,8},{8,12},{12,16},{16,20},{20,24},{24,28},{28,32},{32,36}... | collective-permute-start | bytes 1179656 | tf_op jit(solution)/shard_map/ppermute | solution.py:164
  18.6 1.9 %pack.12 = bf16[2,2,3,128,128]{4,3,2,1,0:T(8,128)(2,1)} custom-call(bf16[8,2,2,512,128]{4,3,2,1,0:T(8,128)(2,1)} %bitcast.13), custom_call_target="tpu_custom_call" | custom-call | flops 1048576 | bytes 1048576 | tf_op jit(solution)/shard_map/pack/pallas_call | solution.py:154
  20.5 1.9 %collective-permute-start.4 = (bf16[2,2,3,128,128]{4,3,2,1,0:T(8,128)(2,1)}, bf16[2,2,3,128,128]{4,3,2,1,0:T(8,128)(2,1)S(1)}, u32[]{:S(2)}, u32[]{:S(2)}) collective-permute-start(bf16[2,2,3,128,128]{4,3,2,1,0:T(8,128)(2,1)} %pack.12), channel_id=1, source_target_pairs={{0,4},{4,8},{8,12},{12,16},{16,20},{20,24},{24,28},{28,32},{32,36}... | collective-permute-start | bytes 1179656 | tf_op jit(solution)/shard_map/ppermute | solution.py:164
  22.4 1.9 %pack.13 = bf16[2,2,3,128,128]{4,3,2,1,0:T(8,128)(2,1)} custom-call(bf16[8,2,2,512,128]{4,3,2,1,0:T(8,128)(2,1)} %bitcast.14), custom_call_target="tpu_custom_call" | custom-call | flops 1048576 | bytes 1048576 | tf_op jit(solution)/shard_map/pack/pallas_call | solution.py:154
  24.3 3.0 %collective-permute-start.5 = (bf16[2,2,3,128,128]{4,3,2,1,0:T(8,128)(2,1)}, bf16[2,2,3,128,128]{4,3,2,1,0:T(8,128)(2,1)S(1)}, u32[]{:S(2)}, u32[]{:S(2)}) collective-permute-start(bf16[2,2,3,128,128]{4,3,2,1,0:T(8,128)(2,1)} %pack.13), channel_id=1, source_target_pairs={{0,4},{4,8},{8,12},{12,16},{16,20},{20,24},{24,28},{28,32},{32,36}... | collective-permute-start | bytes 1179656 | tf_op jit(solution)/shard_map/ppermute | solution.py:164
  27.4 1.9 %pack.14 = bf16[2,2,3,128,128]{4,3,2,1,0:T(8,128)(2,1)} custom-call(bf16[8,2,2,512,128]{4,3,2,1,0:T(8,128)(2,1)} %bitcast.15), custom_call_target="tpu_custom_call" | custom-call | flops 1048576 | bytes 1048576 | tf_op jit(solution)/shard_map/pack/pallas_call | solution.py:154
  29.3 0.0 collective-permute-done.1.refs_1_
  29.3 4.3 %collective-permute-start.6 = (bf16[2,2,3,128,128]{4,3,2,1,0:T(8,128)(2,1)}, bf16[2,2,3,128,128]{4,3,2,1,0:T(8,128)(2,1)S(1)}, u32[]{:S(2)}, u32[]{:S(2)}) collective-permute-start(bf16[2,2,3,128,128]{4,3,2,1,0:T(8,128)(2,1)} %pack.14), channel_id=1, source_target_pairs={{0,4},{4,8},{8,12},{12,16},{16,20},{20,24},{24,28},{28,32},{32,36}... | collective-permute-start | bytes 1179656 | tf_op jit(solution)/shard_map/ppermute | solution.py:164
  33.6 1.9 %pack.15 = bf16[2,2,3,128,128]{4,3,2,1,0:T(8,128)(2,1)} custom-call(bf16[8,2,2,512,128]{4,3,2,1,0:T(8,128)(2,1)} %bitcast.16), custom_call_target="tpu_custom_call" | custom-call | flops 1048576 | bytes 1048576 | tf_op jit(solution)/shard_map/pack/pallas_call | solution.py:154
  35.5 0.0 collective-permute-done.2.refs_1_
  35.5 0.0 copy-start.2
  35.5 4.3 %collective-permute-start.7 = (bf16[2,2,3,128,128]{4,3,2,1,0:T(8,128)(2,1)}, bf16[2,2,3,128,128]{4,3,2,1,0:T(8,128)(2,1)S(1)}, u32[]{:S(2)}, u32[]{:S(2)}) collective-permute-start(bf16[2,2,3,128,128]{4,3,2,1,0:T(8,128)(2,1)} %pack.15), channel_id=1, source_target_pairs={{0,4},{4,8},{8,12},{12,16},{16,20},{20,24},{24,28},{28,32},{32,36}... | collective-permute-start | bytes 1179656 | tf_op jit(solution)/shard_map/ppermute | solution.py:164
  39.8 1.9 %pack.8 = bf16[2,2,3,128,128]{4,3,2,1,0:T(8,128)(2,1)} custom-call(bf16[8,2,2,512,128]{4,3,2,1,0:T(8,128)(2,1)} %bitcast.17), custom_call_target="tpu_custom_call" | custom-call | flops 1048576 | bytes 1048576 | tf_op jit(solution)/shard_map/pack/pallas_call | solution.py:154
  41.7 0.0 copy-done.1
  41.7 0.0 collective-permute-done.3.refs_1_
  41.7 0.0 copy-start.5
  41.7 1.9 %collective-permute-start = (bf16[2,2,3,128,128]{4,3,2,1,0:T(8,128)(2,1)}, bf16[2,2,3,128,128]{4,3,2,1,0:T(8,128)(2,1)S(1)}, u32[]{:S(2)}, u32[]{:S(2)}) collective-permute-start(bf16[2,2,3,128,128]{4,3,2,1,0:T(8,128)(2,1)} %pack.8), channel_id=1, source_target_pairs={{0,4},{4,8},{8,12},{12,16},{16,20},{20,24},{24,28},{28,32},{32,36}... | collective-permute-start | bytes 1179656 | tf_op jit(solution)/shard_map/ppermute | solution.py:164
  43.6 3.0 %chunk.7.refs_7_ = f32[128,128]{1,0:T(8,128)} custom-call(bf16[8,2,2,512,128]{4,3,2,1,0:T(8,128)(2,1)} %bitcast.18, bf16[2,2,3,128,128]{4,3,2,1,0:T(8,128)(2,1)} %copy-done.1, f32[512,128]{1,0:T(8,128)} %bitcast.26, bf16[256,256]{1,0:T(8,128)(2,1)} %constant.9.clone.refs_3_, bf16[256,256]{1,0:T(8,128)(2,1)} %constant.8.clone.refs_4_, ...), custom_call_target="tpu_custom_call" | custom-call | flops 314572800 | bytes 2097152 | tf_op jit(solution)/shard_map/chunk/pallas_call | solution.py:178
  46.6 0.0 copy-done.2
  46.6 3.0 %chunk.8.refs_8_ = f32[128,128]{1,0:T(8,128)} custom-call(bf16[8,2,2,512,128]{4,3,2,1,0:T(8,128)(2,1)} %bitcast.19, bf16[2,2,3,128,128]{4,3,2,1,0:T(8,128)(2,1)} %copy-done.2, f32[512,128]{1,0:T(8,128)} %bitcast.27, bf16[256,256]{1,0:T(8,128)(2,1)} %constant.9.clone.refs_3_, bf16[256,256]{1,0:T(8,128)(2,1)} %constant.8.clone.refs_4_, ...), custom_call_target="tpu_custom_call" | custom-call | flops 314572800 | bytes 2097152 | tf_op jit(solution)/shard_map/chunk/pallas_call | solution.py:178
  49.6 0.0 copy-done.5
  49.7 3.0 %chunk.9.refs_9_ = f32[128,128]{1,0:T(8,128)} custom-call(bf16[8,2,2,512,128]{4,3,2,1,0:T(8,128)(2,1)} %bitcast.20, bf16[2,2,3,128,128]{4,3,2,1,0:T(8,128)(2,1)} %copy-done.5, f32[512,128]{1,0:T(8,128)} %bitcast.28, bf16[256,256]{1,0:T(8,128)(2,1)} %constant.9.clone.refs_3_, bf16[256,256]{1,0:T(8,128)(2,1)} %constant.8.clone.refs_4_, ...), custom_call_target="tpu_custom_call" | custom-call | flops 314572800 | bytes 2097152 | tf_op jit(solution)/shard_map/chunk/pallas_call | solution.py:178
  52.7 0.0 collective-permute-done.4.refs_1_
  52.7 0.0 copy-start.4
  52.7 0.7 copy-done.4
  53.4 3.0 %chunk.10.refs_10_ = f32[128,128]{1,0:T(8,128)} custom-call(bf16[8,2,2,512,128]{4,3,2,1,0:T(8,128)(2,1)} %bitcast.21, bf16[2,2,3,128,128]{4,3,2,1,0:T(8,128)(2,1)} %copy-done.4, f32[512,128]{1,0:T(8,128)} %bitcast.29, bf16[256,256]{1,0:T(8,128)(2,1)} %constant.9.clone.refs_3_, bf16[256,256]{1,0:T(8,128)(2,1)} %constant.8.clone.refs_4_, ...), custom_call_target="tpu_custom_call" | custom-call | flops 314572800 | bytes 2097152 | tf_op jit(solution)/shard_map/chunk/pallas_call | solution.py:178
  56.4 0.0 collective-permute-done.5.refs_1_
  56.4 0.0 copy-start.3
  56.4 0.8 copy-done.3
  57.2 3.0 %chunk.11.refs_11_ = f32[128,128]{1,0:T(8,128)} custom-call(bf16[8,2,2,512,128]{4,3,2,1,0:T(8,128)(2,1)} %bitcast.22, bf16[2,2,3,128,128]{4,3,2,1,0:T(8,128)(2,1)} %copy-done.3, f32[512,128]{1,0:T(8,128)} %bitcast.30, bf16[256,256]{1,0:T(8,128)(2,1)} %constant.9.clone.refs_3_, bf16[256,256]{1,0:T(8,128)(2,1)} %constant.8.clone.refs_4_, ...), custom_call_target="tpu_custom_call" | custom-call | flops 314572800 | bytes 2097152 | tf_op jit(solution)/shard_map/chunk/pallas_call | solution.py:178
  60.2 4.0 %collective-permute-done.6.refs_1_ = bf16[2,2,3,128,128]{4,3,2,1,0:T(8,128)(2,1)S(1)} collective-permute-done((bf16[2,2,3,128,128]{4,3,2,1,0:T(8,128)(2,1)}, bf16[2,2,3,128,128]{4,3,2,1,0:T(8,128)(2,1)S(1)}, u32[]{:S(2)}, u32[]{:S(2)}) %collective-permute-start.6) | collective-permute-done | bytes 393248 | tf_op jit(solution)/shard_map/ppermute | solution.py:164
  64.2 0.0 copy-start.6
  64.2 0.7 copy-done.6
  64.9 3.0 %chunk.12.refs_12_ = f32[128,128]{1,0:T(8,128)} custom-call(bf16[8,2,2,512,128]{4,3,2,1,0:T(8,128)(2,1)} %bitcast.23, bf16[2,2,3,128,128]{4,3,2,1,0:T(8,128)(2,1)} %copy-done.6, f32[512,128]{1,0:T(8,128)} %bitcast.31, bf16[256,256]{1,0:T(8,128)(2,1)} %constant.9.clone.refs_3_, bf16[256,256]{1,0:T(8,128)(2,1)} %constant.8.clone.refs_4_, ...), custom_call_target="tpu_custom_call" | custom-call | flops 314572800 | bytes 2097152 | tf_op jit(solution)/shard_map/chunk/pallas_call | solution.py:178
  67.9 4.7 %collective-permute-done.7.refs_1_ = bf16[2,2,3,128,128]{4,3,2,1,0:T(8,128)(2,1)S(1)} collective-permute-done((bf16[2,2,3,128,128]{4,3,2,1,0:T(8,128)(2,1)}, bf16[2,2,3,128,128]{4,3,2,1,0:T(8,128)(2,1)S(1)}, u32[]{:S(2)}, u32[]{:S(2)}) %collective-permute-start.7) | collective-permute-done | bytes 393248 | tf_op jit(solution)/shard_map/ppermute | solution.py:164
  72.6 0.0 copy-start.7
  72.6 0.8 copy-done.7
  73.3 3.0 %chunk.13.refs_13_ = f32[128,128]{1,0:T(8,128)} custom-call(bf16[8,2,2,512,128]{4,3,2,1,0:T(8,128)(2,1)} %bitcast.24, bf16[2,2,3,128,128]{4,3,2,1,0:T(8,128)(2,1)} %copy-done.7, f32[512,128]{1,0:T(8,128)} %bitcast.32, bf16[256,256]{1,0:T(8,128)(2,1)} %constant.9.clone.refs_3_, bf16[256,256]{1,0:T(8,128)(2,1)} %constant.8.clone.refs_4_, ...), custom_call_target="tpu_custom_call" | custom-call | flops 314572800 | bytes 2097152 | tf_op jit(solution)/shard_map/chunk/pallas_call | solution.py:178
  76.4 3.8 %collective-permute-done.refs_1_ = bf16[2,2,3,128,128]{4,3,2,1,0:T(8,128)(2,1)S(1)} collective-permute-done((bf16[2,2,3,128,128]{4,3,2,1,0:T(8,128)(2,1)}, bf16[2,2,3,128,128]{4,3,2,1,0:T(8,128)(2,1)S(1)}, u32[]{:S(2)}, u32[]{:S(2)}) %collective-permute-start) | collective-permute-done | bytes 393248 | tf_op jit(solution)/shard_map/ppermute | solution.py:164
  80.2 0.7 copy-done
  80.9 3.3 %last.1 = bf16[128,16,128]{2,1,0:T(8,128)(2,1)} custom-call(bf16[8,2,2,512,128]{4,3,2,1,0:T(8,128)(2,1)} %bitcast.25, bf16[2,2,3,128,128]{4,3,2,1,0:T(8,128)(2,1)} %copy-done, f32[512,128]{1,0:T(8,128)} %bitcast.33, bf16[256,256]{1,0:T(8,128)(2,1)} %constant.9.clone.refs_3_, bf16[256,256]{1,0:T(8,128)(2,1)} %constant.8.clone.refs_4_, ...), custom_call_target="tpu_custom_call" | custom-call | flops 314572800 | bytes 2097152 | tf_op jit(solution)/shard_map/last/pallas_call | solution.py:190
  84.2 30.0 %all_to_all.5.in_ref = bf16[128,16,128]{2,1,0:T(8,128)(2,1)} all-to-all(bf16[128,16,128]{2,1,0:T(8,128)(2,1)} %last.1), channel_id=1, replica_groups=mesh['tm'=128,'chan'=4] {'tm'}, dimensions={0} | all-to-all | bytes 1048576 | tf_op jit(solution)/shard_map/all_to_all | solution.py:200
  114.3 2.1 %tree.1 = f32[2,16,1024]{2,1,0:T(8,128)} custom-call(bf16[128,16,128]{2,1,0:T(8,128)(2,1)} %all_to_all.5.in_ref), custom_call_target="tpu_custom_call" | custom-call | flops 4194304 | bytes 1048576 | tf_op jit(solution)/shard_map/tree/pallas_call | solution.py:202
  (2 shorter events, 0.0 us)
Async XLA Ops:
  1.9 27.4 %collective-permute-start.1 = (bf16[2,2,3,128,128]{4,3,2,1,0:T(8,128)(2,1)}, bf16[2,2,3,128,128]{4,3,2,1,0:T(8,128)(2,1)S(1)}, u32[]{:S(2)}, u32[]{:S(2)}) collective-permute-start(bf16[2,2,3,128,128]{4,3,2,1,0:T(8,128)(2,1)} %pack.9), channel_id=1, source_target_pairs={{0,4},{4,8},{8,12},{12,16},{16,20},{20,24},{24,28},{28,32},{32,36}... | collective-permute-start | bytes 1179656 | tf_op jit(solution)/shard_map/ppermute | solution.py:164
  8.1 27.4 %collective-permute-start.2 = (bf16[2,2,3,128,128]{4,3,2,1,0:T(8,128)(2,1)}, bf16[2,2,3,128,128]{4,3,2,1,0:T(8,128)(2,1)S(1)}, u32[]{:S(2)}, u32[]{:S(2)}) collective-permute-start(bf16[2,2,3,128,128]{4,3,2,1,0:T(8,128)(2,1)} %pack.10), channel_id=1, source_target_pairs={{0,4},{4,8},{8,12},{12,16},{16,20},{20,24},{24,28},{28,32},{32,36}... | collective-permute-start | bytes 1179656 | tf_op jit(solution)/shard_map/ppermute | solution.py:164
  14.3 27.4 %collective-permute-start.3 = (bf16[2,2,3,128,128]{4,3,2,1,0:T(8,128)(2,1)}, bf16[2,2,3,128,128]{4,3,2,1,0:T(8,128)(2,1)S(1)}, u32[]{:S(2)}, u32[]{:S(2)}) collective-permute-start(bf16[2,2,3,128,128]{4,3,2,1,0:T(8,128)(2,1)} %pack.11), channel_id=1, source_target_pairs={{0,4},{4,8},{8,12},{12,16},{16,20},{20,24},{24,28},{28,32},{32,36}... | collective-permute-start | bytes 1179656 | tf_op jit(solution)/shard_map/ppermute | solution.py:164
  20.5 32.2 %collective-permute-start.4 = (bf16[2,2,3,128,128]{4,3,2,1,0:T(8,128)(2,1)}, bf16[2,2,3,128,128]{4,3,2,1,0:T(8,128)(2,1)S(1)}, u32[]{:S(2)}, u32[]{:S(2)}) collective-permute-start(bf16[2,2,3,128,128]{4,3,2,1,0:T(8,128)(2,1)} %pack.12), channel_id=1, source_target_pairs={{0,4},{4,8},{8,12},{12,16},{16,20},{20,24},{24,28},{28,32},{32,36}... | collective-permute-start | bytes 1179656 | tf_op jit(solution)/shard_map/ppermute | solution.py:164
  24.3 32.1 %collective-permute-start.5 = (bf16[2,2,3,128,128]{4,3,2,1,0:T(8,128)(2,1)}, bf16[2,2,3,128,128]{4,3,2,1,0:T(8,128)(2,1)S(1)}, u32[]{:S(2)}, u32[]{:S(2)}) collective-permute-start(bf16[2,2,3,128,128]{4,3,2,1,0:T(8,128)(2,1)} %pack.13), channel_id=1, source_target_pairs={{0,4},{4,8},{8,12},{12,16},{16,20},{20,24},{24,28},{28,32},{32,36}... | collective-permute-start | bytes 1179656 | tf_op jit(solution)/shard_map/ppermute | solution.py:164
  29.3 12.4 %copy-start.1 = (bf16[2,2,3,128,128]{4,3,2,1,0:T(8,128)(2,1)}, bf16[2,2,3,128,128]{4,3,2,1,0:T(8,128)(2,1)S(1)}, u32[]{:S(2)}) copy-start(bf16[2,2,3,128,128]{4,3,2,1,0:T(8,128)(2,1)S(1)} %collective-permute-done.1.refs_1_) | copy-start | bytes 1179652
  29.3 34.9 %collective-permute-start.6 = (bf16[2,2,3,128,128]{4,3,2,1,0:T(8,128)(2,1)}, bf16[2,2,3,128,128]{4,3,2,1,0:T(8,128)(2,1)S(1)}, u32[]{:S(2)}, u32[]{:S(2)}) collective-permute-start(bf16[2,2,3,128,128]{4,3,2,1,0:T(8,128)(2,1)} %pack.14), channel_id=1, source_target_pairs={{0,4},{4,8},{8,12},{12,16},{16,20},{20,24},{24,28},{28,32},{32,36}... | collective-permute-start | bytes 1179656 | tf_op jit(solution)/shard_map/ppermute | solution.py:164
  35.5 11.2 %copy-start.2 = (bf16[2,2,3,128,128]{4,3,2,1,0:T(8,128)(2,1)}, bf16[2,2,3,128,128]{4,3,2,1,0:T(8,128)(2,1)S(1)}, u32[]{:S(2)}) copy-start(bf16[2,2,3,128,128]{4,3,2,1,0:T(8,128)(2,1)S(1)} %collective-permute-done.2.refs_1_) | copy-start | bytes 1179652
  35.5 37.1 %collective-permute-start.7 = (bf16[2,2,3,128,128]{4,3,2,1,0:T(8,128)(2,1)}, bf16[2,2,3,128,128]{4,3,2,1,0:T(8,128)(2,1)S(1)}, u32[]{:S(2)}, u32[]{:S(2)}) collective-permute-start(bf16[2,2,3,128,128]{4,3,2,1,0:T(8,128)(2,1)} %pack.15), channel_id=1, source_target_pairs={{0,4},{4,8},{8,12},{12,16},{16,20},{20,24},{24,28},{28,32},{32,36}... | collective-permute-start | bytes 1179656 | tf_op jit(solution)/shard_map/ppermute | solution.py:164
  41.7 8.0 %copy-start.5 = (bf16[2,2,3,128,128]{4,3,2,1,0:T(8,128)(2,1)}, bf16[2,2,3,128,128]{4,3,2,1,0:T(8,128)(2,1)S(1)}, u32[]{:S(2)}) copy-start(bf16[2,2,3,128,128]{4,3,2,1,0:T(8,128)(2,1)S(1)} %collective-permute-done.3.refs_1_) | copy-start | bytes 1179652
  41.7 38.5 %collective-permute-start = (bf16[2,2,3,128,128]{4,3,2,1,0:T(8,128)(2,1)}, bf16[2,2,3,128,128]{4,3,2,1,0:T(8,128)(2,1)S(1)}, u32[]{:S(2)}, u32[]{:S(2)}) collective-permute-start(bf16[2,2,3,128,128]{4,3,2,1,0:T(8,128)(2,1)} %pack.8), channel_id=1, source_target_pairs={{0,4},{4,8},{8,12},{12,16},{16,20},{20,24},{24,28},{28,32},{32,36}... | collective-permute-start | bytes 1179656 | tf_op jit(solution)/shard_map/ppermute | solution.py:164
  52.7 0.7 copy-start.4
  56.4 0.8 copy-start.3
  64.2 0.7 copy-start.6
  72.6 0.8 copy-start.7
  80.2 0.7 copy-start

commit v2 on v1

--- a/solution.py
+++ b/solution.py
@@ -12,6 +12,8 @@
 NT = 16
 SIDE = 128
 BLOCK = 16
+SENT = 10
+VMEM = pltpu.CompilerParams(vmem_limit_bytes=12 << 20)
 
 
 def tables(side):
@@ -76,32 +78,30 @@
 
 
 def last_kernel(*refs):
-    ins, before, out_ref, scratch = refs[:7], refs[7:-4], refs[-4], refs[-3:]
-    last = chunk_power(*ins, *scratch)
-    each = SIDE // 8
-    tiles = []
-    for ref in before:
-        tiles += [ref[pl.ds(8 * i, 8), :] for i in range(each)]
-    tiles += [last[8 * i : 8 * i + 8] for i in range(each)]
-    zero = jnp.zeros((8, SIDE), jnp.float32)
-    row = lax.broadcasted_iota(jnp.int32, (8, SIDE), 0)
-    for d in range(len(tiles)):
-        after = tiles[d + 1] if d + 1 < len(tiles) else zero
-        prior = tiles[d - 1] if d else zero
-        edge = jnp.where(row == 0, after, jnp.where(row == 7, prior, 0.0))
-        out_ref[d] = jnp.concatenate([tiles[d], edge], axis=0).astype(jnp.bfloat16)
-
-
-def tree_kernel(in_ref, out_ref, flat):
-    sources = in_ref.shape[0]
-    per = sources // NT
+    ins, before, out_ref, scratch, every, apart = refs[:7], refs[7:-6], refs[-6], refs[-5:-2], refs[-2], refs[-1]
+    for c, ref in enumerate(before):
+        every[pl.ds(c * SIDE, SIDE), :] = ref[...]
+    every[pl.ds(len(before) * SIDE, SIDE), :] = chunk_power(*ins, *scratch)
+    peers = apart.shape[0] // SENT
+    for j in range(8):
+        apart[pl.ds(j, peers, stride=SENT), :] = every[pl.ds(j, peers, stride=8), :]
+    apart[pl.ds(8, peers - 1, stride=SENT), :] = every[pl.ds(8, peers - 1, stride=8), :]
+    apart[pl.ds(SENT + 9, peers - 1, stride=SENT), :] = every[pl.ds(7, peers - 1, stride=8), :]
+    apart[pl.ds(SENT * (peers - 1) + 8, 1), :] = jnp.zeros((1, SIDE), jnp.float32)
+    apart[pl.ds(9, 1), :] = jnp.zeros((1, SIDE), jnp.float32)
+    out_ref[...] = apart[...].astype(jnp.bfloat16)
+
+
+def tree_kernel(in_ref, out_ref, wide, steps, flat):
+    per = in_ref.shape[0] // SENT // NT
     lane = lax.broadcasted_iota(jnp.int32, (16, SIDE), 1)
-    steps = []
-    for s in range(NT):
-        value = in_ref[s * per].astype(jnp.float32)
+    wide[...] = in_ref[...].astype(jnp.float32)
+    steps[...] = jnp.zeros(steps.shape, jnp.float32)
+    for j in range(SENT):
+        value = wide[pl.ds(j, NT, stride=SENT * per), :]
         for i in range(1, per):
-            value = value + in_ref[s * per + i].astype(jnp.float32)
-        steps.append(value)
+            value = value + wide[pl.ds(SENT * i + j, NT, stride=SENT * per), :]
+        steps[pl.ds(15 if j == 9 else j, NT, stride=16), :] = value
 
     def moved(value, move, sense):
         if move == 0:
@@ -113,7 +113,7 @@
         return jnp.where(lane >= move, here, pltpu.roll(here, 1, 0))
 
     for which, sense in enumerate((1, -1)):
-        level = [[value] for value in steps]
+        level = [[steps[pl.ds(16 * s, 16), :]] for s in range(NT)]
         length = 1
         while len(level) > 1:
             level = [
@@ -158,7 +158,8 @@
             out_specs=whole(halo),
             out_shape=jax.ShapeDtypeStruct(halo, jnp.bfloat16),
             scratch_shapes=[pltpu.VMEM((SIDE * frames, SIDE), jnp.float32)],
-            cost_estimate=pl.CostEstimate(flops=1 << 20, bytes_accessed=1 << 20, transcendentals=0),
+            compiler_params=VMEM,
+        cost_estimate=pl.CostEstimate(flops=1 << 20, bytes_accessed=1 << 20, transcendentals=0),
             name="pack",
         )(rows)
         near.append(lax.ppermute(packed, "tm", pairs))
@@ -182,22 +183,26 @@
                 out_specs=whole(tile),
                 out_shape=jax.ShapeDtypeStruct(tile, jnp.float32),
                 scratch_shapes=scratch,
+                compiler_params=VMEM,
                 cost_estimate=cost,
                 name="chunk",
             )(rows, near[c], *constants)
         )
-    sent = (peers, 16, SIDE)
+    sent = (peers * SENT, SIDE)
     out = pl.pallas_call(
         last_kernel,
         grid=(1,),
         in_specs=[block_of(channels - 1), whole(halo)] + specs + [whole(tile)] * (channels - 1),
         out_specs=whole(sent),
         out_shape=jax.ShapeDtypeStruct(sent, jnp.bfloat16),
-        scratch_shapes=scratch,
+        scratch_shapes=scratch
+        + [pltpu.VMEM((channels * SIDE, SIDE), jnp.float32), pltpu.VMEM(sent, jnp.float32)],
+        compiler_params=VMEM,
         cost_estimate=cost,
         name="last",
     )(rows, near[channels - 1], *constants, *powers)
-    owned = lax.all_to_all(out, "tm", split_axis=0, concat_axis=0, tiled=True)
+    pairs_of_rows = out.reshape(peers, SENT // 2, 2, SIDE)
+    owned = lax.all_to_all(pairs_of_rows, "tm", split_axis=0, concat_axis=0, tiled=True).reshape(sent)
     result = (2, NT, channels * length // peers)
     return pl.pallas_call(
         tree_kernel,
@@ -205,7 +210,12 @@
         in_specs=[whole(sent)],
         out_specs=whole(result),
         out_shape=jax.ShapeDtypeStruct(result, jnp.float32),
-        scratch_shapes=[pltpu.VMEM((8 * NT, SIDE), jnp.float32)],
+        scratch_shapes=[
+            pltpu.VMEM(sent, jnp.float32),
+            pltpu.VMEM((16 * NT, SIDE), jnp.float32),
+            pltpu.VMEM((8 * NT, SIDE), jnp.float32),
+        ],
+        compiler_params=VMEM,
         cost_estimate=pl.CostEstimate(flops=1 << 22, bytes_accessed=1 << 20, transcendentals=0),
         name="tree",
     )(owned)

time: 117 us -> 109 us (0.932)
  waiting for transfers between devices: 12.5 us -> 45 us
  Pallas kernels: 41.8 us -> 10.8 us
  blocking collectives: 30 us -> 25.7 us
  starting transfers between devices: 28.2 us -> 24.6 us
  local copies, waits for them, and re-layouts: 3.76 us -> 2.22 us
    ppermute x8, waiting for transfers between devices: 12.5 us -> 45 us  [per_device(): near.append(lax.ppermute(packed, 'tm', pairs))]
    pallas_call x8, Pallas kernels: 15.3 us -> 0.98 us  [per_device(): pl.pallas_call(pack_kernel, grid=(1,), in_specs=[block_of(c)], out_specs=...]
    pallas_call x7, Pallas kernels: 21.1 us -> 7.37 us  [per_device(): pl.pallas_call(chunk_kernel, grid=(1,), in_specs=[block_of(c), whole(halo...]
    all_to_all x1, blocking collectives: 30 us -> 25.7 us  [per_device(): lax.all_to_all(pairs_of_rows, 'tm', split_axis=0, concat_axis=0, tiled=True)]
    ppermute x8, starting transfers between devices: 28.2 us -> 24.6 us  [per_device(): near.append(lax.ppermute(packed, 'tm', pairs))]
    pallas_call x1, Pallas kernels: 3.3 us -> 1.11 us  [per_device(): pl.pallas_call(last_kernel, grid=(1,), in_specs=[block_of(channels - 1),...]
    unnamed x16 -> x12, local copies, waits for them, and re-layouts: 3.76 us -> 2.22 us
  transfers between devices with their start and end apart: 8 -> 8, of which waited for: 3 -> 8; matrix products, arithmetic and copies ran while one was open for 0% -> 0% of each run, Pallas kernels for 30% -> 8%
where the time goes in v2:
time: 109 us
  waiting for transfers between devices  45 us (41%)
  blocking collectives  25.7 us (24%)
  starting transfers between devices  24.6 us (23%)
  Pallas kernels  10.8 us (10%)
  local copies, waits for them, and re-layouts  2.22 us (2%)
    ppermute x8, waiting for transfers between devices, per_device(): near.append(lax.ppermute(packed, 'tm', pairs))  45 us
    all_to_all x1, blocking collectives, per_device(): lax.all_to_all(pairs_of_rows, 'tm', split_axis=0, concat_axis=0, tiled=True)  25.7 us
    ppermute x8, starting transfers between devices, per_device(): near.append(lax.ppermute(packed, 'tm', pairs))  24.6 us
    pallas_call x7, Pallas kernels, per_device(): pl.pallas_call(chunk_kernel, grid=(1,), in_specs=[block_of(c), whole(halo...  7.37 us
    unnamed x12, local copies, waits for them, and re-layouts  2.22 us
  transfers between devices with their start and end apart: 8, of which 8 were waited for; matrix products, arithmetic and copies ran while one was open for 0% of the time, Pallas kernels for 8%

profile of v2, /device:TPU:8, one launch (start us, length us, event | category | flops | bytes accessed | tf_op | source)
XLA Modules:
  0.0 108.5 jit_solution(13335503935585020633)
XLA Ops:
  0.0 0.0 copy-start
  0.0 2.2 %copy-done = bf16[8,2,2,4,16384]{4,3,2,1,0:T(4,128)(2,1)S(1)} copy-done((bf16[8,2,2,4,16384]{4,3,2,1,0:T(4,128)(2,1)S(1)}, bf16[8,2,2,4,16384]{4,3,2,1,0:T(4,128)(2,1)}, u32[]{:S(2)}) %copy-start) | copy-done | bytes 4194328
  2.2 0.1 pack.9
  2.3 4.3 %collective-permute-start.1 = (bf16[2,2,3,128,128]{4,3,2,1,0:T(8,128)(2,1)S(1)}, bf16[2,2,3,128,128]{4,3,2,1,0:T(8,128)(2,1)S(1)}, u32[]{:S(2)}, u32[]{:S(2)}) collective-permute-start(bf16[2,2,3,128,128]{4,3,2,1,0:T(8,128)(2,1)S(1)} %pack.9), channel_id=1, source_target_pairs={{0,4},{4,8},{8,12},{12,16},{16,20},{20,24},{24,28},{28,32},{32,36}... | collective-permute-start | bytes 1179656 | tf_op jit(solution)/shard_map/ppermute | solution.py:165
  6.6 0.1 pack.10
  6.7 4.3 %collective-permute-start.2 = (bf16[2,2,3,128,128]{4,3,2,1,0:T(8,128)(2,1)S(1)}, bf16[2,2,3,128,128]{4,3,2,1,0:T(8,128)(2,1)S(1)}, u32[]{:S(2)}, u32[]{:S(2)}) collective-permute-start(bf16[2,2,3,128,128]{4,3,2,1,0:T(8,128)(2,1)S(1)} %pack.10), channel_id=1, source_target_pairs={{0,4},{4,8},{8,12},{12,16},{16,20},{20,24},{24,28},{28,32},{32,36}... | collective-permute-start | bytes 1179656 | tf_op jit(solution)/shard_map/ppermute | solution.py:165
  11.0 0.1 pack.11
  11.1 4.3 %collective-permute-start.3 = (bf16[2,2,3,128,128]{4,3,2,1,0:T(8,128)(2,1)S(1)}, bf16[2,2,3,128,128]{4,3,2,1,0:T(8,128)(2,1)S(1)}, u32[]{:S(2)}, u32[]{:S(2)}) collective-permute-start(bf16[2,2,3,128,128]{4,3,2,1,0:T(8,128)(2,1)S(1)} %pack.11), channel_id=1, source_target_pairs={{0,4},{4,8},{8,12},{12,16},{16,20},{20,24},{24,28},{28,32},{32,36}... | collective-permute-start | bytes 1179656 | tf_op jit(solution)/shard_map/ppermute | solution.py:165
  15.4 0.1 pack.12
  15.6 1.9 %collective-permute-start.4 = (bf16[2,2,3,128,128]{4,3,2,1,0:T(8,128)(2,1)S(1)}, bf16[2,2,3,128,128]{4,3,2,1,0:T(8,128)(2,1)S(1)}, u32[]{:S(2)}, u32[]{:S(2)}) collective-permute-start(bf16[2,2,3,128,128]{4,3,2,1,0:T(8,128)(2,1)S(1)} %pack.12), channel_id=1, source_target_pairs={{0,4},{4,8},{8,12},{12,16},{16,20},{20,24},{24,28},{28,32},{32,36}... | collective-permute-start | bytes 1179656 | tf_op jit(solution)/shard_map/ppermute | solution.py:165
  17.5 0.1 pack.13
  17.6 3.0 %collective-permute-start.5 = (bf16[2,2,3,128,128]{4,3,2,1,0:T(8,128)(2,1)S(1)}, bf16[2,2,3,128,128]{4,3,2,1,0:T(8,128)(2,1)S(1)}, u32[]{:S(2)}, u32[]{:S(2)}) collective-permute-start(bf16[2,2,3,128,128]{4,3,2,1,0:T(8,128)(2,1)S(1)} %pack.13), channel_id=1, source_target_pairs={{0,4},{4,8},{8,12},{12,16},{16,20},{20,24},{24,28},{28,32},{32,36}... | collective-permute-start | bytes 1179656 | tf_op jit(solution)/shard_map/ppermute | solution.py:165
  20.6 0.1 pack.14
  20.8 0.0 copy-start.1
  20.8 0.0 copy-start.2
  20.8 0.0 copy-start.3
  20.8 0.0 copy-start.4
  20.8 0.0 copy-start.5
  20.8 1.4 %collective-permute-done.1.refs_1_ = bf16[2,2,3,128,128]{4,3,2,1,0:T(8,128)(2,1)S(1)} collective-permute-done((bf16[2,2,3,128,128]{4,3,2,1,0:T(8,128)(2,1)S(1)}, bf16[2,2,3,128,128]{4,3,2,1,0:T(8,128)(2,1)S(1)}, u32[]{:S(2)}, u32[]{:S(2)}) %collective-permute-start.1) | collective-permute-done | bytes 393248 | tf_op jit(solution)/shard_map/ppermute | solution.py:165
  22.2 3.0 %collective-permute-start.6 = (bf16[2,2,3,128,128]{4,3,2,1,0:T(8,128)(2,1)S(1)}, bf16[2,2,3,128,128]{4,3,2,1,0:T(8,128)(2,1)S(1)}, u32[]{:S(2)}, u32[]{:S(2)}) collective-permute-start(bf16[2,2,3,128,128]{4,3,2,1,0:T(8,128)(2,1)S(1)} %pack.14), channel_id=1, source_target_pairs={{0,4},{4,8},{8,12},{12,16},{16,20},{20,24},{24,28},{28,32},{32,36}... | collective-permute-start | bytes 1179656 | tf_op jit(solution)/shard_map/ppermute | solution.py:165
  25.3 0.1 pack.15
  25.4 5.3 %collective-permute-done.2.refs_1_ = bf16[2,2,3,128,128]{4,3,2,1,0:T(8,128)(2,1)S(1)} collective-permute-done((bf16[2,2,3,128,128]{4,3,2,1,0:T(8,128)(2,1)S(1)}, bf16[2,2,3,128,128]{4,3,2,1,0:T(8,128)(2,1)S(1)}, u32[]{:S(2)}, u32[]{:S(2)}) %collective-permute-start.2) | collective-permute-done | bytes 393248 | tf_op jit(solution)/shard_map/ppermute | solution.py:165
  30.7 1.9 %collective-permute-start.7 = (bf16[2,2,3,128,128]{4,3,2,1,0:T(8,128)(2,1)S(1)}, bf16[2,2,3,128,128]{4,3,2,1,0:T(8,128)(2,1)S(1)}, u32[]{:S(2)}, u32[]{:S(2)}) collective-permute-start(bf16[2,2,3,128,128]{4,3,2,1,0:T(8,128)(2,1)S(1)} %pack.15), channel_id=1, source_target_pairs={{0,4},{4,8},{8,12},{12,16},{16,20},{20,24},{24,28},{28,32},{32,36}... | collective-permute-start | bytes 1179656 | tf_op jit(solution)/shard_map/ppermute | solution.py:165
  32.6 0.1 pack.8
  32.7 6.4 %collective-permute-done.3.refs_1_ = bf16[2,2,3,128,128]{4,3,2,1,0:T(8,128)(2,1)S(1)} collective-permute-done((bf16[2,2,3,128,128]{4,3,2,1,0:T(8,128)(2,1)S(1)}, bf16[2,2,3,128,128]{4,3,2,1,0:T(8,128)(2,1)S(1)}, u32[]{:S(2)}, u32[]{:S(2)}) %collective-permute-start.3) | collective-permute-done | bytes 393248 | tf_op jit(solution)/shard_map/ppermute | solution.py:165
  39.1 1.9 %collective-permute-start = (bf16[2,2,3,128,128]{4,3,2,1,0:T(8,128)(2,1)S(1)}, bf16[2,2,3,128,128]{4,3,2,1,0:T(8,128)(2,1)S(1)}, u32[]{:S(2)}, u32[]{:S(2)}) collective-permute-start(bf16[2,2,3,128,128]{4,3,2,1,0:T(8,128)(2,1)S(1)} %pack.8), channel_id=1, source_target_pairs={{0,4},{4,8},{8,12},{12,16},{16,20},{20,24},{24,28},{28,32},{32,36}... | collective-permute-start | bytes 1179656 | tf_op jit(solution)/shard_map/ppermute | solution.py:165
  41.0 0.0 copy-done.1
  41.0 0.0 copy-done.2
  41.0 0.0 copy-done.3
  41.0 0.0 copy-done.4
  41.0 0.0 copy-done.5
  41.0 1.1 chunk.7.refs_7_
  42.1 1.1 chunk.8.refs_8_
  43.2 1.1 chunk.9.refs_9_
  44.2 3.3 %collective-permute-done.4.refs_1_ = bf16[2,2,3,128,128]{4,3,2,1,0:T(8,128)(2,1)S(1)} collective-permute-done((bf16[2,2,3,128,128]{4,3,2,1,0:T(8,128)(2,1)S(1)}, bf16[2,2,3,128,128]{4,3,2,1,0:T(8,128)(2,1)S(1)}, u32[]{:S(2)}, u32[]{:S(2)}) %collective-permute-start.4) | collective-permute-done | bytes 393248 | tf_op jit(solution)/shard_map/ppermute | solution.py:165
  47.5 1.1 chunk.10.refs_10_
  48.6 7.4 %collective-permute-done.5.refs_1_ = bf16[2,2,3,128,128]{4,3,2,1,0:T(8,128)(2,1)S(1)} collective-permute-done((bf16[2,2,3,128,128]{4,3,2,1,0:T(8,128)(2,1)S(1)}, bf16[2,2,3,128,128]{4,3,2,1,0:T(8,128)(2,1)S(1)}, u32[]{:S(2)}, u32[]{:S(2)}) %collective-permute-start.5) | collective-permute-done | bytes 393248 | tf_op jit(solution)/shard_map/ppermute | solution.py:165
  55.9 1.1 chunk.11.refs_11_
  57.0 7.4 %collective-permute-done.6.refs_1_ = bf16[2,2,3,128,128]{4,3,2,1,0:T(8,128)(2,1)S(1)} collective-permute-done((bf16[2,2,3,128,128]{4,3,2,1,0:T(8,128)(2,1)S(1)}, bf16[2,2,3,128,128]{4,3,2,1,0:T(8,128)(2,1)S(1)}, u32[]{:S(2)}, u32[]{:S(2)}) %collective-permute-start.6) | collective-permute-done | bytes 393248 | tf_op jit(solution)/shard_map/ppermute | solution.py:165
  64.4 1.1 chunk.12.refs_12_
  65.4 7.4 %collective-permute-done.7.refs_1_ = bf16[2,2,3,128,128]{4,3,2,1,0:T(8,128)(2,1)S(1)} collective-permute-done((bf16[2,2,3,128,128]{4,3,2,1,0:T(8,128)(2,1)S(1)}, bf16[2,2,3,128,128]{4,3,2,1,0:T(8,128)(2,1)S(1)}, u32[]{:S(2)}, u32[]{:S(2)}) %collective-permute-start.7) | collective-permute-done | bytes 393248 | tf_op jit(solution)/shard_map/ppermute | solution.py:165
  72.8 1.1 chunk.13.refs_13_
  73.8 6.5 %collective-permute-done.refs_1_ = bf16[2,2,3,128,128]{4,3,2,1,0:T(8,128)(2,1)S(1)} collective-permute-done((bf16[2,2,3,128,128]{4,3,2,1,0:T(8,128)(2,1)S(1)}, bf16[2,2,3,128,128]{4,3,2,1,0:T(8,128)(2,1)S(1)}, u32[]{:S(2)}, u32[]{:S(2)}) %collective-permute-start) | collective-permute-done | bytes 393248 | tf_op jit(solution)/shard_map/ppermute | solution.py:165
  80.4 1.1 %last.1 = bf16[1280,128]{1,0:T(8,128)(2,1)S(1)} custom-call(bf16[8,2,2,512,128]{4,3,2,1,0:T(8,128)(2,1)S(1)} %bitcast.27, bf16[2,2,3,128,128]{4,3,2,1,0:T(8,128)(2,1)S(1)} %collective-permute-done.refs_1_, f32[512,128]{1,0:T(8,128)S(1)} %bitcast.35, bf16[256,256]{1,0:T(8,128)(2,1)S(1)} %copy-done.3, bf16[256,256]{1,0:T(8,128)(2,1)S(1)} %copy-done.2, ...), custom_call_target="tpu_custom_call" | custom-call | flops 314572800 | bytes 2097152 | tf_op jit(solution)/shard_map/last/pallas_call | solution.py:192
  81.5 25.7 %all_to_all.5 = bf16[128,5,2,128]{3,2,1,0:T(2,128)(2,1)S(1)} all-to-all(bf16[128,5,2,128]{3,2,1,0:T(2,128)(2,1)S(1)} %bitcast.36), channel_id=1, replica_groups=mesh['tm'=128,'chan'=4] {'tm'}, dimensions={0} | all-to-all | bytes 655360 | tf_op jit(solution)/shard_map/all_to_all | solution.py:205
  107.2 1.3 %tree.1 = f32[2,16,1024]{2,1,0:T(8,128)} custom-call(bf16[1280,128]{1,0:T(8,128)(2,1)S(1)} %bitcast.37), custom_call_target="tpu_custom_call" | custom-call | flops 4194304 | bytes 1048576 | tf_op jit(solution)/shard_map/tree/pallas_call | solution.py:207
Async XLA Ops:
  0.0 2.2 %copy-start = (bf16[8,2,2,4,16384]{4,3,2,1,0:T(4,128)(2,1)S(1)}, bf16[8,2,2,4,16384]{4,3,2,1,0:T(4,128)(2,1)}, u32[]{:S(2)}) copy-start(bf16[8,2,2,4,16384]{4,3,2,1,0:T(4,128)(2,1)} %param.6) | copy-start | bytes 12582916
  2.3 19.9 %collective-permute-start.1 = (bf16[2,2,3,128,128]{4,3,2,1,0:T(8,128)(2,1)S(1)}, bf16[2,2,3,128,128]{4,3,2,1,0:T(8,128)(2,1)S(1)}, u32[]{:S(2)}, u32[]{:S(2)}) collective-permute-start(bf16[2,2,3,128,128]{4,3,2,1,0:T(8,128)(2,1)S(1)} %pack.9), channel_id=1, source_target_pairs={{0,4},{4,8},{8,12},{12,16},{16,20},{20,24},{24,28},{28,32},{32,36}... | collective-permute-start | bytes 1179656 | tf_op jit(solution)/shard_map/ppermute | solution.py:165
  6.7 23.9 %collective-permute-start.2 = (bf16[2,2,3,128,128]{4,3,2,1,0:T(8,128)(2,1)S(1)}, bf16[2,2,3,128,128]{4,3,2,1,0:T(8,128)(2,1)S(1)}, u32[]{:S(2)}, u32[]{:S(2)}) collective-permute-start(bf16[2,2,3,128,128]{4,3,2,1,0:T(8,128)(2,1)S(1)} %pack.10), channel_id=1, source_target_pairs={{0,4},{4,8},{8,12},{12,16},{16,20},{20,24},{24,28},{28,32},{32,36}... | collective-permute-start | bytes 1179656 | tf_op jit(solution)/shard_map/ppermute | solution.py:165
  11.1 27.9 %collective-permute-start.3 = (bf16[2,2,3,128,128]{4,3,2,1,0:T(8,128)(2,1)S(1)}, bf16[2,2,3,128,128]{4,3,2,1,0:T(8,128)(2,1)S(1)}, u32[]{:S(2)}, u32[]{:S(2)}) collective-permute-start(bf16[2,2,3,128,128]{4,3,2,1,0:T(8,128)(2,1)S(1)} %pack.11), channel_id=1, source_target_pairs={{0,4},{4,8},{8,12},{12,16},{16,20},{20,24},{24,28},{28,32},{32,36}... | collective-permute-start | bytes 1179656 | tf_op jit(solution)/shard_map/ppermute | solution.py:165
  15.6 32.0 %collective-permute-start.4 = (bf16[2,2,3,128,128]{4,3,2,1,0:T(8,128)(2,1)S(1)}, bf16[2,2,3,128,128]{4,3,2,1,0:T(8,128)(2,1)S(1)}, u32[]{:S(2)}, u32[]{:S(2)}) collective-permute-start(bf16[2,2,3,128,128]{4,3,2,1,0:T(8,128)(2,1)S(1)} %pack.12), channel_id=1, source_target_pairs={{0,4},{4,8},{8,12},{12,16},{16,20},{20,24},{24,28},{28,32},{32,36}... | collective-permute-start | bytes 1179656 | tf_op jit(solution)/shard_map/ppermute | solution.py:165
  17.6 38.3 %collective-permute-start.5 = (bf16[2,2,3,128,128]{4,3,2,1,0:T(8,128)(2,1)S(1)}, bf16[2,2,3,128,128]{4,3,2,1,0:T(8,128)(2,1)S(1)}, u32[]{:S(2)}, u32[]{:S(2)}) collective-permute-start(bf16[2,2,3,128,128]{4,3,2,1,0:T(8,128)(2,1)S(1)} %pack.13), channel_id=1, source_target_pairs={{0,4},{4,8},{8,12},{12,16},{16,20},{20,24},{24,28},{28,32},{32,36}... | collective-permute-start | bytes 1179656 | tf_op jit(solution)/shard_map/ppermute | solution.py:165
  20.8 20.2 %copy-start.1 = (f32[4,16384]{1,0:T(4,128)S(1)}, f32[4,16384]{1,0:T(4,128)}, u32[]{:S(2)}) copy-start(f32[4,16384]{1,0:T(4,128)} %param.7) | copy-start | bytes 786436
  20.8 20.2 %copy-start.2 = (bf16[256,256]{1,0:T(8,128)(2,1)S(1)}, bf16[256,256]{1,0:T(8,128)(2,1)}, u32[]{:S(2)}) copy-start(bf16[256,256]{1,0:T(8,128)(2,1)} %constant.8.clone.refs_4_) | copy-start | bytes 393220
  20.8 20.2 %copy-start.3 = (bf16[256,256]{1,0:T(8,128)(2,1)S(1)}, bf16[256,256]{1,0:T(8,128)(2,1)}, u32[]{:S(2)}) copy-start(bf16[256,256]{1,0:T(8,128)(2,1)} %constant.9.clone.refs_3_) | copy-start | bytes 393220
  20.8 20.2 %copy-start.4 = (f32[128,128]{1,0:T(8,128)S(1)}, f32[128,128]{1,0:T(8,128)}, u32[]{:S(2)}) copy-start(f32[128,128]{1,0:T(8,128)} %constant.10.clone.refs_5_) | copy-start | bytes 196612
  20.8 20.2 %copy-start.5 = (f32[128,128]{1,0:T(8,128)S(1)}, f32[128,128]{1,0:T(8,128)}, u32[]{:S(2)}) copy-start(f32[128,128]{1,0:T(8,128)} %constant.11.clone.refs_6_) | copy-start | bytes 196612
  22.2 42.1 %collective-permute-start.6 = (bf16[2,2,3,128,128]{4,3,2,1,0:T(8,128)(2,1)S(1)}, bf16[2,2,3,128,128]{4,3,2,1,0:T(8,128)(2,1)S(1)}, u32[]{:S(2)}, u32[]{:S(2)}) collective-permute-start(bf16[2,2,3,128,128]{4,3,2,1,0:T(8,128)(2,1)S(1)} %pack.14), channel_id=1, source_target_pairs={{0,4},{4,8},{8,12},{12,16},{16,20},{20,24},{24,28},{28,32},{32,36}... | collective-permute-start | bytes 1179656 | tf_op jit(solution)/shard_map/ppermute | solution.py:165
  30.7 42.1 %collective-permute-start.7 = (bf16[2,2,3,128,128]{4,3,2,1,0:T(8,128)(2,1)S(1)}, bf16[2,2,3,128,128]{4,3,2,1,0:T(8,128)(2,1)S(1)}, u32[]{:S(2)}, u32[]{:S(2)}) collective-permute-start(bf16[2,2,3,128,128]{4,3,2,1,0:T(8,128)(2,1)S(1)} %pack.15), channel_id=1, source_target_pairs={{0,4},{4,8},{8,12},{12,16},{16,20},{20,24},{24,28},{28,32},{32,36}... | collective-permute-start | bytes 1179656 | tf_op jit(solution)/shard_map/ppermute | solution.py:165
  39.1 41.3 %collective-permute-start = (bf16[2,2,3,128,128]{4,3,2,1,0:T(8,128)(2,1)S(1)}, bf16[2,2,3,128,128]{4,3,2,1,0:T(8,128)(2,1)S(1)}, u32[]{:S(2)}, u32[]{:S(2)}) collective-permute-start(bf16[2,2,3,128,128]{4,3,2,1,0:T(8,128)(2,1)S(1)} %pack.8), channel_id=1, source_target_pairs={{0,4},{4,8},{8,12},{12,16},{16,20},{20,24},{24,28},{28,32},{32,36}... | collective-permute-start | bytes 1179656 | tf_op jit(solution)/shard_map/ppermute | solution.py:165

commit v3 on v2

v3 whole, which is shorter than its diff:
```python
import math

import jax
import jax.numpy as jnp
import ml_dtypes
import numpy as np
from jax import lax
from jax.experimental import pallas as pl
from jax.experimental.pallas import tpu as pltpu
from jax.sharding import Mesh
from jax.sharding import PartitionSpec as P

NT = 16
SIDE = 128
BLOCK = 16
AHEAD = 4
SENT = 9
PARAMS = pltpu.CompilerParams(vmem_limit_bytes=12 << 20)
FIRST = pltpu.CompilerParams(vmem_limit_bytes=63_000_000)
VMEM = pl.BlockSpec(memory_space=pltpu.VMEM)
ANY = pl.BlockSpec(memory_space=pl.ANY)


def tables(side):
    index = np.arange(side, dtype=np.int64)
    angle = -2.0 * math.pi / side * ((index[:, None] * index[None, :]) % side)
    re = (np.cos(angle) / math.sqrt(side)).astype(ml_dtypes.bfloat16)
    im = (np.sin(angle) / math.sqrt(side)).astype(ml_dtypes.bfloat16)
    fourier = np.block([[re, -im], [im, re]])
    turn = -2.0 * math.pi / (side * side) * (index[:, None] * index[None, :])
    return fourier, np.cos(turn).astype(np.float32), np.sin(turn).astype(np.float32)


def channel_at(place, half):
    lower = place + 4 if place < 4 else 3 if place == 4 else place - 5
    return lower + half * (place - lower)


def receiver_half():
    half, last = lax.axis_index("half"), lax.axis_size("tm") - 1
    return jnp.where((half == 0) & (lax.axis_index("tm") == last), 1, half)


def spread(value, rows, out_ref, p, r):
    frames = value.shape[0] // SIDE
    rows[...] = value.astype(jnp.float32)
    for t in range(1, frames):
        out_ref[p, r, t - 1] = rows[pl.ds(t, SIDE, stride=frames), :].astype(jnp.bfloat16)


def first_pack_kernel(v_ref, out_ref, block, rows, sems):
    channel = channel_at(0, receiver_half())
    copies = {}
    for p in range(2):
        for r in range(2):
            copies[p, r] = pltpu.make_async_copy(v_ref.at[channel, p, r], block.at[p, r], sems.at[p, r])
            copies[p, r].start()
    for p in range(2):
        for r in range(2):
            copies[p, r].wait()
            spread(block[p, r], rows.at[p, r], out_ref, p, r)


def pack_kernel(place, pols, v_ref, out_ref, rows):
    channel = channel_at(place, receiver_half())
    for i, p in enumerate(pols):
        for r in range(2):
            spread(v_ref[channel, p, r], rows.at[r], out_ref, i, r)


def chunk_power(place, pols, ins, scratch):
    v_ref, h_ref, taps_ref, fourier_ref, back_ref, cos_ref, sin_ref = ins
    rows, wide, tall = scratch
    channel = channel_at(place, lax.axis_index("half"))
    frames = v_ref.shape[3] // SIDE
    count = taps_ref.shape[0] // SIDE
    lane = lax.broadcasted_iota(jnp.int32, (BLOCK, SIDE), 1)
    sign = 1.0 - 2.0 * (lane % 2).astype(jnp.float32)
    total = None
    for i, p in enumerate(pols):
        for r in range(2):
            rows[r] = v_ref[channel, p, r].astype(jnp.float32)
        for n in range(0, SIDE, BLOCK):
            shaped = [
                taps_ref[pl.ds(count * n + k, BLOCK, stride=count), :] * sign for k in range(count)
            ]
            for r in range(2):
                frame = [h_ref[i, r, t, pl.ds(n, BLOCK), :].astype(jnp.float32) for t in range(count - 1)]
                frame += [rows[r, pl.ds(frames * n + t, BLOCK, stride=frames), :] for t in range(frames)]
                for t in range(frames):
                    value = shaped[0] * frame[t + count - 1]
                    for k in range(1, count):
                        value = value + shaped[k] * frame[t + count - 1 - k]
                    wide[pl.ds(r * SIDE + n, BLOCK), pl.ds(t * SIDE, SIDE)] = value.astype(jnp.bfloat16)
        first = jnp.dot(fourier_ref[...], wide[...], preferred_element_type=jnp.float32)
        cos, sin = cos_ref[...], sin_ref[...]
        for t in range(frames):
            re = first[:SIDE, t * SIDE : (t + 1) * SIDE]
            im = first[SIDE:, t * SIDE : (t + 1) * SIDE]
            tall[pl.ds(t * SIDE, SIDE), pl.ds(0, SIDE)] = (re * cos - im * sin).astype(jnp.bfloat16)
            tall[pl.ds(t * SIDE, SIDE), pl.ds(SIDE, SIDE)] = (re * sin + im * cos).astype(jnp.bfloat16)
        spectrum = jnp.dot(tall[...], back_ref[...], preferred_element_type=jnp.float32)
        square = spectrum * spectrum
        for t in range(frames):
            part = square[t * SIDE : (t + 1) * SIDE]
            part = part[:, :SIDE] + part[:, SIDE:]
            total = part if total is None else total + part
    return total


def chunk_kernel(place, *refs):
    ins, out_ref, scratch = refs[:7], refs[7], refs[8:]
    out_ref[...] = chunk_power(place, (0, 1), ins, scratch).T


def first_half_kernel(place, *refs):
    ins, out_ref, scratch = refs[:7], refs[7], refs[8:]
    out_ref[...] = chunk_power(place, (0,), ins, scratch)


def lay_out(every, apart, peers, step, start):
    for j in range(8):
        apart[pl.ds(start + j, peers, stride=step), :] = every[pl.ds(8 + j, peers, stride=8), :]
    lane = lax.broadcasted_iota(jnp.int32, (peers, SIDE), 1)
    after = every[pl.ds(16, peers, stride=8), :]
    before = every[pl.ds(7, peers, stride=8), :]
    apart[pl.ds(start + 8, peers, stride=step), :] = jnp.where(lane < SIDE // 2, after, before)


def ends(every, before, after):
    count = every.shape[0]
    every[pl.ds(0, 8), :] = before
    every[pl.ds(count - 8, 8), :] = after


def ship_kernel(p0, p1, p2, p3, border, out_ref):
    half = lax.axis_index("half")
    zero = jnp.zeros((8, SIDE), jnp.float32)
    before = jnp.where(half == 0, border[pl.ds(SIDE - 8, 8), :], zero)
    after = jnp.where(half == 1, border[pl.ds(0, 8), :], zero)
    out_ref[pl.ds(0, 16), :] = jnp.concatenate([zero, before], axis=0).astype(jnp.bfloat16)
    for i, ref in enumerate((p0, p1, p2, p3)):
        out_ref[pl.ds(16 + i * SIDE, SIDE), :] = ref[...].astype(jnp.bfloat16)
    out_ref[pl.ds(16 + 4 * SIDE, 16), :] = jnp.concatenate([after, zero], axis=0).astype(jnp.bfloat16)


def last_kernel(place, *refs):
    ins, (part, p0, p3, border, p5, p6, theirs, relayed), out_ref = refs[:7], refs[7:15], refs[15]
    scratch, (every, apart, plain) = refs[16:19], refs[19:]
    half = lax.axis_index("half")
    peers = apart.shape[0] // (2 * SENT)
    plain[...] = theirs[...].astype(jnp.float32) + relayed[...].astype(jnp.float32)
    lay_out(plain.at[pl.ds(8, plain.shape[0] - 16)], apart, peers, 2 * SENT, SENT)

    def put(slot, value):
        every[pl.ds(pl.multiple_of(8 + slot * SIDE, 8), SIDE), :] = value

    put(3 * (1 - half), border[...])
    put(half, p5[...])
    put(1 + half, p6[...])
    zero = jnp.zeros((8, SIDE), jnp.float32)
    ends(
        every,
        jnp.where(half == 1, p3[pl.ds(SIDE - 8, 8), :], zero),
        jnp.where(half == 0, p0[pl.ds(0, 8), :], zero),
    )
    put(2 + half, (part[...] + chunk_power(place, (1,), ins, scratch)).T)
    lay_out(every, apart, peers, 2 * SENT, 0)
    out_ref[...] = apart[...].astype(jnp.bfloat16)


def tree_kernel(scale, in_ref, out_ref, wide, steps, flat):
    half = lax.axis_index("half")
    step = 2 * SENT
    sources = in_ref.shape[0] // step
    per = sources // (NT // 2)
    lane = lax.broadcasted_iota(jnp.int32, (16, SIDE), 1)
    wide[...] = in_ref[...].astype(jnp.float32)
    steps[...] = jnp.zeros(steps.shape, jnp.float32)
    for whose in range(2):
        base = 8 * 16 * (half if whose == 0 else 1 - half)
        for j in range(SENT):
            value = wide[pl.ds(whose * SENT + j, 8, stride=step * per), :]
            for i in range(1, per):
                value = value + wide[pl.ds(step * i + whose * SENT + j, 8, stride=step * per), :]
            for row in (j,) if j < 8 else (8, 15):
                if whose == 0:
                    steps[pl.ds(base + row, 8, stride=16), :] = value
                else:
                    steps[pl.ds(base + 6 * 16 + row, 2, stride=16), :] = value[:2]
                    steps[pl.ds(base + row, 6, stride=16), :] = value[2:]

    def moved(value, move, sense):
        if move == 0:
            return value
        if sense > 0:
            here = pltpu.roll(value, SIDE - move, 1)
            return jnp.where(lane < SIDE - move, here, pltpu.roll(here, 15, 0))
        here = pltpu.roll(value, move, 1)
        return jnp.where(lane >= move, here, pltpu.roll(here, 1, 0))

    for which, sense in enumerate((1, -1)):
        level = [[steps[pl.ds(16 * s, 16), :]] for s in range(NT)]
        length = 1
        while len(level) > 1:
            level = [
                [
                    level[j][d // 2] + moved(level[j + 1][d // 2], d - d // 2, sense)
                    for d in range(2 * length)
                ]
                for j in range(0, len(level), 2)
            ]
            length *= 2
        for d in range(NT):
            flat[pl.ds(8 * d, 8), :] = level[0][d][:8]
        for r in range(8):
            out_ref[which, :, pl.ds(r * SIDE, SIDE)] = flat[pl.ds(r, NT, stride=8), :] * scale


def call(body, name, args, shape, dtype, scratch, flops=1 << 20, after=(), specs=None, params=PARAMS):
    def ordered(*refs):
        body(*refs[: len(args)], *refs[len(args) + len(after) :])

    return pl.pallas_call(
        ordered,
        in_specs=(specs or [VMEM] * len(args)) + [ANY] * len(after),
        out_specs=VMEM,
        out_shape=jax.ShapeDtypeStruct(shape, dtype),
        scratch_shapes=scratch,
        compiler_params=params,
        cost_estimate=pl.CostEstimate(flops=flops, bytes_accessed=1 << 20, transcendentals=0),
        name=name,
    )(*args, *after)


def bind(body, *first):
    def bound(*refs):
        body(*first, *refs)

    return bound


def per_device(voltages, taps):
    channels, _, _, frames, length = voltages.shape
    count = taps.shape[0]
    peers = lax.axis_size("tm")
    f32, bf16 = jnp.float32, jnp.bfloat16
    fourier, cos, sin = tables(SIDE)
    back = jnp.asarray(np.ascontiguousarray(fourier.T))
    fourier, cos, sin = jnp.asarray(fourier), jnp.asarray(cos), jnp.asarray(sin)
    rows = voltages.reshape(channels, 2, 2, frames, SIDE, SIDE).transpose(0, 1, 2, 4, 3, 5)
    rows = rows.reshape(channels, 2, 2, SIDE * frames, SIDE)
    coefficients = taps.reshape(count, SIDE, SIDE).transpose(1, 0, 2).reshape(SIDE * count, SIDE)
    pairs = [(i, i + 1) for i in range(2 * peers - 1)]
    tile = (SIDE, SIDE)

    halo = (2, 2, count - 1, SIDE, SIDE)
    interleaved = (SIDE * frames, SIDE)
    first = call(
        first_pack_kernel,
        "pack_first",
        [rows],
        halo,
        bf16,
        [
            pltpu.VMEM((2, 2) + interleaved, bf16),
            pltpu.VMEM((2, 2) + interleaved, f32),
            pltpu.SemaphoreType.DMA((2, 2)),
        ],
        specs=[ANY],
        params=FIRST,
    )
    packs = [first]
    near = [lax.ppermute(first, ("half", "tm"), pairs)]

    def send(place, pols, after):
        shape = (len(pols),) + halo[1:]
        body = bind(pack_kernel, place, pols)
        value = call(body, "pack", [rows], shape, bf16, [pltpu.VMEM((2,) + interleaved, f32)], after=after)
        packs.append(value)
        near.append(lax.ppermute(value, ("half", "tm"), pairs))

    constants = [coefficients, fourier, back, cos, sin]
    scratch = [
        pltpu.VMEM((2,) + interleaved, f32),
        pltpu.VMEM((2 * SIDE, frames * SIDE), bf16),
        pltpu.VMEM((frames * SIDE, 2 * SIDE), bf16),
    ]
    flops = 300 << 20
    for place in range(1, AHEAD):
        send(place, (0, 1), [first])
    power = []
    last = channels - 1
    for place in range(last):
        args = [rows, near[place], *constants]
        power.append(call(bind(chunk_kernel, place), "chunk", args, tile, f32, scratch, flops, after=power[-1:]))
        if place + AHEAD < last:
            send(place + AHEAD, (0, 1), power[-1:])
        elif place + AHEAD == last:
            send(last, (0,), power[-1:])
            send(last, (1,), power[-1:])
    args = [rows, near[last], *constants]
    part = call(bind(first_half_kernel, last), "chunk_half", args, tile, f32, scratch, flops // 2, after=power[-1:])
    plane = 2 * peers // channels
    shipped = (16 + channels // 2 * SIDE + 16, SIDE)
    ship = call(ship_kernel, "ship", power[:5], shipped, bf16, [], after=[packs[-1]])
    across, edge = [], (channels // 2 - 1) * plane + plane - 1
    for i in range(2 * peers):
        half, at = divmod(i, peers)
        across.append((i, (1 - half) * peers + (at + plane) % peers))
    straight = [pair for pair in across if pair[0] != edge]
    target = dict(across)[edge]
    beside = edge - 4
    theirs = lax.ppermute(ship, ("half", "tm"), straight)
    relayed = lax.ppermute(ship, ("half", "tm"), [(edge, beside)])
    relayed = lax.ppermute(relayed, ("half", "tm"), [(beside, target)])
    every = pltpu.VMEM((8 + 4 * SIDE + 8, SIDE), f32)
    sent = (2 * peers * SENT, SIDE)
    out = call(
        bind(last_kernel, last),
        "last",
        [rows, near[last + 1], *constants, part, power[0], power[3], power[4], power[5], power[6], theirs, relayed],
        sent,
        bf16,
        scratch + [every, pltpu.VMEM(sent, f32), pltpu.VMEM(shipped, f32)],
        flops // 2,
    )
    out = out.reshape(peers, SENT, 2, SIDE)
    owned = lax.all_to_all(out, "tm", split_axis=0, concat_axis=0, tiled=True).reshape(sent)
    scale = 1.0 / (frames * 2 * peers)
    return call(
        bind(tree_kernel, scale),
        "tree",
        [owned],
        (2, NT, channels * length // (2 * peers)),
        f32,
        [pltpu.VMEM(sent, f32), pltpu.VMEM((16 * NT, SIDE), f32), pltpu.VMEM((8 * NT, SIDE), f32)],
    )


def solution(mesh):
    peers, groups = mesh.shape["tm"], mesh.shape["chan"]
    halves = Mesh(mesh.devices.reshape(2, peers // 2, groups), ("half", "tm", "chan"))
    split = ("half", "tm")
    placed = (P("chan", None, None, split, None), P())
    return jax.shard_map(per_device, mesh=halves, in_specs=placed, out_specs=P("chan", None, split), check_vma=False)
```

time: 109 us -> 102 us (0.936)
  the two profiles are of different devices: /device:TPU:8 before, /device:TPU:256 now
where the time goes in v3:
time: 102 us; the launch traced here: 101 us
  starting transfers between devices  46 us (45%)
  blocking collectives  22.6 us (22%)
  waiting for transfers between devices  16.4 us (16%)
  Pallas kernels  12.9 us (13%)
  local copies, waits for them, and re-layouts  3.22 us (3%)
    ppermute x8, starting transfers between devices, send(): near.append(lax.ppermute(value, ('half', 'tm'), pairs))  29.8 us
    all_to_all x1, blocking collectives, per_device(): lax.all_to_all(out, 'tm', split_axis=0, concat_axis=0, tiled=True)  22.6 us
    ppermute x8, waiting for transfers between devices, send(): near.append(lax.ppermute(value, ('half', 'tm'), pairs))  12.9 us
    pallas_call x20, Pallas kernels, call(): pl.pallas_call(ordered, in_specs=(specs or [VMEM] * len(args)) + [ANY] *...  12.9 us
    ppermute x1, starting transfers between devices, per_device(): theirs = lax.ppermute(ship, ('half', 'tm'), straight)  11.5 us
    ppermute x1, waiting for transfers between devices, per_device(): theirs = lax.ppermute(ship, ('half', 'tm'), straight)  3.42 us
    ppermute x1, starting transfers between devices, per_device(): near = [lax.ppermute(first, ('half', 'tm'), pairs)]  3.4 us
    unnamed x18, local copies, waits for them, and re-layouts  3.22 us
  transfers between devices with their start and end apart: 12, of which 4 were waited for; matrix products, arithmetic and copies ran while one was open for 0% of the time, Pallas kernels for 9%

profile of v3, /device:TPU:256, one launch (start us, length us, event | category | flops | bytes accessed | tf_op | source)
XLA Modules:
  0.0 101.5 jit_solution(14336306181829170651)
XLA Ops:
  0.0 1.9 %pack_first.1.refs_1_ = bf16[2,2,3,128,128]{4,3,2,1,0:T(8,128)(2,1)} custom-call(bf16[8,2,2,512,128]{4,3,2,1,0:T(8,128)(2,1)} %bitcast.12), custom_call_target="tpu_custom_call" | custom-call | flops 1048576 | bytes 1048576 | tf_op jit(solution)/shard_map/pack_first/pallas_call | solution.py:224
  1.9 3.4 %collective-permute-start.3 = (bf16[2,2,3,128,128]{4,3,2,1,0:T(8,128)(2,1)}, bf16[2,2,3,128,128]{4,3,2,1,0:T(8,128)(2,1)S(1)}, u32[]{:S(2)}, u32[]{:S(2)}) collective-permute-start(bf16[2,2,3,128,128]{4,3,2,1,0:T(8,128)(2,1)} %pack_first.1.refs_1_), channel_id=1, source_target_pairs={{0,4},{4,8},{8,12},{12,16},{16,20},{20,24},{24,28},{28,32},{32,36}... | collective-permute-start | bytes 1179656 | tf_op jit(solution)/shard_map/ppermute | solution.py:274
  5.3 0.0 copy-start
  5.3 2.2 %copy-done = bf16[8,2,2,4,16384]{4,3,2,1,0:T(4,128)(2,1)S(1)} copy-done((bf16[8,2,2,4,16384]{4,3,2,1,0:T(4,128)(2,1)S(1)}, bf16[8,2,2,4,16384]{4,3,2,1,0:T(4,128)(2,1)}, u32[]{:S(2)}) %copy-start) | copy-done | bytes 4194328
  7.5 1.0 copy-done.5
  8.5 0.1 pack.10
  8.6 0.0 copy-start.2
  8.7 0.0 copy-start.3
  8.7 0.0 copy-start.4
  8.7 0.0 copy-start.7
  8.7 0.0 copy-start.8
  8.7 3.5 %collective-permute-start.2 = (bf16[2,2,3,128,128]{4,3,2,1,0:T(8,128)(2,1)S(1)}, bf16[2,2,3,128,128]{4,3,2,1,0:T(8,128)(2,1)S(1)}, u32[]{:S(2)}, u32[]{:S(2)}) collective-permute-start(bf16[2,2,3,128,128]{4,3,2,1,0:T(8,128)(2,1)S(1)} %pack.10), channel_id=1, source_target_pairs={{0,4},{4,8},{8,12},{12,16},{16,20},{20,24},{24,28},{28,32},{32,36}... | collective-permute-start | bytes 1179656 | tf_op jit(solution)/shard_map/ppermute | solution.py:281
  12.2 0.1 pack.9
  12.4 3.4 %collective-permute-start.1 = (bf16[2,2,3,128,128]{4,3,2,1,0:T(8,128)(2,1)S(1)}, bf16[2,2,3,128,128]{4,3,2,1,0:T(8,128)(2,1)S(1)}, u32[]{:S(2)}, u32[]{:S(2)}) collective-permute-start(bf16[2,2,3,128,128]{4,3,2,1,0:T(8,128)(2,1)S(1)} %pack.9), channel_id=1, source_target_pairs={{0,4},{4,8},{8,12},{12,16},{16,20},{20,24},{24,28},{28,32},{32,36}... | collective-permute-start | bytes 1179656 | tf_op jit(solution)/shard_map/ppermute | solution.py:281
  15.8 0.1 pack.8
  15.9 3.4 %collective-permute-start = (bf16[2,2,3,128,128]{4,3,2,1,0:T(8,128)(2,1)S(1)}, bf16[2,2,3,128,128]{4,3,2,1,0:T(8,128)(2,1)S(1)}, u32[]{:S(2)}, u32[]{:S(2)}) collective-permute-start(bf16[2,2,3,128,128]{4,3,2,1,0:T(8,128)(2,1)S(1)} %pack.8), channel_id=1, source_target_pairs={{0,4},{4,8},{8,12},{12,16},{16,20},{20,24},{24,28},{28,32},{32,36}... | collective-permute-start | bytes 1179656 | tf_op jit(solution)/shard_map/ppermute | solution.py:281
  19.3 1.1 %chunk.7.refs_7_.refs_1_.refs_0_.refs_8_ = f32[128,128]{1,0:T(8,128)S(1)} custom-call(bf16[8,2,2,512,128]{4,3,2,1,0:T(8,128)(2,1)S(1)} %bitcast.16, bf16[2,2,3,128,128]{4,3,2,1,0:T(8,128)(2,1)S(1)} %collective-permute-done.3.refs_1_, f32[512,128]{1,0:T(8,128)S(1)} %bitcast.30, bf16[256,256]{1,0:T(8,128)(2,1)S(1)} %copy-done.4, ...), custom_call_target="tpu_custom_call" | custom-call | flops 314572800 | bytes 1048576 | tf_op jit(solution)/shard_map/chunk/pallas_call | solution.py:224
  20.4 0.1 pack.15
  20.5 3.4 %collective-permute-start.8 = (bf16[2,2,3,128,128]{4,3,2,1,0:T(8,128)(2,1)S(1)}, bf16[2,2,3,128,128]{4,3,2,1,0:T(8,128)(2,1)S(1)}, u32[]{:S(2)}, u32[]{:S(2)}) collective-permute-start(bf16[2,2,3,128,128]{4,3,2,1,0:T(8,128)(2,1)S(1)} %pack.15), channel_id=1, source_target_pairs={{0,4},{4,8},{8,12},{12,16},{16,20},{20,24},{24,28},{28,32},{32,36}... | collective-permute-start | bytes 1179656 | tf_op jit(solution)/shard_map/ppermute | solution.py:281
  23.9 0.0 collective-permute-done.2.refs_1_
  23.9 1.1 %chunk.8.refs_7_.refs_1_ = f32[128,128]{1,0:T(8,128)S(1)} custom-call(bf16[8,2,2,512,128]{4,3,2,1,0:T(8,128)(2,1)S(1)} %bitcast.18, bf16[2,2,3,128,128]{4,3,2,1,0:T(8,128)(2,1)S(1)} %collective-permute-done.2.refs_1_, f32[512,128]{1,0:T(8,128)S(1)} %bitcast.31, bf16[256,256]{1,0:T(8,128)(2,1)S(1)} %copy-done.4, bf16[256,256]{1,0:T(8,128)(2,1)S(1)} %copy-done.3, ...), custom_call_target="tpu_custom_call" | custom-call | flops 314572800 | bytes 1048576 | tf_op jit(solution)/shard_map/chunk/pallas_call | solution.py:224
  25.0 0.1 pack.14
  25.1 3.9 %collective-permute-start.7 = (bf16[2,2,3,128,128]{4,3,2,1,0:T(8,128)(2,1)S(1)}, bf16[2,2,3,128,128]{4,3,2,1,0:T(8,128)(2,1)S(1)}, u32[]{:S(2)}, u32[]{:S(2)}) collective-permute-start(bf16[2,2,3,128,128]{4,3,2,1,0:T(8,128)(2,1)S(1)} %pack.14), channel_id=1, source_target_pairs={{0,4},{4,8},{8,12},{12,16},{16,20},{20,24},{24,28},{28,32},{32,36}... | collective-permute-start | bytes 1179656 | tf_op jit(solution)/shard_map/ppermute | solution.py:281
  29.0 2.8 %collective-permute-done.1.refs_1_ = bf16[2,2,3,128,128]{4,3,2,1,0:T(8,128)(2,1)S(1)} collective-permute-done((bf16[2,2,3,128,128]{4,3,2,1,0:T(8,128)(2,1)S(1)}, bf16[2,2,3,128,128]{4,3,2,1,0:T(8,128)(2,1)S(1)}, u32[]{:S(2)}, u32[]{:S(2)}) %collective-permute-start.1) | collective-permute-done | bytes 393248 | tf_op jit(solution)/shard_map/ppermute | solution.py:281
  31.9 1.0 %chunk.9.refs_7_.refs_1_.refs_2_ = f32[128,128]{1,0:T(8,128)S(1)} custom-call(bf16[8,2,2,512,128]{4,3,2,1,0:T(8,128)(2,1)S(1)} %bitcast.20, bf16[2,2,3,128,128]{4,3,2,1,0:T(8,128)(2,1)S(1)} %collective-permute-done.1.refs_1_, f32[512,128]{1,0:T(8,128)S(1)} %bitcast.32, bf16[256,256]{1,0:T(8,128)(2,1)S(1)} %copy-done.4, bf16[256,256]{1,0:T(8,128)(2,1)S(1)} %copy-done.3, ...), custom_call_target="tpu_custom_call" | custom-call | flops 314572800 | bytes 1048576 | tf_op jit(solution)/shard_map/chunk/pallas_call | solution.py:224
  32.9 0.1 pack.13
  33.1 4.4 %collective-permute-start.6 = (bf16[2,2,3,128,128]{4,3,2,1,0:T(8,128)(2,1)S(1)}, bf16[2,2,3,128,128]{4,3,2,1,0:T(8,128)(2,1)S(1)}, u32[]{:S(2)}, u32[]{:S(2)}) collective-permute-start(bf16[2,2,3,128,128]{4,3,2,1,0:T(8,128)(2,1)S(1)} %pack.13), channel_id=1, source_target_pairs={{0,4},{4,8},{8,12},{12,16},{16,20},{20,24},{24,28},{28,32},{32,36}... | collective-permute-start | bytes 1179656 | tf_op jit(solution)/shard_map/ppermute | solution.py:281
  37.5 2.8 %collective-permute-done.refs_1_ = bf16[2,2,3,128,128]{4,3,2,1,0:T(8,128)(2,1)S(1)} collective-permute-done((bf16[2,2,3,128,128]{4,3,2,1,0:T(8,128)(2,1)S(1)}, bf16[2,2,3,128,128]{4,3,2,1,0:T(8,128)(2,1)S(1)}, u32[]{:S(2)}, u32[]{:S(2)}) %collective-permute-start) | collective-permute-done | bytes 393248 | tf_op jit(solution)/shard_map/ppermute | solution.py:281
  40.3 1.0 %chunk.10.refs_1_.refs_7_.refs_3_.refs_9_ = f32[128,128]{1,0:T(8,128)S(1)} custom-call(bf16[8,2,2,512,128]{4,3,2,1,0:T(8,128)(2,1)S(1)} %bitcast.22, bf16[2,2,3,128,128]{4,3,2,1,0:T(8,128)(2,1)S(1)} %collective-permute-done.refs_1_, f32[512,128]{1,0:T(8,128)S(1)} %bitcast.33, bf16[256,256]{1,0:T(8,128)(2,1)S(1)} %copy-done.4, ...), custom_call_target="tpu_custom_call" | custom-call | flops 314572800 | bytes 1048576 | tf_op jit(solution)/shard_map/chunk/pallas_call | solution.py:224
  41.3 0.0 copy-start.1
  41.4 0.1 pack.11.refs_5_
  41.4 7.3 %collective-permute-done.8.refs_1_ = bf16[2,2,3,128,128]{4,3,2,1,0:T(8,128)(2,1)S(1)} collective-permute-done((bf16[2,2,3,128,128]{4,3,2,1,0:T(8,128)(2,1)S(1)}, bf16[2,2,3,128,128]{4,3,2,1,0:T(8,128)(2,1)S(1)}, u32[]{:S(2)}, u32[]{:S(2)}) %collective-permute-start.8) | collective-permute-done | bytes 393248 | tf_op jit(solution)/shard_map/ppermute | solution.py:281
  48.7 1.1 %chunk.11.refs_7_.refs_4_.refs_10_ = f32[128,128]{1,0:T(8,128)S(1)} custom-call(bf16[8,2,2,512,128]{4,3,2,1,0:T(8,128)(2,1)S(1)} %bitcast.24, bf16[2,2,3,128,128]{4,3,2,1,0:T(8,128)(2,1)S(1)} %collective-permute-done.8.refs_1_, f32[512,128]{1,0:T(8,128)S(1)} %bitcast.34, bf16[256,256]{1,0:T(8,128)(2,1)S(1)} %copy-done.4, bf16[256,256]{1,0:T(8,128)(2,1)S(1)} %copy-done.3, ...), custom_call_target="tpu_custom_call" | custom-call | flops 314572800 | bytes 1048576 | tf_op jit(solution)/shard_map/chunk/pallas_call | solution.py:224
  49.8 0.7 collective-permute-start.10
  50.5 0.1 pack.12
  50.6 4.4 %collective-permute-start.5 = (bf16[1,2,3,128,128]{4,3,2,1,0:T(8,128)(2,1)S(1)}, bf16[1,2,3,128,128]{4,3,2,1,0:T(8,128)(2,1)S(1)}, u32[]{:S(2)}, u32[]{:S(2)}) collective-permute-start(bf16[1,2,3,128,128]{4,3,2,1,0:T(8,128)(2,1)S(1)} %pack.12), channel_id=1, source_target_pairs={{0,4},{4,8},{8,12},{12,16},{16,20},{20,24},{24,28},{28,32},{32,36}... | collective-permute-start | bytes 589832 | tf_op jit(solution)/shard_map/ppermute | solution.py:281
  55.0 3.4 %collective-permute-start.4 = (bf16[1,2,3,128,128]{4,3,2,1,0:T(8,128)(2,1)S(1)}, bf16[1,2,3,128,128]{4,3,2,1,0:T(8,128)(2,1)S(1)}, u32[]{:S(2)}, u32[]{:S(2)}) collective-permute-start(bf16[1,2,3,128,128]{4,3,2,1,0:T(8,128)(2,1)S(1)} %pack.11.refs_5_), channel_id=1, source_target_pairs={{0,4},{4,8},{8,12},{12,16},{16,20},{20,24},{24,28},{28,32},{32,36}... | collective-permute-start | bytes 589832 | tf_op jit(solution)/shard_map/ppermute | solution.py:281
  58.4 11.5 %collective-permute-start.9 = (bf16[544,128]{1,0:T(8,128)(2,1)S(1)}, bf16[544,128]{1,0:T(8,128)(2,1)S(1)}, u32[]{:S(2)}, u32[]{:S(2)}) collective-permute-start(bf16[544,128]{1,0:T(8,128)(2,1)S(1)} %ship.1), channel_id=1, source_target_pairs={{0,320},{4,324},{8,328},{12,332},{16,336},{20,340},{24,344},{28,34... | collective-permute-start | bytes 417800 | tf_op jit(solution)/shard_map/ppermute | solution.py:314
  69.9 0.0 collective-permute-done.10
  69.9 0.7 collective-permute-start.11
  70.6 1.1 %chunk.12.refs_7_.refs_11_ = f32[128,128]{1,0:T(8,128)S(1)} custom-call(bf16[8,2,2,512,128]{4,3,2,1,0:T(8,128)(2,1)S(1)} %bitcast.26, bf16[2,2,3,128,128]{4,3,2,1,0:T(8,128)(2,1)S(1)} %collective-permute-done.7.refs_1_, f32[512,128]{1,0:T(8,128)S(1)} %bitcast.35, bf16[256,256]{1,0:T(8,128)(2,1)S(1)} %copy-done.4, bf16[256,256]{1,0:T(8,128)(2,1)S(1)} %copy-done.3, ...), custom_call_target="tpu_custom_call" | custom-call | flops 314572800 | bytes 1048576 | tf_op jit(solution)/shard_map/chunk/pallas_call | solution.py:224
  71.6 0.0 collective-permute-done.6.refs_1_
  71.7 1.1 %chunk.13.refs_7_.refs_12_ = f32[128,128]{1,0:T(8,128)S(1)} custom-call(bf16[8,2,2,512,128]{4,3,2,1,0:T(8,128)(2,1)S(1)} %bitcast.27, bf16[2,2,3,128,128]{4,3,2,1,0:T(8,128)(2,1)S(1)} %collective-permute-done.6.refs_1_, f32[512,128]{1,0:T(8,128)S(1)} %bitcast.36, bf16[256,256]{1,0:T(8,128)(2,1)S(1)} %copy-done.4, bf16[256,256]{1,0:T(8,128)(2,1)S(1)} %copy-done.3, ...), custom_call_target="tpu_custom_call" | custom-call | flops 314572800 | bytes 1048576 | tf_op jit(solution)/shard_map/chunk/pallas_call | solution.py:224
  72.7 0.6 chunk_half.1.refs_7_
  73.3 3.4 %collective-permute-done.9.refs_13_ = bf16[544,128]{1,0:T(8,128)(2,1)S(1)} collective-permute-done((bf16[544,128]{1,0:T(8,128)(2,1)S(1)}, bf16[544,128]{1,0:T(8,128)(2,1)S(1)}, u32[]{:S(2)}, u32[]{:S(2)}) %collective-permute-start.9) | collective-permute-done | bytes 139296 | tf_op jit(solution)/shard_map/ppermute | solution.py:314
  76.8 0.8 last.1
  77.6 22.6 %all_to_all.5 = bf16[64,9,2,128]{3,2,1,0:T(2,128)(2,1)S(1)} all-to-all(bf16[64,9,2,128]{3,2,1,0:T(2,128)(2,1)S(1)} %bitcast.39), channel_id=1, replica_groups=mesh['half'=2,'tm'=64,'chan'=4] {'tm'}, dimensions={0} | all-to-all | bytes 589824 | tf_op jit(solution)/shard_map/all_to_all | solution.py:329
  100.2 1.3 %tree.1 = f32[2,16,1024]{2,1,0:T(8,128)} custom-call(bf16[1152,128]{1,0:T(8,128)(2,1)S(1)} %bitcast.40), custom_call_target="tpu_custom_call" | custom-call | flops 1048576 | bytes 1048576 | tf_op jit(solution)/shard_map/tree/pallas_call | solution.py:224
  (15 shorter events, 0.0 us)
Async XLA Ops:
  1.9 17.4 %collective-permute-start.3 = (bf16[2,2,3,128,128]{4,3,2,1,0:T(8,128)(2,1)}, bf16[2,2,3,128,128]{4,3,2,1,0:T(8,128)(2,1)S(1)}, u32[]{:S(2)}, u32[]{:S(2)}) collective-permute-start(bf16[2,2,3,128,128]{4,3,2,1,0:T(8,128)(2,1)} %pack_first.1.refs_1_), channel_id=1, source_target_pairs={{0,4},{4,8},{8,12},{12,16},{16,20},{20,24},{24,28},{28,32},{32,36}... | collective-permute-start | bytes 1179656 | tf_op jit(solution)/shard_map/ppermute | solution.py:274
  5.3 2.2 %copy-start = (bf16[8,2,2,4,16384]{4,3,2,1,0:T(4,128)(2,1)S(1)}, bf16[8,2,2,4,16384]{4,3,2,1,0:T(4,128)(2,1)}, u32[]{:S(2)}) copy-start(bf16[8,2,2,4,16384]{4,3,2,1,0:T(4,128)(2,1)} %param.6) | copy-start | bytes 12582916
  7.5 1.0 copy-start.5
  8.5 3.7 %copy-start.6 = (bf16[2,2,3,128,128]{4,3,2,1,0:T(8,128)(2,1)S(1)}, bf16[2,2,3,128,128]{4,3,2,1,0:T(8,128)(2,1)}, u32[]{:S(2)}) copy-start(bf16[2,2,3,128,128]{4,3,2,1,0:T(8,128)(2,1)} %pack_first.1.refs_1_) | copy-start | bytes 1179652
  8.6 10.6 %copy-start.2 = (f32[4,16384]{1,0:T(4,128)S(1)}, f32[4,16384]{1,0:T(4,128)}, u32[]{:S(2)}) copy-start(f32[4,16384]{1,0:T(4,128)} %param.7) | copy-start | bytes 786436
  8.7 10.6 %copy-start.3 = (bf16[256,256]{1,0:T(8,128)(2,1)S(1)}, bf16[256,256]{1,0:T(8,128)(2,1)}, u32[]{:S(2)}) copy-start(bf16[256,256]{1,0:T(8,128)(2,1)} %constant.8.clone.refs_4_) | copy-start | bytes 393220
  8.7 10.6 %copy-start.4 = (bf16[256,256]{1,0:T(8,128)(2,1)S(1)}, bf16[256,256]{1,0:T(8,128)(2,1)}, u32[]{:S(2)}) copy-start(bf16[256,256]{1,0:T(8,128)(2,1)} %constant.9.clone.refs_3_) | copy-start | bytes 393220
  8.7 10.6 %copy-start.7 = (f32[128,128]{1,0:T(8,128)S(1)}, f32[128,128]{1,0:T(8,128)}, u32[]{:S(2)}) copy-start(f32[128,128]{1,0:T(8,128)} %constant.10.clone.refs_5_) | copy-start | bytes 196612
  8.7 10.6 %copy-start.8 = (f32[128,128]{1,0:T(8,128)S(1)}, f32[128,128]{1,0:T(8,128)}, u32[]{:S(2)}) copy-start(f32[128,128]{1,0:T(8,128)} %constant.11.clone.refs_6_) | copy-start | bytes 196612
  8.7 15.2 %collective-permute-start.2 = (bf16[2,2,3,128,128]{4,3,2,1,0:T(8,128)(2,1)S(1)}, bf16[2,2,3,128,128]{4,3,2,1,0:T(8,128)(2,1)S(1)}, u32[]{:S(2)}, u32[]{:S(2)}) collective-permute-start(bf16[2,2,3,128,128]{4,3,2,1,0:T(8,128)(2,1)S(1)} %pack.10), channel_id=1, source_target_pairs={{0,4},{4,8},{8,12},{12,16},{16,20},{20,24},{24,28},{28,32},{32,36}... | collective-permute-start | bytes 1179656 | tf_op jit(solution)/shard_map/ppermute | solution.py:281
  12.4 19.5 %collective-permute-start.1 = (bf16[2,2,3,128,128]{4,3,2,1,0:T(8,128)(2,1)S(1)}, bf16[2,2,3,128,128]{4,3,2,1,0:T(8,128)(2,1)S(1)}, u32[]{:S(2)}, u32[]{:S(2)}) collective-permute-start(bf16[2,2,3,128,128]{4,3,2,1,0:T(8,128)(2,1)S(1)} %pack.9), channel_id=1, source_target_pairs={{0,4},{4,8},{8,12},{12,16},{16,20},{20,24},{24,28},{28,32},{32,36}... | collective-permute-start | bytes 1179656 | tf_op jit(solution)/shard_map/ppermute | solution.py:281
  15.9 24.4 %collective-permute-start = (bf16[2,2,3,128,128]{4,3,2,1,0:T(8,128)(2,1)S(1)}, bf16[2,2,3,128,128]{4,3,2,1,0:T(8,128)(2,1)S(1)}, u32[]{:S(2)}, u32[]{:S(2)}) collective-permute-start(bf16[2,2,3,128,128]{4,3,2,1,0:T(8,128)(2,1)S(1)} %pack.8), channel_id=1, source_target_pairs={{0,4},{4,8},{8,12},{12,16},{16,20},{20,24},{24,28},{28,32},{32,36}... | collective-permute-start | bytes 1179656 | tf_op jit(solution)/shard_map/ppermute | solution.py:281
  20.5 28.2 %collective-permute-start.8 = (bf16[2,2,3,128,128]{4,3,2,1,0:T(8,128)(2,1)S(1)}, bf16[2,2,3,128,128]{4,3,2,1,0:T(8,128)(2,1)S(1)}, u32[]{:S(2)}, u32[]{:S(2)}) collective-permute-start(bf16[2,2,3,128,128]{4,3,2,1,0:T(8,128)(2,1)S(1)} %pack.15), channel_id=1, source_target_pairs={{0,4},{4,8},{8,12},{12,16},{16,20},{20,24},{24,28},{28,32},{32,36}... | collective-permute-start | bytes 1179656 | tf_op jit(solution)/shard_map/ppermute | solution.py:281
  25.1 33.2 %collective-permute-start.7 = (bf16[2,2,3,128,128]{4,3,2,1,0:T(8,128)(2,1)S(1)}, bf16[2,2,3,128,128]{4,3,2,1,0:T(8,128)(2,1)S(1)}, u32[]{:S(2)}, u32[]{:S(2)}) collective-permute-start(bf16[2,2,3,128,128]{4,3,2,1,0:T(8,128)(2,1)S(1)} %pack.14), channel_id=1, source_target_pairs={{0,4},{4,8},{8,12},{12,16},{16,20},{20,24},{24,28},{28,32},{32,36}... | collective-permute-start | bytes 1179656 | tf_op jit(solution)/shard_map/ppermute | solution.py:281
  33.1 38.6 %collective-permute-start.6 = (bf16[2,2,3,128,128]{4,3,2,1,0:T(8,128)(2,1)S(1)}, bf16[2,2,3,128,128]{4,3,2,1,0:T(8,128)(2,1)S(1)}, u32[]{:S(2)}, u32[]{:S(2)}) collective-permute-start(bf16[2,2,3,128,128]{4,3,2,1,0:T(8,128)(2,1)S(1)} %pack.13), channel_id=1, source_target_pairs={{0,4},{4,8},{8,12},{12,16},{16,20},{20,24},{24,28},{28,32},{32,36}... | collective-permute-start | bytes 1179656 | tf_op jit(solution)/shard_map/ppermute | solution.py:281
  41.3 9.1 %copy-start.1 = (bf16[8,2,2,4,16384]{4,3,2,1,0:T(4,128)(2,1)S(1)}, bf16[8,2,2,4,16384]{4,3,2,1,0:T(4,128)(2,1)}, u32[]{:S(2)}) copy-start(bf16[8,2,2,4,16384]{4,3,2,1,0:T(4,128)(2,1)} %param.6) | copy-start | bytes 12582916
  49.8 20.1 %collective-permute-start.10 = (bf16[544,128]{1,0:T(8,128)(2,1)S(1)}, bf16[544,128]{1,0:T(8,128)(2,1)S(1)}, u32[]{:S(2)}, u32[]{:S(2)}) collective-permute-start(bf16[544,128]{1,0:T(8,128)(2,1)S(1)} %ship.1), channel_id=1, source_target_pairs={{252,236},{253,237},{254,238},{255,239}} | collective-permute-start | bytes 417800 | tf_op jit(solution)/shard_map/ppermute | solution.py:315
  50.6 22.1 %collective-permute-start.5 = (bf16[1,2,3,128,128]{4,3,2,1,0:T(8,128)(2,1)S(1)}, bf16[1,2,3,128,128]{4,3,2,1,0:T(8,128)(2,1)S(1)}, u32[]{:S(2)}, u32[]{:S(2)}) collective-permute-start(bf16[1,2,3,128,128]{4,3,2,1,0:T(8,128)(2,1)S(1)} %pack.12), channel_id=1, source_target_pairs={{0,4},{4,8},{8,12},{12,16},{16,20},{20,24},{24,28},{28,32},{32,36}... | collective-permute-start | bytes 589832 | tf_op jit(solution)/shard_map/ppermute | solution.py:281
  55.0 18.4 %collective-permute-start.4 = (bf16[1,2,3,128,128]{4,3,2,1,0:T(8,128)(2,1)S(1)}, bf16[1,2,3,128,128]{4,3,2,1,0:T(8,128)(2,1)S(1)}, u32[]{:S(2)}, u32[]{:S(2)}) collective-permute-start(bf16[1,2,3,128,128]{4,3,2,1,0:T(8,128)(2,1)S(1)} %pack.11.refs_5_), channel_id=1, source_target_pairs={{0,4},{4,8},{8,12},{12,16},{16,20},{20,24},{24,28},{28,32},{32,36}... | collective-permute-start | bytes 589832 | tf_op jit(solution)/shard_map/ppermute | solution.py:281
  58.4 18.4 %collective-permute-start.9 = (bf16[544,128]{1,0:T(8,128)(2,1)S(1)}, bf16[544,128]{1,0:T(8,128)(2,1)S(1)}, u32[]{:S(2)}, u32[]{:S(2)}) collective-permute-start(bf16[544,128]{1,0:T(8,128)(2,1)S(1)} %ship.1), channel_id=1, source_target_pairs={{0,320},{4,324},{8,328},{12,332},{16,336},{20,340},{24,344},{28,34... | collective-permute-start | bytes 417800 | tf_op jit(solution)/shard_map/ppermute | solution.py:314
  69.9 6.9 %collective-permute-start.11 = (bf16[544,128]{1,0:T(8,128)(2,1)S(1)}, bf16[544,128]{1,0:T(8,128)(2,1)S(1)}, u32[]{:S(2)}, u32[]{:S(2)}) collective-permute-start(bf16[544,128]{1,0:T(8,128)(2,1)S(1)} %collective-permute-done.10), channel_id=1, source_target_pairs={{236,316},{237,317},{238,318},{239,319}} | collective-permute-start | bytes 417800 | tf_op jit(solution)/shard_map/ppermute | solution.py:316

commit v4 on v3

--- a/solution.py
+++ b/solution.py
@@ -16,7 +16,7 @@
 AHEAD = 4
 SENT = 9
 PARAMS = pltpu.CompilerParams(vmem_limit_bytes=12 << 20)
-FIRST = pltpu.CompilerParams(vmem_limit_bytes=63_000_000)
+FIRST = pltpu.CompilerParams(vmem_limit_bytes=56_000_000)
 VMEM = pl.BlockSpec(memory_space=pltpu.VMEM)
 ANY = pl.BlockSpec(memory_space=pl.ANY)
 
@@ -289,11 +289,26 @@
     flops = 300 << 20
     for place in range(1, AHEAD):
         send(place, (0, 1), [first])
+    plane = 2 * peers // channels
+    shipped = (16 + channels // 2 * SIDE + 16, SIDE)
+    across, edge = [], (channels // 2 - 1) * plane + plane - 1
+    for i in range(2 * peers):
+        half, at = divmod(i, peers)
+        across.append((i, (1 - half) * peers + (at + plane) % peers))
+    straight = [pair for pair in across if pair[0] != edge]
+    target = dict(across)[edge]
+    beside = edge - 4
     power = []
     last = channels - 1
     for place in range(last):
         args = [rows, near[place], *constants]
-        power.append(call(bind(chunk_kernel, place), "chunk", args, tile, f32, scratch, flops, after=power[-1:]))
+        order = power[-1:] + ([theirs, by] if place == last - 2 else [])
+        power.append(call(bind(chunk_kernel, place), "chunk", args, tile, f32, scratch, flops, after=order))
+        if place == channels // 2:
+            ship = call(ship_kernel, "ship", power[:5], shipped, bf16, [], after=[packs[-1]])
+            theirs = lax.ppermute(ship, ("half", "tm"), straight)
+            by = lax.ppermute(ship, ("half", "tm"), [(edge, beside)])
+            relayed = lax.ppermute(by, ("half", "tm"), [(beside, target)])
         if place + AHEAD < last:
             send(place + AHEAD, (0, 1), power[-1:])
         elif place + AHEAD == last:
@@ -301,19 +316,6 @@
             send(last, (1,), power[-1:])
     args = [rows, near[last], *constants]
     part = call(bind(first_half_kernel, last), "chunk_half", args, tile, f32, scratch, flops // 2, after=power[-1:])
-    plane = 2 * peers // channels
-    shipped = (16 + channels // 2 * SIDE + 16, SIDE)
-    ship = call(ship_kernel, "ship", power[:5], shipped, bf16, [], after=[packs[-1]])
-    across, edge = [], (channels // 2 - 1) * plane + plane - 1
-    for i in range(2 * peers):
-        half, at = divmod(i, peers)
-        across.append((i, (1 - half) * peers + (at + plane) % peers))
-    straight = [pair for pair in across if pair[0] != edge]
-    target = dict(across)[edge]
-    beside = edge - 4
-    theirs = lax.ppermute(ship, ("half", "tm"), straight)
-    relayed = lax.ppermute(ship, ("half", "tm"), [(edge, beside)])
-    relayed = lax.ppermute(relayed, ("half", "tm"), [(beside, target)])
     every = pltpu.VMEM((8 + 4 * SIDE + 8, SIDE), f32)
     sent = (2 * peers * SENT, SIDE)
     out = call(

time: 102 us -> 101 us (level)
  the two profiles are of different devices: /device:TPU:256 before, /device:TPU:2 now
where the time goes in v4:
time: 101 us; the launch traced here: 100 us
  starting transfers between devices  33.7 us (33%)
  waiting for transfers between devices  33 us (33%)
  blocking collectives  20.7 us (20%)
  Pallas kernels  12.5 us (12%)
    ppermute x8, waiting for transfers between devices, send(): near.append(lax.ppermute(value, ('half', 'tm'), pairs))  28.6 us
    ppermute x8, starting transfers between devices, send(): near.append(lax.ppermute(value, ('half', 'tm'), pairs))  21 us
    all_to_all x1, blocking collectives, per_device(): lax.all_to_all(out, 'tm', split_axis=0, concat_axis=0, tiled=True)  20.7 us
    pallas_call x20, Pallas kernels, call(): pl.pallas_call(ordered, in_specs=(specs or [VMEM] * len(args)) + [ANY] *...  12.5 us
    ppermute x1, starting transfers between devices, per_device(): theirs = lax.ppermute(ship, ('half', 'tm'), straight)  6.95 us
    ppermute x1, starting transfers between devices, per_device(): near = [lax.ppermute(first, ('half', 'tm'), pairs)]  4.41 us
    ppermute x1, waiting for transfers between devices, per_device(): near = [lax.ppermute(first, ('half', 'tm'), pairs)]  2.39 us
    ppermute x1, waiting for transfers between devices, per_device(): theirs = lax.ppermute(ship, ('half', 'tm'), straight)  2.05 us
  transfers between devices with their start and end apart: 12, of which 8 were waited for; matrix products, arithmetic and copies ran while one was open for 0% of the time, Pallas kernels for 9%

profile of v4, /device:TPU:2, one launch (start us, length us, event | category | flops | bytes accessed | tf_op | source)
XLA Modules:
  0.0 100.2 jit_solution(15667878891932909411)
XLA Ops:
  0.0 1.3 %pack_first.1.refs_1_ = bf16[2,2,3,128,128]{4,3,2,1,0:T(8,128)(2,1)S(1)} custom-call(bf16[8,2,2,512,128]{4,3,2,1,0:T(8,128)(2,1)} %bitcast.12), custom_call_target="tpu_custom_call" | custom-call | flops 1048576 | bytes 1048576 | tf_op jit(solution)/shard_map/pack_first/pallas_call | solution.py:224
  1.3 4.4 %collective-permute-start.3 = (bf16[2,2,3,128,128]{4,3,2,1,0:T(8,128)(2,1)S(1)}, bf16[2,2,3,128,128]{4,3,2,1,0:T(8,128)(2,1)S(1)}, u32[]{:S(2)}, u32[]{:S(2)}) collective-permute-start(bf16[2,2,3,128,128]{4,3,2,1,0:T(8,128)(2,1)S(1)} %pack_first.1.refs_1_), channel_id=1, source_target_pairs={{0,4},{4,8},{8,12},{12,16},{16,20},{20,24},{24,28},{28,32},{32,36}... | collective-permute-start | bytes 1179656 | tf_op jit(solution)/shard_map/ppermute | solution.py:274
  5.7 0.1 pack.10
  5.9 0.0 copy-start.1
  5.9 0.0 copy-start.2
  5.9 0.0 copy-start.3
  5.9 0.0 copy-start.4
  5.9 0.0 copy-start.5
  6.0 4.4 %collective-permute-start.2 = (bf16[2,2,3,128,128]{4,3,2,1,0:T(8,128)(2,1)S(1)}, bf16[2,2,3,128,128]{4,3,2,1,0:T(8,128)(2,1)S(1)}, u32[]{:S(2)}, u32[]{:S(2)}) collective-permute-start(bf16[2,2,3,128,128]{4,3,2,1,0:T(8,128)(2,1)S(1)} %pack.10), channel_id=1, source_target_pairs={{0,4},{4,8},{8,12},{12,16},{16,20},{20,24},{24,28},{28,32},{32,36}... | collective-permute-start | bytes 1179656 | tf_op jit(solution)/shard_map/ppermute | solution.py:281
  10.4 0.1 pack.9
  10.5 4.3 %collective-permute-start.1 = (bf16[2,2,3,128,128]{4,3,2,1,0:T(8,128)(2,1)S(1)}, bf16[2,2,3,128,128]{4,3,2,1,0:T(8,128)(2,1)S(1)}, u32[]{:S(2)}, u32[]{:S(2)}) collective-permute-start(bf16[2,2,3,128,128]{4,3,2,1,0:T(8,128)(2,1)S(1)} %pack.9), channel_id=1, source_target_pairs={{0,4},{4,8},{8,12},{12,16},{16,20},{20,24},{24,28},{28,32},{32,36}... | collective-permute-start | bytes 1179656 | tf_op jit(solution)/shard_map/ppermute | solution.py:281
  14.8 0.1 pack.8
  14.9 1.9 %collective-permute-start = (bf16[2,2,3,128,128]{4,3,2,1,0:T(8,128)(2,1)S(1)}, bf16[2,2,3,128,128]{4,3,2,1,0:T(8,128)(2,1)S(1)}, u32[]{:S(2)}, u32[]{:S(2)}) collective-permute-start(bf16[2,2,3,128,128]{4,3,2,1,0:T(8,128)(2,1)S(1)} %pack.8), channel_id=1, source_target_pairs={{0,4},{4,8},{8,12},{12,16},{16,20},{20,24},{24,28},{28,32},{32,36}... | collective-permute-start | bytes 1179656 | tf_op jit(solution)/shard_map/ppermute | solution.py:281
  16.9 2.4 %collective-permute-done.3.refs_1_ = bf16[2,2,3,128,128]{4,3,2,1,0:T(8,128)(2,1)S(1)} collective-permute-done((bf16[2,2,3,128,128]{4,3,2,1,0:T(8,128)(2,1)S(1)}, bf16[2,2,3,128,128]{4,3,2,1,0:T(8,128)(2,1)S(1)}, u32[]{:S(2)}, u32[]{:S(2)}) %collective-permute-start.3) | collective-permute-done | bytes 393248 | tf_op jit(solution)/shard_map/ppermute | solution.py:274
  19.3 1.1 %chunk.7.refs_7_.refs_1_.refs_0_.refs_8_ = f32[128,128]{1,0:T(8,128)S(1)} custom-call(bf16[8,2,2,512,128]{4,3,2,1,0:T(8,128)(2,1)S(1)} %bitcast.16, bf16[2,2,3,128,128]{4,3,2,1,0:T(8,128)(2,1)S(1)} %collective-permute-done.3.refs_1_, f32[512,128]{1,0:T(8,128)S(1)} %bitcast.30, bf16[256,256]{1,0:T(8,128)(2,1)S(1)} %copy-done.3, ...), custom_call_target="tpu_custom_call" | custom-call | flops 314572800 | bytes 1048576 | tf_op jit(solution)/shard_map/chunk/pallas_call | solution.py:224
  20.4 0.1 pack.15
  20.5 1.9 %collective-permute-start.8 = (bf16[2,2,3,128,128]{4,3,2,1,0:T(8,128)(2,1)S(1)}, bf16[2,2,3,128,128]{4,3,2,1,0:T(8,128)(2,1)S(1)}, u32[]{:S(2)}, u32[]{:S(2)}) collective-permute-start(bf16[2,2,3,128,128]{4,3,2,1,0:T(8,128)(2,1)S(1)} %pack.15), channel_id=1, source_target_pairs={{0,4},{4,8},{8,12},{12,16},{16,20},{20,24},{24,28},{28,32},{32,36}... | collective-permute-start | bytes 1179656 | tf_op jit(solution)/shard_map/ppermute | solution.py:281
  22.4 5.3 %collective-permute-done.2.refs_1_ = bf16[2,2,3,128,128]{4,3,2,1,0:T(8,128)(2,1)S(1)} collective-permute-done((bf16[2,2,3,128,128]{4,3,2,1,0:T(8,128)(2,1)S(1)}, bf16[2,2,3,128,128]{4,3,2,1,0:T(8,128)(2,1)S(1)}, u32[]{:S(2)}, u32[]{:S(2)}) %collective-permute-start.2) | collective-permute-done | bytes 393248 | tf_op jit(solution)/shard_map/ppermute | solution.py:281
  27.7 1.1 %chunk.8.refs_7_.refs_1_ = f32[128,128]{1,0:T(8,128)S(1)} custom-call(bf16[8,2,2,512,128]{4,3,2,1,0:T(8,128)(2,1)S(1)} %bitcast.18, bf16[2,2,3,128,128]{4,3,2,1,0:T(8,128)(2,1)S(1)} %collective-permute-done.2.refs_1_, f32[512,128]{1,0:T(8,128)S(1)} %bitcast.31, bf16[256,256]{1,0:T(8,128)(2,1)S(1)} %copy-done.3, bf16[256,256]{1,0:T(8,128)(2,1)S(1)} %copy-done.2, ...), custom_call_target="tpu_custom_call" | custom-call | flops 314572800 | bytes 1048576 | tf_op jit(solution)/shard_map/chunk/pallas_call | solution.py:224
  28.8 0.1 pack.14
  28.9 1.9 %collective-permute-start.7 = (bf16[2,2,3,128,128]{4,3,2,1,0:T(8,128)(2,1)S(1)}, bf16[2,2,3,128,128]{4,3,2,1,0:T(8,128)(2,1)S(1)}, u32[]{:S(2)}, u32[]{:S(2)}) collective-permute-start(bf16[2,2,3,128,128]{4,3,2,1,0:T(8,128)(2,1)S(1)} %pack.14), channel_id=1, source_target_pairs={{0,4},{4,8},{8,12},{12,16},{16,20},{20,24},{24,28},{28,32},{32,36}... | collective-permute-start | bytes 1179656 | tf_op jit(solution)/shard_map/ppermute | solution.py:281
  30.8 5.3 %collective-permute-done.1.refs_1_ = bf16[2,2,3,128,128]{4,3,2,1,0:T(8,128)(2,1)S(1)} collective-permute-done((bf16[2,2,3,128,128]{4,3,2,1,0:T(8,128)(2,1)S(1)}, bf16[2,2,3,128,128]{4,3,2,1,0:T(8,128)(2,1)S(1)}, u32[]{:S(2)}, u32[]{:S(2)}) %collective-permute-start.1) | collective-permute-done | bytes 393248 | tf_op jit(solution)/shard_map/ppermute | solution.py:281
  36.1 1.1 %chunk.9.refs_7_.refs_1_.refs_2_ = f32[128,128]{1,0:T(8,128)S(1)} custom-call(bf16[8,2,2,512,128]{4,3,2,1,0:T(8,128)(2,1)S(1)} %bitcast.20, bf16[2,2,3,128,128]{4,3,2,1,0:T(8,128)(2,1)S(1)} %collective-permute-done.1.refs_1_, f32[512,128]{1,0:T(8,128)S(1)} %bitcast.32, bf16[256,256]{1,0:T(8,128)(2,1)S(1)} %copy-done.3, bf16[256,256]{1,0:T(8,128)(2,1)S(1)} %copy-done.2, ...), custom_call_target="tpu_custom_call" | custom-call | flops 314572800 | bytes 1048576 | tf_op jit(solution)/shard_map/chunk/pallas_call | solution.py:224
  37.2 0.1 pack.13
  37.3 1.9 %collective-permute-start.6 = (bf16[2,2,3,128,128]{4,3,2,1,0:T(8,128)(2,1)S(1)}, bf16[2,2,3,128,128]{4,3,2,1,0:T(8,128)(2,1)S(1)}, u32[]{:S(2)}, u32[]{:S(2)}) collective-permute-start(bf16[2,2,3,128,128]{4,3,2,1,0:T(8,128)(2,1)S(1)} %pack.13), channel_id=1, source_target_pairs={{0,4},{4,8},{8,12},{12,16},{16,20},{20,24},{24,28},{28,32},{32,36}... | collective-permute-start | bytes 1179656 | tf_op jit(solution)/shard_map/ppermute | solution.py:281
  39.2 5.3 %collective-permute-done.refs_1_ = bf16[2,2,3,128,128]{4,3,2,1,0:T(8,128)(2,1)S(1)} collective-permute-done((bf16[2,2,3,128,128]{4,3,2,1,0:T(8,128)(2,1)S(1)}, bf16[2,2,3,128,128]{4,3,2,1,0:T(8,128)(2,1)S(1)}, u32[]{:S(2)}, u32[]{:S(2)}) %collective-permute-start) | collective-permute-done | bytes 393248 | tf_op jit(solution)/shard_map/ppermute | solution.py:281
  44.5 1.1 %chunk.10.refs_1_.refs_7_.refs_3_.refs_9_ = f32[128,128]{1,0:T(8,128)S(1)} custom-call(bf16[8,2,2,512,128]{4,3,2,1,0:T(8,128)(2,1)S(1)} %bitcast.22, bf16[2,2,3,128,128]{4,3,2,1,0:T(8,128)(2,1)S(1)} %collective-permute-done.refs_1_, f32[512,128]{1,0:T(8,128)S(1)} %bitcast.33, bf16[256,256]{1,0:T(8,128)(2,1)S(1)} %copy-done.3, ...), custom_call_target="tpu_custom_call" | custom-call | flops 314572800 | bytes 1048576 | tf_op jit(solution)/shard_map/chunk/pallas_call | solution.py:224
  45.6 0.1 pack.11.refs_5_
  45.7 7.3 %collective-permute-done.8.refs_1_ = bf16[2,2,3,128,128]{4,3,2,1,0:T(8,128)(2,1)S(1)} collective-permute-done((bf16[2,2,3,128,128]{4,3,2,1,0:T(8,128)(2,1)S(1)}, bf16[2,2,3,128,128]{4,3,2,1,0:T(8,128)(2,1)S(1)}, u32[]{:S(2)}, u32[]{:S(2)}) %collective-permute-start.8) | collective-permute-done | bytes 393248 | tf_op jit(solution)/shard_map/ppermute | solution.py:281
  53.0 1.1 %chunk.11.refs_4_.refs_7_.refs_10_ = f32[128,128]{1,0:T(8,128)S(1)} custom-call(bf16[8,2,2,512,128]{4,3,2,1,0:T(8,128)(2,1)S(1)} %bitcast.24, bf16[2,2,3,128,128]{4,3,2,1,0:T(8,128)(2,1)S(1)} %collective-permute-done.8.refs_1_, f32[512,128]{1,0:T(8,128)S(1)} %bitcast.34, bf16[256,256]{1,0:T(8,128)(2,1)S(1)} %copy-done.3, bf16[256,256]{1,0:T(8,128)(2,1)S(1)} %copy-done.2, ...), custom_call_target="tpu_custom_call" | custom-call | flops 314572800 | bytes 1048576 | tf_op jit(solution)/shard_map/chunk/pallas_call | solution.py:224
  54.1 0.7 collective-permute-start.10
  54.7 6.9 %collective-permute-start.9 = (bf16[544,128]{1,0:T(8,128)(2,1)S(1)}, bf16[544,128]{1,0:T(8,128)(2,1)S(1)}, u32[]{:S(2)}, u32[]{:S(2)}) collective-permute-start(bf16[544,128]{1,0:T(8,128)(2,1)S(1)} %ship.1), channel_id=1, source_target_pairs={{0,320},{4,324},{8,328},{12,332},{16,336},{20,340},{24,344},{28,34... | collective-permute-start | bytes 417800 | tf_op jit(solution)/shard_map/ppermute | solution.py:309
  61.7 0.1 pack.12
  61.8 1.9 %collective-permute-start.5 = (bf16[1,2,3,128,128]{4,3,2,1,0:T(8,128)(2,1)S(1)}, bf16[1,2,3,128,128]{4,3,2,1,0:T(8,128)(2,1)S(1)}, u32[]{:S(2)}, u32[]{:S(2)}) collective-permute-start(bf16[1,2,3,128,128]{4,3,2,1,0:T(8,128)(2,1)S(1)} %pack.12), channel_id=1, source_target_pairs={{0,4},{4,8},{8,12},{12,16},{16,20},{20,24},{24,28},{28,32},{32,36}... | collective-permute-start | bytes 589832 | tf_op jit(solution)/shard_map/ppermute | solution.py:281
  63.7 2.7 %collective-permute-start.4 = (bf16[1,2,3,128,128]{4,3,2,1,0:T(8,128)(2,1)S(1)}, bf16[1,2,3,128,128]{4,3,2,1,0:T(8,128)(2,1)S(1)}, u32[]{:S(2)}, u32[]{:S(2)}) collective-permute-start(bf16[1,2,3,128,128]{4,3,2,1,0:T(8,128)(2,1)S(1)} %pack.11.refs_5_), channel_id=1, source_target_pairs={{0,4},{4,8},{8,12},{12,16},{16,20},{20,24},{24,28},{28,32},{32,36}... | collective-permute-start | bytes 589832 | tf_op jit(solution)/shard_map/ppermute | solution.py:281
  66.4 0.0 collective-permute-done.10.refs_9_
  66.5 0.7 collective-permute-start.11
  67.1 2.1 %collective-permute-done.9.refs_8_.refs_13_ = bf16[544,128]{1,0:T(8,128)(2,1)S(1)} collective-permute-done((bf16[544,128]{1,0:T(8,128)(2,1)S(1)}, bf16[544,128]{1,0:T(8,128)(2,1)S(1)}, u32[]{:S(2)}, u32[]{:S(2)}) %collective-permute-start.9) | collective-permute-done | bytes 139296 | tf_op jit(solution)/shard_map/ppermute | solution.py:309
  69.2 1.1 %chunk.12.refs_7_.refs_11_ = f32[128,128]{1,0:T(8,128)S(1)} custom-call(bf16[8,2,2,512,128]{4,3,2,1,0:T(8,128)(2,1)S(1)} %bitcast.26, bf16[2,2,3,128,128]{4,3,2,1,0:T(8,128)(2,1)S(1)} %collective-permute-done.7.refs_1_, f32[512,128]{1,0:T(8,128)S(1)} %bitcast.35, bf16[256,256]{1,0:T(8,128)(2,1)S(1)} %copy-done.3, bf16[256,256]{1,0:T(8,128)(2,1)S(1)} %copy-done.2, ...), custom_call_target="tpu_custom_call" | custom-call | flops 314572800 | bytes 1048576 | tf_op jit(solution)/shard_map/chunk/pallas_call | solution.py:224
  70.3 0.0 collective-permute-done.6.refs_1_
  70.3 1.1 %chunk.13.refs_7_.refs_12_ = f32[128,128]{1,0:T(8,128)S(1)} custom-call(bf16[8,2,2,512,128]{4,3,2,1,0:T(8,128)(2,1)S(1)} %bitcast.27, bf16[2,2,3,128,128]{4,3,2,1,0:T(8,128)(2,1)S(1)} %collective-permute-done.6.refs_1_, f32[512,128]{1,0:T(8,128)S(1)} %bitcast.36, bf16[256,256]{1,0:T(8,128)(2,1)S(1)} %copy-done.3, bf16[256,256]{1,0:T(8,128)(2,1)S(1)} %copy-done.2, ...), custom_call_target="tpu_custom_call" | custom-call | flops 314572800 | bytes 1048576 | tf_op jit(solution)/shard_map/chunk/pallas_call | solution.py:224
  71.3 2.9 %collective-permute-done.5.refs_1_ = bf16[1,2,3,128,128]{4,3,2,1,0:T(8,128)(2,1)S(1)} collective-permute-done((bf16[1,2,3,128,128]{4,3,2,1,0:T(8,128)(2,1)S(1)}, bf16[1,2,3,128,128]{4,3,2,1,0:T(8,128)(2,1)S(1)}, u32[]{:S(2)}, u32[]{:S(2)}) %collective-permute-start.5) | collective-permute-done | bytes 196640 | tf_op jit(solution)/shard_map/ppermute | solution.py:281
  74.2 0.6 chunk_half.1.refs_7_
  74.8 2.6 %collective-permute-done.4.refs_1_ = bf16[1,2,3,128,128]{4,3,2,1,0:T(8,128)(2,1)S(1)} collective-permute-done((bf16[1,2,3,128,128]{4,3,2,1,0:T(8,128)(2,1)S(1)}, bf16[1,2,3,128,128]{4,3,2,1,0:T(8,128)(2,1)S(1)}, u32[]{:S(2)}, u32[]{:S(2)}) %collective-permute-start.4) | collective-permute-done | bytes 196640 | tf_op jit(solution)/shard_map/ppermute | solution.py:281
  77.4 0.0 collective-permute-done.11.refs_14_
  77.4 0.8 last.1
  78.2 20.7 %all_to_all.5 = bf16[64,9,2,128]{3,2,1,0:T(2,128)(2,1)S(1)} all-to-all(bf16[64,9,2,128]{3,2,1,0:T(2,128)(2,1)S(1)} %bitcast.39), channel_id=1, replica_groups=mesh['half'=2,'tm'=64,'chan'=4] {'tm'}, dimensions={0} | all-to-all | bytes 589824 | tf_op jit(solution)/shard_map/all_to_all | solution.py:331
  98.9 1.3 %tree.1 = f32[2,16,1024]{2,1,0:T(8,128)} custom-call(bf16[1152,128]{1,0:T(8,128)(2,1)S(1)} %bitcast.40), custom_call_target="tpu_custom_call" | custom-call | flops 1048576 | bytes 1048576 | tf_op jit(solution)/shard_map/tree/pallas_call | solution.py:224
  (9 shorter events, 0.0 us)
Async XLA Ops:
  0.0 5.7 %copy-start = (bf16[8,2,2,4,16384]{4,3,2,1,0:T(4,128)(2,1)S(1)}, bf16[8,2,2,4,16384]{4,3,2,1,0:T(4,128)(2,1)}, u32[]{:S(2)}) copy-start(bf16[8,2,2,4,16384]{4,3,2,1,0:T(4,128)(2,1)} %param.6) | copy-start | bytes 12582916
  1.3 17.9 %collective-permute-start.3 = (bf16[2,2,3,128,128]{4,3,2,1,0:T(8,128)(2,1)S(1)}, bf16[2,2,3,128,128]{4,3,2,1,0:T(8,128)(2,1)S(1)}, u32[]{:S(2)}, u32[]{:S(2)}) collective-permute-start(bf16[2,2,3,128,128]{4,3,2,1,0:T(8,128)(2,1)S(1)} %pack_first.1.refs_1_), channel_id=1, source_target_pairs={{0,4},{4,8},{8,12},{12,16},{16,20},{20,24},{24,28},{28,32},{32,36}... | collective-permute-start | bytes 1179656 | tf_op jit(solution)/shard_map/ppermute | solution.py:274
  5.9 13.4 %copy-start.1 = (f32[4,16384]{1,0:T(4,128)S(1)}, f32[4,16384]{1,0:T(4,128)}, u32[]{:S(2)}) copy-start(f32[4,16384]{1,0:T(4,128)} %param.7) | copy-start | bytes 786436
  5.9 13.4 %copy-start.2 = (bf16[256,256]{1,0:T(8,128)(2,1)S(1)}, bf16[256,256]{1,0:T(8,128)(2,1)}, u32[]{:S(2)}) copy-start(bf16[256,256]{1,0:T(8,128)(2,1)} %constant.8.clone.refs_4_) | copy-start | bytes 393220
  5.9 13.3 %copy-start.3 = (bf16[256,256]{1,0:T(8,128)(2,1)S(1)}, bf16[256,256]{1,0:T(8,128)(2,1)}, u32[]{:S(2)}) copy-start(bf16[256,256]{1,0:T(8,128)(2,1)} %constant.9.clone.refs_3_) | copy-start | bytes 393220
  5.9 13.3 %copy-start.4 = (f32[128,128]{1,0:T(8,128)S(1)}, f32[128,128]{1,0:T(8,128)}, u32[]{:S(2)}) copy-start(f32[128,128]{1,0:T(8,128)} %constant.10.clone.refs_5_) | copy-start | bytes 196612
  5.9 13.3 %copy-start.5 = (f32[128,128]{1,0:T(8,128)S(1)}, f32[128,128]{1,0:T(8,128)}, u32[]{:S(2)}) copy-start(f32[128,128]{1,0:T(8,128)} %constant.11.clone.refs_6_) | copy-start | bytes 196612
  6.0 21.7 %collective-permute-start.2 = (bf16[2,2,3,128,128]{4,3,2,1,0:T(8,128)(2,1)S(1)}, bf16[2,2,3,128,128]{4,3,2,1,0:T(8,128)(2,1)S(1)}, u32[]{:S(2)}, u32[]{:S(2)}) collective-permute-start(bf16[2,2,3,128,128]{4,3,2,1,0:T(8,128)(2,1)S(1)} %pack.10), channel_id=1, source_target_pairs={{0,4},{4,8},{8,12},{12,16},{16,20},{20,24},{24,28},{28,32},{32,36}... | collective-permute-start | bytes 1179656 | tf_op jit(solution)/shard_map/ppermute | solution.py:281
  10.5 25.6 %collective-permute-start.1 = (bf16[2,2,3,128,128]{4,3,2,1,0:T(8,128)(2,1)S(1)}, bf16[2,2,3,128,128]{4,3,2,1,0:T(8,128)(2,1)S(1)}, u32[]{:S(2)}, u32[]{:S(2)}) collective-permute-start(bf16[2,2,3,128,128]{4,3,2,1,0:T(8,128)(2,1)S(1)} %pack.9), channel_id=1, source_target_pairs={{0,4},{4,8},{8,12},{12,16},{16,20},{20,24},{24,28},{28,32},{32,36}... | collective-permute-start | bytes 1179656 | tf_op jit(solution)/shard_map/ppermute | solution.py:281
  14.9 29.6 %collective-permute-start = (bf16[2,2,3,128,128]{4,3,2,1,0:T(8,128)(2,1)S(1)}, bf16[2,2,3,128,128]{4,3,2,1,0:T(8,128)(2,1)S(1)}, u32[]{:S(2)}, u32[]{:S(2)}) collective-permute-start(bf16[2,2,3,128,128]{4,3,2,1,0:T(8,128)(2,1)S(1)} %pack.8), channel_id=1, source_target_pairs={{0,4},{4,8},{8,12},{12,16},{16,20},{20,24},{24,28},{28,32},{32,36}... | collective-permute-start | bytes 1179656 | tf_op jit(solution)/shard_map/ppermute | solution.py:281
  20.5 32.5 %collective-permute-start.8 = (bf16[2,2,3,128,128]{4,3,2,1,0:T(8,128)(2,1)S(1)}, bf16[2,2,3,128,128]{4,3,2,1,0:T(8,128)(2,1)S(1)}, u32[]{:S(2)}, u32[]{:S(2)}) collective-permute-start(bf16[2,2,3,128,128]{4,3,2,1,0:T(8,128)(2,1)S(1)} %pack.15), channel_id=1, source_target_pairs={{0,4},{4,8},{8,12},{12,16},{16,20},{20,24},{24,28},{28,32},{32,36}... | collective-permute-start | bytes 1179656 | tf_op jit(solution)/shard_map/ppermute | solution.py:281
  28.9 34.8 %collective-permute-start.7 = (bf16[2,2,3,128,128]{4,3,2,1,0:T(8,128)(2,1)S(1)}, bf16[2,2,3,128,128]{4,3,2,1,0:T(8,128)(2,1)S(1)}, u32[]{:S(2)}, u32[]{:S(2)}) collective-permute-start(bf16[2,2,3,128,128]{4,3,2,1,0:T(8,128)(2,1)S(1)} %pack.14), channel_id=1, source_target_pairs={{0,4},{4,8},{8,12},{12,16},{16,20},{20,24},{24,28},{28,32},{32,36}... | collective-permute-start | bytes 1179656 | tf_op jit(solution)/shard_map/ppermute | solution.py:281
  37.3 32.9 %collective-permute-start.6 = (bf16[2,2,3,128,128]{4,3,2,1,0:T(8,128)(2,1)S(1)}, bf16[2,2,3,128,128]{4,3,2,1,0:T(8,128)(2,1)S(1)}, u32[]{:S(2)}, u32[]{:S(2)}) collective-permute-start(bf16[2,2,3,128,128]{4,3,2,1,0:T(8,128)(2,1)S(1)} %pack.13), channel_id=1, source_target_pairs={{0,4},{4,8},{8,12},{12,16},{16,20},{20,24},{24,28},{28,32},{32,36}... | collective-permute-start | bytes 1179656 | tf_op jit(solution)/shard_map/ppermute | solution.py:281
  54.1 12.4 %collective-permute-start.10 = (bf16[544,128]{1,0:T(8,128)(2,1)S(1)}, bf16[544,128]{1,0:T(8,128)(2,1)S(1)}, u32[]{:S(2)}, u32[]{:S(2)}) collective-permute-start(bf16[544,128]{1,0:T(8,128)(2,1)S(1)} %ship.1), channel_id=1, source_target_pairs={{252,236},{253,237},{254,238},{255,239}} | collective-permute-start | bytes 417800 | tf_op jit(solution)/shard_map/ppermute | solution.py:310
  54.7 14.5 %collective-permute-start.9 = (bf16[544,128]{1,0:T(8,128)(2,1)S(1)}, bf16[544,128]{1,0:T(8,128)(2,1)S(1)}, u32[]{:S(2)}, u32[]{:S(2)}) collective-permute-start(bf16[544,128]{1,0:T(8,128)(2,1)S(1)} %ship.1), channel_id=1, source_target_pairs={{0,320},{4,324},{8,328},{12,332},{16,336},{20,340},{24,344},{28,34... | collective-permute-start | bytes 417800 | tf_op jit(solution)/shard_map/ppermute | solution.py:309
  61.8 12.4 %collective-permute-start.5 = (bf16[1,2,3,128,128]{4,3,2,1,0:T(8,128)(2,1)S(1)}, bf16[1,2,3,128,128]{4,3,2,1,0:T(8,128)(2,1)S(1)}, u32[]{:S(2)}, u32[]{:S(2)}) collective-permute-start(bf16[1,2,3,128,128]{4,3,2,1,0:T(8,128)(2,1)S(1)} %pack.12), channel_id=1, source_target_pairs={{0,4},{4,8},{8,12},{12,16},{16,20},{20,24},{24,28},{28,32},{32,36}... | collective-permute-start | bytes 589832 | tf_op jit(solution)/shard_map/ppermute | solution.py:281
  63.7 13.7 %collective-permute-start.4 = (bf16[1,2,3,128,128]{4,3,2,1,0:T(8,128)(2,1)S(1)}, bf16[1,2,3,128,128]{4,3,2,1,0:T(8,128)(2,1)S(1)}, u32[]{:S(2)}, u32[]{:S(2)}) collective-permute-start(bf16[1,2,3,128,128]{4,3,2,1,0:T(8,128)(2,1)S(1)} %pack.11.refs_5_), channel_id=1, source_target_pairs={{0,4},{4,8},{8,12},{12,16},{16,20},{20,24},{24,28},{28,32},{32,36}... | collective-permute-start | bytes 589832 | tf_op jit(solution)/shard_map/ppermute | solution.py:281
  66.5 11.0 %collective-permute-start.11 = (bf16[544,128]{1,0:T(8,128)(2,1)S(1)}, bf16[544,128]{1,0:T(8,128)(2,1)S(1)}, u32[]{:S(2)}, u32[]{:S(2)}) collective-permute-start(bf16[544,128]{1,0:T(8,128)(2,1)S(1)} %collective-permute-done.10.refs_9_), channel_id=1, source_target_pairs={{236,316},{237,317},{238,318},{239,319}} | collective-permute-start | bytes 417800 | tf_op jit(solution)/shard_map/ppermute | solution.py:311

commit v5 on v4

--- a/solution.py
+++ b/solution.py
@@ -68,54 +68,103 @@
             spread(v_ref[channel, p, r], rows.at[r], out_ref, i, r)
 
 
-def chunk_power(place, pols, ins, scratch):
-    v_ref, h_ref, taps_ref, fourier_ref, back_ref, cos_ref, sin_ref = ins
-    rows, wide, tall = scratch
-    channel = channel_at(place, lax.axis_index("half"))
+def filtered(ins, channel, p, halo, times, rows, put):
+    v_ref, taps_ref = ins[:2]
     frames = v_ref.shape[3] // SIDE
     count = taps_ref.shape[0] // SIDE
     lane = lax.broadcasted_iota(jnp.int32, (BLOCK, SIDE), 1)
     sign = 1.0 - 2.0 * (lane % 2).astype(jnp.float32)
+    for r in range(2):
+        rows[r] = v_ref[channel, p, r].astype(jnp.float32)
+    for n in range(0, SIDE, BLOCK):
+        shaped = [taps_ref[pl.ds(count * n + k, BLOCK, stride=count), :] * sign for k in range(count)]
+        for r in range(2):
+            frame = {t: rows[r, pl.ds(frames * n + t, BLOCK, stride=frames), :] for t in range(max(times) + 1)}
+            if halo is not None:
+                for t in range(1 - count, 0):
+                    frame[t] = halo[r, t + count - 1, pl.ds(n, BLOCK), :].astype(jnp.float32)
+            for t in times:
+                value = shaped[0] * frame[t]
+                for k in range(1, count):
+                    if t - k in frame:
+                        value = value + shaped[k] * frame[t - k]
+                put(r, n, t, value)
+
+
+def into(wide, order):
+    def put(r, n, t, value):
+        wide[pl.ds(r * SIDE + n, BLOCK), pl.ds(order.index(t) * SIDE, SIDE)] = value.astype(jnp.bfloat16)
+
+    return put
+
+
+def power_of(ins, wide, tall, many):
+    fourier_ref, back_ref, cos_ref, sin_ref = ins[2:]
+    span = many * SIDE
+    first = jnp.dot(fourier_ref[...], wide[:, pl.ds(0, span)], preferred_element_type=jnp.float32)
+    cos, sin = cos_ref[...], sin_ref[...]
+    for i in range(many):
+        re = first[:SIDE, i * SIDE : (i + 1) * SIDE]
+        im = first[SIDE:, i * SIDE : (i + 1) * SIDE]
+        tall[pl.ds(i * SIDE, SIDE), pl.ds(0, SIDE)] = (re * cos - im * sin).astype(jnp.bfloat16)
+        tall[pl.ds(i * SIDE, SIDE), pl.ds(SIDE, SIDE)] = (re * sin + im * cos).astype(jnp.bfloat16)
+    spectrum = jnp.dot(tall[pl.ds(0, span), :], back_ref[...], preferred_element_type=jnp.float32)
+    square = spectrum * spectrum
     total = None
-    for i, p in enumerate(pols):
+    for i in range(many):
+        part = square[i * SIDE : (i + 1) * SIDE]
+        part = part[:, :SIDE] + part[:, SIDE:]
+        total = part if total is None else total + part
+    return total
+
+
+def chunk_kernel(place, *refs):
+    ins, near, out_ref, (rows, wide, tall) = refs[:6], refs[6], refs[7], refs[8:]
+    channel = channel_at(place, lax.axis_index("half"))
+    times = list(range(ins[0].shape[3] // SIDE))
+    total = None
+    for p in range(2):
+        filtered(ins, channel, p, near.at[p], times, rows, into(wide, times))
+        power = power_of(ins, wide, tall, len(times))
+        total = power if total is None else total + power
+    out_ref[...] = total.T
+
+
+def early_kernel(place, *refs):
+    ins, near, out_ref, sums_ref, (rows, wide, tall) = refs[:6], refs[6], refs[7], refs[8], refs[9:]
+    channel = channel_at(place, lax.axis_index("half"))
+    frames = ins[0].shape[3] // SIDE
+    times = list(range(frames))
+    filtered(ins, channel, 0, near.at[0], times, rows, into(wide, times))
+    total = power_of(ins, wide, tall, frames)
+    whole = into(wide, [frames - 1])
+
+    def put(r, n, t, value):
+        if t == frames - 1:
+            whole(r, n, t, value)
+        else:
+            sums_ref[r, t, pl.ds(n, BLOCK), :] = value
+
+    filtered(ins, channel, 1, None, times, rows, put)
+    out_ref[...] = total + power_of(ins, wide, tall, 1)
+
+
+def late_power(ins, late, sums_ref, wide, tall):
+    taps_ref = ins[1]
+    count = taps_ref.shape[0] // SIDE
+    lane = lax.broadcasted_iota(jnp.int32, (BLOCK, SIDE), 1)
+    sign = 1.0 - 2.0 * (lane % 2).astype(jnp.float32)
+    put = into(wide, list(range(count - 1)))
+    for n in range(0, SIDE, BLOCK):
+        shaped = [taps_ref[pl.ds(count * n + k, BLOCK, stride=count), :] * sign for k in range(1, count)]
         for r in range(2):
-            rows[r] = v_ref[channel, p, r].astype(jnp.float32)
-        for n in range(0, SIDE, BLOCK):
-            shaped = [
-                taps_ref[pl.ds(count * n + k, BLOCK, stride=count), :] * sign for k in range(count)
-            ]
-            for r in range(2):
-                frame = [h_ref[i, r, t, pl.ds(n, BLOCK), :].astype(jnp.float32) for t in range(count - 1)]
-                frame += [rows[r, pl.ds(frames * n + t, BLOCK, stride=frames), :] for t in range(frames)]
-                for t in range(frames):
-                    value = shaped[0] * frame[t + count - 1]
-                    for k in range(1, count):
-                        value = value + shaped[k] * frame[t + count - 1 - k]
-                    wide[pl.ds(r * SIDE + n, BLOCK), pl.ds(t * SIDE, SIDE)] = value.astype(jnp.bfloat16)
-        first = jnp.dot(fourier_ref[...], wide[...], preferred_element_type=jnp.float32)
-        cos, sin = cos_ref[...], sin_ref[...]
-        for t in range(frames):
-            re = first[:SIDE, t * SIDE : (t + 1) * SIDE]
-            im = first[SIDE:, t * SIDE : (t + 1) * SIDE]
-            tall[pl.ds(t * SIDE, SIDE), pl.ds(0, SIDE)] = (re * cos - im * sin).astype(jnp.bfloat16)
-            tall[pl.ds(t * SIDE, SIDE), pl.ds(SIDE, SIDE)] = (re * sin + im * cos).astype(jnp.bfloat16)
-        spectrum = jnp.dot(tall[...], back_ref[...], preferred_element_type=jnp.float32)
-        square = spectrum * spectrum
-        for t in range(frames):
-            part = square[t * SIDE : (t + 1) * SIDE]
-            part = part[:, :SIDE] + part[:, SIDE:]
-            total = part if total is None else total + part
-    return total
-
-
-def chunk_kernel(place, *refs):
-    ins, out_ref, scratch = refs[:7], refs[7], refs[8:]
-    out_ref[...] = chunk_power(place, (0, 1), ins, scratch).T
-
-
-def first_half_kernel(place, *refs):
-    ins, out_ref, scratch = refs[:7], refs[7], refs[8:]
-    out_ref[...] = chunk_power(place, (0,), ins, scratch)
+            frame = [late[0, r, t, pl.ds(n, BLOCK), :].astype(jnp.float32) for t in range(count - 1)]
+            for t in range(count - 1):
+                value = sums_ref[r, t, pl.ds(n, BLOCK), :]
+                for k in range(t + 1, count):
+                    value = value + shaped[k - 1] * frame[t - k + count - 1]
+                put(r, n, t, value)
+    return power_of(ins, wide, tall, count - 1)
 
 
 def lay_out(every, apart, peers, step, start):
@@ -144,13 +193,11 @@
     out_ref[pl.ds(16 + 4 * SIDE, 16), :] = jnp.concatenate([after, zero], axis=0).astype(jnp.bfloat16)
 
 
-def last_kernel(place, *refs):
-    ins, (part, p0, p3, border, p5, p6, theirs, relayed), out_ref = refs[:7], refs[7:15], refs[15]
-    scratch, (every, apart, plain) = refs[16:19], refs[19:]
+def lay_kernel(p0, p3, border, p5, p6, theirs, relayed, out_ref, every, plain):
     half = lax.axis_index("half")
-    peers = apart.shape[0] // (2 * SENT)
+    peers = out_ref.shape[0] // (2 * SENT)
     plain[...] = theirs[...].astype(jnp.float32) + relayed[...].astype(jnp.float32)
-    lay_out(plain.at[pl.ds(8, plain.shape[0] - 16)], apart, peers, 2 * SENT, SENT)
+    lay_out(plain.at[pl.ds(8, plain.shape[0] - 16)], out_ref, peers, 2 * SENT, SENT)
 
     def put(slot, value):
         every[pl.ds(pl.multiple_of(8 + slot * SIDE, 8), SIDE), :] = value
@@ -158,15 +205,38 @@
     put(3 * (1 - half), border[...])
     put(half, p5[...])
     put(1 + half, p6[...])
+    put(2 + half, jnp.zeros((SIDE, SIDE), jnp.float32))
     zero = jnp.zeros((8, SIDE), jnp.float32)
     ends(
         every,
         jnp.where(half == 1, p3[pl.ds(SIDE - 8, 8), :], zero),
         jnp.where(half == 0, p0[pl.ds(0, 8), :], zero),
     )
-    put(2 + half, (part[...] + chunk_power(place, (1,), ins, scratch)).T)
-    lay_out(every, apart, peers, 2 * SENT, 0)
-    out_ref[...] = apart[...].astype(jnp.bfloat16)
+    lay_out(every, out_ref, peers, 2 * SENT, 0)
+
+
+def last_kernel(*refs):
+    ins, (late, part, sums_ref, border, p6, laid), out_ref, same_ref = refs[:6], refs[6:12], refs[12], refs[13]
+    wide, tall, every = refs[14:]
+    half = lax.axis_index("half")
+    value = (part[...] + late_power(ins, late, sums_ref, wide, tall)).T
+    every[pl.ds(8, SIDE), :] = value
+    zero = jnp.zeros((8, SIDE), jnp.float32)
+    ends(every, p6[pl.ds(SIDE - 8, 8), :], jnp.where(half == 0, border[pl.ds(0, 8), :], zero))
+    group = SIDE // 8
+    stride = 2 * SENT
+    start = group * stride * (2 + half)
+    lay_out(every, same_ref, group, stride, start)
+    lane = lax.broadcasted_iota(jnp.int32, (1, SIDE), 1)
+    row = pl.ds(start - stride + 8, 1)
+    same_ref[row, :] = jnp.where(lane < SIDE // 2, value[:1], same_ref[row, :])
+
+    @pl.when(half == 0)
+    def _():
+        row = pl.ds(3 * group * stride + 8, 1)
+        same_ref[row, :] = jnp.where(lane < SIDE // 2, same_ref[row, :], value[SIDE - 1 :])
+
+    out_ref[...] = same_ref[...].astype(jnp.bfloat16)
 
 
 def tree_kernel(scale, in_ref, out_ref, wide, steps, flat):
@@ -217,16 +287,19 @@
             out_ref[which, :, pl.ds(r * SIDE, SIDE)] = flat[pl.ds(r, NT, stride=8), :] * scale
 
 
-def call(body, name, args, shape, dtype, scratch, flops=1 << 20, after=(), specs=None, params=PARAMS):
+def call(body, name, args, shape, dtype, scratch, flops=1 << 20, after=(), specs=None, params=PARAMS, alias=None):
+    several = isinstance(shape, list)
+
     def ordered(*refs):
         body(*refs[: len(args)], *refs[len(args) + len(after) :])
 
     return pl.pallas_call(
         ordered,
         in_specs=(specs or [VMEM] * len(args)) + [ANY] * len(after),
-        out_specs=VMEM,
-        out_shape=jax.ShapeDtypeStruct(shape, dtype),
+        out_specs=[VMEM] * len(shape) if several else VMEM,
+        out_shape=[jax.ShapeDtypeStruct(*each) for each in shape] if several else jax.ShapeDtypeStruct(shape, dtype),
         scratch_shapes=scratch,
+        input_output_aliases=alias or {},
         compiler_params=params,
         cost_estimate=pl.CostEstimate(flops=flops, bytes_accessed=1 << 20, transcendentals=0),
         name=name,
@@ -271,14 +344,14 @@
         params=FIRST,
     )
     packs = [first]
-    near = [lax.ppermute(first, ("half", "tm"), pairs)]
+    near = [[lax.ppermute(first, ("half", "tm"), pairs)]] + [[] for _ in range(channels - 1)]
 
     def send(place, pols, after):
         shape = (len(pols),) + halo[1:]
         body = bind(pack_kernel, place, pols)
         value = call(body, "pack", [rows], shape, bf16, [pltpu.VMEM((2,) + interleaved, f32)], after=after)
         packs.append(value)
-        near.append(lax.ppermute(value, ("half", "tm"), pairs))
+        near[place].append(lax.ppermute(value, ("half", "tm"), pairs))
 
     constants = [coefficients, fourier, back, cos, sin]
     scratch = [
@@ -301,9 +374,10 @@
     power = []
     last = channels - 1
     for place in range(last):
-        args = [rows, near[place], *constants]
+        args = [rows, *constants, *near[place]]
         order = power[-1:] + ([theirs, by] if place == last - 2 else [])
-        power.append(call(bind(chunk_kernel, place), "chunk", args, tile, f32, scratch, flops, after=order))
+        body = bind(chunk_kernel, place)
+        power.append(call(body, "chunk", args, tile, f32, scratch, flops, after=order))
         if place == channels // 2:
             ship = call(ship_kernel, "ship", power[:5], shipped, bf16, [], after=[packs[-1]])
             theirs = lax.ppermute(ship, ("half", "tm"), straight)
@@ -314,18 +388,36 @@
         elif place + AHEAD == last:
             send(last, (0,), power[-1:])
             send(last, (1,), power[-1:])
-    args = [rows, near[last], *constants]
-    part = call(bind(first_half_kernel, last), "chunk_half", args, tile, f32, scratch, flops // 2, after=power[-1:])
-    every = pltpu.VMEM((8 + 4 * SIDE + 8, SIDE), f32)
+    sums = (2, count - 1) + tile
+    part, begun = call(
+        bind(early_kernel, last),
+        "chunk_early",
+        [rows, *constants, near[last][0]],
+        [(tile, f32), (sums, f32)],
+        None,
+        scratch,
+        flops,
+        after=power[-1:],
+    )
     sent = (2 * peers * SENT, SIDE)
-    out = call(
-        bind(last_kernel, last),
+    laid = call(
+        lay_kernel,
+        "lay",
+        [power[0], power[3], *power[4:7], theirs, relayed],
+        sent,
+        f32,
+        [pltpu.VMEM((8 + 4 * SIDE + 8, SIDE), f32), pltpu.VMEM(shipped, f32)],
+        after=[part],
+    )
+    out, _ = call(
+        last_kernel,
         "last",
-        [rows, near[last + 1], *constants, part, power[0], power[3], power[4], power[5], power[6], theirs, relayed],
-        sent,
-        bf16,
-        scratch + [every, pltpu.VMEM(sent, f32), pltpu.VMEM(shipped, f32)],
+        [rows, *constants, near[last][1], part, begun, power[4], power[6], laid],
+        [(sent, bf16), (sent, f32)],
+        None,
+        scratch[1:] + [pltpu.VMEM((8 + SIDE + 8, SIDE), f32)],
         flops // 2,
+        alias={11: 1},
     )
     out = out.reshape(peers, SENT, 2, SIDE)
     owned = lax.all_to_all(out, "tm", split_axis=0, concat_axis=0, tiled=True).reshape(sent)

time: 101 us -> 100 us (0.990)
    pallas_call x20 -> x21, Pallas kernels: 12.5 us -> 12.7 us  [call(): pl.pallas_call(ordered, in_specs=(specs or [VMEM] * len(args)) + [ANY] *...]
where the time goes in v5:
time: 100 us
  starting transfers between devices  33.7 us (34%)
  waiting for transfers between devices  32.6 us (33%)
  blocking collectives  20.7 us (21%)
  Pallas kernels  12.7 us (13%)
    ppermute x8, waiting for transfers between devices, send(): near[place].append(lax.ppermute(value, ('half', 'tm'), pairs))  28.2 us
    ppermute x8, starting transfers between devices, send(): near[place].append(lax.ppermute(value, ('half', 'tm'), pairs))  21 us
    all_to_all x1, blocking collectives, per_device(): lax.all_to_all(out, 'tm', split_axis=0, concat_axis=0, tiled=True)  20.7 us
    pallas_call x21, Pallas kernels, call(): pl.pallas_call(ordered, in_specs=(specs or [VMEM] * len(args)) + [ANY] *...  12.7 us
    ppermute x1, starting transfers between devices, per_device(): theirs = lax.ppermute(ship, ('half', 'tm'), straight)  6.95 us
    ppermute x1, starting transfers between devices, per_device(): lax.ppermute(first, ('half', 'tm'), pairs)  4.41 us
    ppermute x1, waiting for transfers between devices, per_device(): lax.ppermute(first, ('half', 'tm'), pairs)  2.39 us
    ppermute x1, waiting for transfers between devices, per_device(): theirs = lax.ppermute(ship, ('half', 'tm'), straight)  2.05 us
  transfers between devices with their start and end apart: 12, of which 8 were waited for; matrix products, arithmetic and copies ran while one was open for 0% of the time, Pallas kernels for 9%

profile of v5, /device:TPU:2, one launch (start us, length us, event | category | flops | bytes accessed | tf_op | source)
XLA Modules:
  0.0 100.0 jit_solution(13996575002598218718)
XLA Ops:
  0.0 1.3 %pack_first.1.refs_1_ = bf16[2,2,3,128,128]{4,3,2,1,0:T(8,128)(2,1)S(1)} custom-call(bf16[8,2,2,512,128]{4,3,2,1,0:T(8,128)(2,1)} %bitcast.12), custom_call_target="tpu_custom_call" | custom-call | flops 1048576 | bytes 1048576 | tf_op jit(solution)/shard_map/pack_first/pallas_call | solution.py:296
  1.3 4.4 %collective-permute-start.3 = (bf16[2,2,3,128,128]{4,3,2,1,0:T(8,128)(2,1)S(1)}, bf16[2,2,3,128,128]{4,3,2,1,0:T(8,128)(2,1)S(1)}, u32[]{:S(2)}, u32[]{:S(2)}) collective-permute-start(bf16[2,2,3,128,128]{4,3,2,1,0:T(8,128)(2,1)S(1)} %pack_first.1.refs_1_), channel_id=1, source_target_pairs={{0,4},{4,8},{8,12},{12,16},{16,20},{20,24},{24,28},{28,32},{32,36}... | collective-permute-start | bytes 1179656 | tf_op jit(solution)/shard_map/ppermute | solution.py:347
  5.7 0.1 pack.10
  5.9 0.0 copy-start.1
  5.9 0.0 copy-start.2
  5.9 0.0 copy-start.3
  5.9 0.0 copy-start.4
  5.9 0.0 copy-start.5
  6.0 4.4 %collective-permute-start.2 = (bf16[2,2,3,128,128]{4,3,2,1,0:T(8,128)(2,1)S(1)}, bf16[2,2,3,128,128]{4,3,2,1,0:T(8,128)(2,1)S(1)}, u32[]{:S(2)}, u32[]{:S(2)}) collective-permute-start(bf16[2,2,3,128,128]{4,3,2,1,0:T(8,128)(2,1)S(1)} %pack.10), channel_id=1, source_target_pairs={{0,4},{4,8},{8,12},{12,16},{16,20},{20,24},{24,28},{28,32},{32,36}... | collective-permute-start | bytes 1179656 | tf_op jit(solution)/shard_map/ppermute | solution.py:354
  10.4 0.1 pack.9
  10.5 4.3 %collective-permute-start.1 = (bf16[2,2,3,128,128]{4,3,2,1,0:T(8,128)(2,1)S(1)}, bf16[2,2,3,128,128]{4,3,2,1,0:T(8,128)(2,1)S(1)}, u32[]{:S(2)}, u32[]{:S(2)}) collective-permute-start(bf16[2,2,3,128,128]{4,3,2,1,0:T(8,128)(2,1)S(1)} %pack.9), channel_id=1, source_target_pairs={{0,4},{4,8},{8,12},{12,16},{16,20},{20,24},{24,28},{28,32},{32,36}... | collective-permute-start | bytes 1179656 | tf_op jit(solution)/shard_map/ppermute | solution.py:354
  14.8 0.1 pack.8
  14.9 1.9 %collective-permute-start = (bf16[2,2,3,128,128]{4,3,2,1,0:T(8,128)(2,1)S(1)}, bf16[2,2,3,128,128]{4,3,2,1,0:T(8,128)(2,1)S(1)}, u32[]{:S(2)}, u32[]{:S(2)}) collective-permute-start(bf16[2,2,3,128,128]{4,3,2,1,0:T(8,128)(2,1)S(1)} %pack.8), channel_id=1, source_target_pairs={{0,4},{4,8},{8,12},{12,16},{16,20},{20,24},{24,28},{28,32},{32,36}... | collective-permute-start | bytes 1179656 | tf_op jit(solution)/shard_map/ppermute | solution.py:354
  16.9 2.4 %collective-permute-done.3.refs_6_ = bf16[2,2,3,128,128]{4,3,2,1,0:T(8,128)(2,1)S(1)} collective-permute-done((bf16[2,2,3,128,128]{4,3,2,1,0:T(8,128)(2,1)S(1)}, bf16[2,2,3,128,128]{4,3,2,1,0:T(8,128)(2,1)S(1)}, u32[]{:S(2)}, u32[]{:S(2)}) %collective-permute-start.3) | collective-permute-done | bytes 393248 | tf_op jit(solution)/shard_map/ppermute | solution.py:347
  19.3 1.1 %chunk.7.refs_7_.refs_1_.refs_0_ = f32[128,128]{1,0:T(8,128)S(1)} custom-call(bf16[8,2,2,512,128]{4,3,2,1,0:T(8,128)(2,1)S(1)} %bitcast.16, f32[512,128]{1,0:T(8,128)S(1)} %bitcast.30, bf16[256,256]{1,0:T(8,128)(2,1)S(1)} %copy-done.3, bf16[256,256]{1,0:T(8,128)(2,1)S(1)} %copy-done.2, f32[128,128]{1,0:T(8,128)S(1)} %copy-done.4, f32[128,128]{1,0:T(8,128)S(1)} %copy-done.5, ...), custom_call_target="tpu_custom_call" | custom-call | flops 314572800 | bytes 1048576 | tf_op jit(solution)/shard_map/chunk/pallas_call | solution.py:296
  20.3 0.1 pack.15
  20.5 1.9 %collective-permute-start.8 = (bf16[2,2,3,128,128]{4,3,2,1,0:T(8,128)(2,1)S(1)}, bf16[2,2,3,128,128]{4,3,2,1,0:T(8,128)(2,1)S(1)}, u32[]{:S(2)}, u32[]{:S(2)}) collective-permute-start(bf16[2,2,3,128,128]{4,3,2,1,0:T(8,128)(2,1)S(1)} %pack.15), channel_id=1, source_target_pairs={{0,4},{4,8},{8,12},{12,16},{16,20},{20,24},{24,28},{28,32},{32,36}... | collective-permute-start | bytes 1179656 | tf_op jit(solution)/shard_map/ppermute | solution.py:354
  22.4 5.3 %collective-permute-done.2.refs_6_ = bf16[2,2,3,128,128]{4,3,2,1,0:T(8,128)(2,1)S(1)} collective-permute-done((bf16[2,2,3,128,128]{4,3,2,1,0:T(8,128)(2,1)S(1)}, bf16[2,2,3,128,128]{4,3,2,1,0:T(8,128)(2,1)S(1)}, u32[]{:S(2)}, u32[]{:S(2)}) %collective-permute-start.2) | collective-permute-done | bytes 393248 | tf_op jit(solution)/shard_map/ppermute | solution.py:354
  27.7 1.1 %chunk.8.refs_7_.refs_1_ = f32[128,128]{1,0:T(8,128)S(1)} custom-call(bf16[8,2,2,512,128]{4,3,2,1,0:T(8,128)(2,1)S(1)} %bitcast.18, f32[512,128]{1,0:T(8,128)S(1)} %bitcast.31, bf16[256,256]{1,0:T(8,128)(2,1)S(1)} %copy-done.3, bf16[256,256]{1,0:T(8,128)(2,1)S(1)} %copy-done.2, f32[128,128]{1,0:T(8,128)S(1)} %copy-done.4, f32[128,128]{1,0:T(8,128)S(1)} %copy-done.5, ...), custom_call_target="tpu_custom_call" | custom-call | flops 314572800 | bytes 1048576 | tf_op jit(solution)/shard_map/chunk/pallas_call | solution.py:296
  28.7 0.1 pack.14
  28.9 1.9 %collective-permute-start.7 = (bf16[2,2,3,128,128]{4,3,2,1,0:T(8,128)(2,1)S(1)}, bf16[2,2,3,128,128]{4,3,2,1,0:T(8,128)(2,1)S(1)}, u32[]{:S(2)}, u32[]{:S(2)}) collective-permute-start(bf16[2,2,3,128,128]{4,3,2,1,0:T(8,128)(2,1)S(1)} %pack.14), channel_id=1, source_target_pairs={{0,4},{4,8},{8,12},{12,16},{16,20},{20,24},{24,28},{28,32},{32,36}... | collective-permute-start | bytes 1179656 | tf_op jit(solution)/shard_map/ppermute | solution.py:354
  30.8 5.3 %collective-permute-done.1.refs_6_ = bf16[2,2,3,128,128]{4,3,2,1,0:T(8,128)(2,1)S(1)} collective-permute-done((bf16[2,2,3,128,128]{4,3,2,1,0:T(8,128)(2,1)S(1)}, bf16[2,2,3,128,128]{4,3,2,1,0:T(8,128)(2,1)S(1)}, u32[]{:S(2)}, u32[]{:S(2)}) %collective-permute-start.1) | collective-permute-done | bytes 393248 | tf_op jit(solution)/shard_map/ppermute | solution.py:354
  36.1 1.0 %chunk.9.refs_7_.refs_1_.refs_2_ = f32[128,128]{1,0:T(8,128)S(1)} custom-call(bf16[8,2,2,512,128]{4,3,2,1,0:T(8,128)(2,1)S(1)} %bitcast.20, f32[512,128]{1,0:T(8,128)S(1)} %bitcast.32, bf16[256,256]{1,0:T(8,128)(2,1)S(1)} %copy-done.3, bf16[256,256]{1,0:T(8,128)(2,1)S(1)} %copy-done.2, f32[128,128]{1,0:T(8,128)S(1)} %copy-done.4, f32[128,128]{1,0:T(8,128)S(1)} %copy-done.5, ...), custom_call_target="tpu_custom_call" | custom-call | flops 314572800 | bytes 1048576 | tf_op jit(solution)/shard_map/chunk/pallas_call | solution.py:296
  37.2 0.1 pack.13
  37.3 1.9 %collective-permute-start.6 = (bf16[2,2,3,128,128]{4,3,2,1,0:T(8,128)(2,1)S(1)}, bf16[2,2,3,128,128]{4,3,2,1,0:T(8,128)(2,1)S(1)}, u32[]{:S(2)}, u32[]{:S(2)}) collective-permute-start(bf16[2,2,3,128,128]{4,3,2,1,0:T(8,128)(2,1)S(1)} %pack.13), channel_id=1, source_target_pairs={{0,4},{4,8},{8,12},{12,16},{16,20},{20,24},{24,28},{28,32},{32,36}... | collective-permute-start | bytes 1179656 | tf_op jit(solution)/shard_map/ppermute | solution.py:354
  39.2 5.3 %collective-permute-done.refs_6_ = bf16[2,2,3,128,128]{4,3,2,1,0:T(8,128)(2,1)S(1)} collective-permute-done((bf16[2,2,3,128,128]{4,3,2,1,0:T(8,128)(2,1)S(1)}, bf16[2,2,3,128,128]{4,3,2,1,0:T(8,128)(2,1)S(1)}, u32[]{:S(2)}, u32[]{:S(2)}) %collective-permute-start) | collective-permute-done | bytes 393248 | tf_op jit(solution)/shard_map/ppermute | solution.py:354
  44.5 1.1 %chunk.10.refs_1_.refs_7_.refs_3_ = f32[128,128]{1,0:T(8,128)S(1)} custom-call(bf16[8,2,2,512,128]{4,3,2,1,0:T(8,128)(2,1)S(1)} %bitcast.22, f32[512,128]{1,0:T(8,128)S(1)} %bitcast.33, bf16[256,256]{1,0:T(8,128)(2,1)S(1)} %copy-done.3, bf16[256,256]{1,0:T(8,128)(2,1)S(1)} %copy-done.2, f32[128,128]{1,0:T(8,128)S(1)} %copy-done.4, f32[128,128]{1,0:T(8,128)S(1)} %copy-done.5, ...), custom_call_target="tpu_custom_call" | custom-call | flops 314572800 | bytes 1048576 | tf_op jit(solution)/shard_map/chunk/pallas_call | solution.py:296
  45.6 0.1 pack.11.refs_5_
  45.7 7.3 %collective-permute-done.8.refs_6_ = bf16[2,2,3,128,128]{4,3,2,1,0:T(8,128)(2,1)S(1)} collective-permute-done((bf16[2,2,3,128,128]{4,3,2,1,0:T(8,128)(2,1)S(1)}, bf16[2,2,3,128,128]{4,3,2,1,0:T(8,128)(2,1)S(1)}, u32[]{:S(2)}, u32[]{:S(2)}) %collective-permute-start.8) | collective-permute-done | bytes 393248 | tf_op jit(solution)/shard_map/ppermute | solution.py:354
  53.0 1.1 %chunk.11.refs_4_.refs_7_.refs_2_.refs_9_ = f32[128,128]{1,0:T(8,128)S(1)} custom-call(bf16[8,2,2,512,128]{4,3,2,1,0:T(8,128)(2,1)S(1)} %bitcast.24, f32[512,128]{1,0:T(8,128)S(1)} %bitcast.34, bf16[256,256]{1,0:T(8,128)(2,1)S(1)} %copy-done.3, bf16[256,256]{1,0:T(8,128)(2,1)S(1)} %copy-done.2, f32[128,128]{1,0:T(8,128)S(1)} %copy-done.4, ...), custom_call_target="tpu_custom_call" | custom-call | flops 314572800 | bytes 1048576 | tf_op jit(solution)/shard_map/chunk/pallas_call | solution.py:296
  54.0 0.7 collective-permute-start.10
  54.7 6.9 %collective-permute-start.9 = (bf16[544,128]{1,0:T(8,128)(2,1)S(1)}, bf16[544,128]{1,0:T(8,128)(2,1)S(1)}, u32[]{:S(2)}, u32[]{:S(2)}) collective-permute-start(bf16[544,128]{1,0:T(8,128)(2,1)S(1)} %ship.1), channel_id=1, source_target_pairs={{0,320},{4,324},{8,328},{12,332},{16,336},{20,340},{24,344},{28,34... | collective-permute-start | bytes 417800 | tf_op jit(solution)/shard_map/ppermute | solution.py:383
  61.7 0.1 pack.12
  61.8 1.9 %collective-permute-start.5 = (bf16[1,2,3,128,128]{4,3,2,1,0:T(8,128)(2,1)S(1)}, bf16[1,2,3,128,128]{4,3,2,1,0:T(8,128)(2,1)S(1)}, u32[]{:S(2)}, u32[]{:S(2)}) collective-permute-start(bf16[1,2,3,128,128]{4,3,2,1,0:T(8,128)(2,1)S(1)} %pack.12), channel_id=1, source_target_pairs={{0,4},{4,8},{8,12},{12,16},{16,20},{20,24},{24,28},{28,32},{32,36}... | collective-permute-start | bytes 589832 | tf_op jit(solution)/shard_map/ppermute | solution.py:354
  63.7 0.0 collective-permute-done.7.refs_6_
  63.7 2.7 %collective-permute-start.4 = (bf16[1,2,3,128,128]{4,3,2,1,0:T(8,128)(2,1)S(1)}, bf16[1,2,3,128,128]{4,3,2,1,0:T(8,128)(2,1)S(1)}, u32[]{:S(2)}, u32[]{:S(2)}) collective-permute-start(bf16[1,2,3,128,128]{4,3,2,1,0:T(8,128)(2,1)S(1)} %pack.11.refs_5_), channel_id=1, source_target_pairs={{0,4},{4,8},{8,12},{12,16},{16,20},{20,24},{24,28},{28,32},{32,36}... | collective-permute-start | bytes 589832 | tf_op jit(solution)/shard_map/ppermute | solution.py:354
  66.4 0.0 collective-permute-done.10.refs_9_
  66.4 0.7 collective-permute-start.11
  67.1 2.1 %collective-permute-done.9.refs_8_.refs_5_ = bf16[544,128]{1,0:T(8,128)(2,1)S(1)} collective-permute-done((bf16[544,128]{1,0:T(8,128)(2,1)S(1)}, bf16[544,128]{1,0:T(8,128)(2,1)S(1)}, u32[]{:S(2)}, u32[]{:S(2)}) %collective-permute-start.9) | collective-permute-done | bytes 139296 | tf_op jit(solution)/shard_map/ppermute | solution.py:383
  69.2 1.0 %chunk.12.refs_7_.refs_3_ = f32[128,128]{1,0:T(8,128)S(1)} custom-call(bf16[8,2,2,512,128]{4,3,2,1,0:T(8,128)(2,1)S(1)} %bitcast.26, f32[512,128]{1,0:T(8,128)S(1)} %bitcast.35, bf16[256,256]{1,0:T(8,128)(2,1)S(1)} %copy-done.3, bf16[256,256]{1,0:T(8,128)(2,1)S(1)} %copy-done.2, f32[128,128]{1,0:T(8,128)S(1)} %copy-done.4, f32[128,128]{1,0:T(8,128)S(1)} %copy-done.5, ...), custom_call_target="tpu_custom_call" | custom-call | flops 314572800 | bytes 1048576 | tf_op jit(solution)/shard_map/chunk/pallas_call | solution.py:296
  70.2 1.1 %chunk.13.refs_7_.refs_4_.refs_10_ = f32[128,128]{1,0:T(8,128)S(1)} custom-call(bf16[8,2,2,512,128]{4,3,2,1,0:T(8,128)(2,1)S(1)} %bitcast.27, f32[512,128]{1,0:T(8,128)S(1)} %bitcast.36, bf16[256,256]{1,0:T(8,128)(2,1)S(1)} %copy-done.3, bf16[256,256]{1,0:T(8,128)(2,1)S(1)} %copy-done.2, f32[128,128]{1,0:T(8,128)S(1)} %copy-done.4, ...), custom_call_target="tpu_custom_call" | custom-call | flops 314572800 | bytes 1048576 | tf_op jit(solution)/shard_map/chunk/pallas_call | solution.py:296
  71.3 2.9 %collective-permute-done.5.refs_6_ = bf16[1,2,3,128,128]{4,3,2,1,0:T(8,128)(2,1)S(1)} collective-permute-done((bf16[1,2,3,128,128]{4,3,2,1,0:T(8,128)(2,1)S(1)}, bf16[1,2,3,128,128]{4,3,2,1,0:T(8,128)(2,1)S(1)}, u32[]{:S(2)}, u32[]{:S(2)}) %collective-permute-start.5) | collective-permute-done | bytes 196640 | tf_op jit(solution)/shard_map/ppermute | solution.py:354
  74.2 0.9 chunk_early.1
  75.1 0.2 lay.1.refs_11_
  75.3 2.1 %collective-permute-done.4.refs_6_ = bf16[1,2,3,128,128]{4,3,2,1,0:T(8,128)(2,1)S(1)} collective-permute-done((bf16[1,2,3,128,128]{4,3,2,1,0:T(8,128)(2,1)S(1)}, bf16[1,2,3,128,128]{4,3,2,1,0:T(8,128)(2,1)S(1)}, u32[]{:S(2)}, u32[]{:S(2)}) %collective-permute-start.4) | collective-permute-done | bytes 196640 | tf_op jit(solution)/shard_map/ppermute | solution.py:354
  77.4 0.6 last.1
  78.0 20.7 %all_to_all.5 = bf16[64,9,2,128]{3,2,1,0:T(2,128)(2,1)S(1)} all-to-all(bf16[64,9,2,128]{3,2,1,0:T(2,128)(2,1)S(1)} %bitcast.40), channel_id=1, replica_groups=mesh['half'=2,'tm'=64,'chan'=4] {'tm'}, dimensions={0} | all-to-all | bytes 589824 | tf_op jit(solution)/shard_map/all_to_all | solution.py:423
  98.7 1.3 %tree.1 = f32[2,16,1024]{2,1,0:T(8,128)} custom-call(bf16[1152,128]{1,0:T(8,128)(2,1)S(1)} %bitcast.39), custom_call_target="tpu_custom_call" | custom-call | flops 1048576 | bytes 1048576 | tf_op jit(solution)/shard_map/tree/pallas_call | solution.py:296
  (10 shorter events, 0.0 us)
Async XLA Ops:
  0.0 5.7 %copy-start = (bf16[8,2,2,4,16384]{4,3,2,1,0:T(4,128)(2,1)S(1)}, bf16[8,2,2,4,16384]{4,3,2,1,0:T(4,128)(2,1)}, u32[]{:S(2)}) copy-start(bf16[8,2,2,4,16384]{4,3,2,1,0:T(4,128)(2,1)} %param.6) | copy-start | bytes 12582916
  1.3 17.9 %collective-permute-start.3 = (bf16[2,2,3,128,128]{4,3,2,1,0:T(8,128)(2,1)S(1)}, bf16[2,2,3,128,128]{4,3,2,1,0:T(8,128)(2,1)S(1)}, u32[]{:S(2)}, u32[]{:S(2)}) collective-permute-start(bf16[2,2,3,128,128]{4,3,2,1,0:T(8,128)(2,1)S(1)} %pack_first.1.refs_1_), channel_id=1, source_target_pairs={{0,4},{4,8},{8,12},{12,16},{16,20},{20,24},{24,28},{28,32},{32,36}... | collective-permute-start | bytes 1179656 | tf_op jit(solution)/shard_map/ppermute | solution.py:347
  5.9 13.4 %copy-start.1 = (f32[4,16384]{1,0:T(4,128)S(1)}, f32[4,16384]{1,0:T(4,128)}, u32[]{:S(2)}) copy-start(f32[4,16384]{1,0:T(4,128)} %param.7) | copy-start | bytes 786436
  5.9 13.4 %copy-start.2 = (bf16[256,256]{1,0:T(8,128)(2,1)S(1)}, bf16[256,256]{1,0:T(8,128)(2,1)}, u32[]{:S(2)}) copy-start(bf16[256,256]{1,0:T(8,128)(2,1)} %constant.8.clone.refs_3_) | copy-start | bytes 393220
  5.9 13.3 %copy-start.3 = (bf16[256,256]{1,0:T(8,128)(2,1)S(1)}, bf16[256,256]{1,0:T(8,128)(2,1)}, u32[]{:S(2)}) copy-start(bf16[256,256]{1,0:T(8,128)(2,1)} %constant.9.clone.refs_2_) | copy-start | bytes 393220
  5.9 13.3 %copy-start.4 = (f32[128,128]{1,0:T(8,128)S(1)}, f32[128,128]{1,0:T(8,128)}, u32[]{:S(2)}) copy-start(f32[128,128]{1,0:T(8,128)} %constant.10.clone.refs_4_) | copy-start | bytes 196612
  5.9 13.3 %copy-start.5 = (f32[128,128]{1,0:T(8,128)S(1)}, f32[128,128]{1,0:T(8,128)}, u32[]{:S(2)}) copy-start(f32[128,128]{1,0:T(8,128)} %constant.11.clone.refs_5_) | copy-start | bytes 196612
  6.0 21.7 %collective-permute-start.2 = (bf16[2,2,3,128,128]{4,3,2,1,0:T(8,128)(2,1)S(1)}, bf16[2,2,3,128,128]{4,3,2,1,0:T(8,128)(2,1)S(1)}, u32[]{:S(2)}, u32[]{:S(2)}) collective-permute-start(bf16[2,2,3,128,128]{4,3,2,1,0:T(8,128)(2,1)S(1)} %pack.10), channel_id=1, source_target_pairs={{0,4},{4,8},{8,12},{12,16},{16,20},{20,24},{24,28},{28,32},{32,36}... | collective-permute-start | bytes 1179656 | tf_op jit(solution)/shard_map/ppermute | solution.py:354
  10.5 25.6 %collective-permute-start.1 = (bf16[2,2,3,128,128]{4,3,2,1,0:T(8,128)(2,1)S(1)}, bf16[2,2,3,128,128]{4,3,2,1,0:T(8,128)(2,1)S(1)}, u32[]{:S(2)}, u32[]{:S(2)}) collective-permute-start(bf16[2,2,3,128,128]{4,3,2,1,0:T(8,128)(2,1)S(1)} %pack.9), channel_id=1, source_target_pairs={{0,4},{4,8},{8,12},{12,16},{16,20},{20,24},{24,28},{28,32},{32,36}... | collective-permute-start | bytes 1179656 | tf_op jit(solution)/shard_map/ppermute | solution.py:354
  14.9 29.6 %collective-permute-start = (bf16[2,2,3,128,128]{4,3,2,1,0:T(8,128)(2,1)S(1)}, bf16[2,2,3,128,128]{4,3,2,1,0:T(8,128)(2,1)S(1)}, u32[]{:S(2)}, u32[]{:S(2)}) collective-permute-start(bf16[2,2,3,128,128]{4,3,2,1,0:T(8,128)(2,1)S(1)} %pack.8), channel_id=1, source_target_pairs={{0,4},{4,8},{8,12},{12,16},{16,20},{20,24},{24,28},{28,32},{32,36}... | collective-permute-start | bytes 1179656 | tf_op jit(solution)/shard_map/ppermute | solution.py:354
  20.5 32.5 %collective-permute-start.8 = (bf16[2,2,3,128,128]{4,3,2,1,0:T(8,128)(2,1)S(1)}, bf16[2,2,3,128,128]{4,3,2,1,0:T(8,128)(2,1)S(1)}, u32[]{:S(2)}, u32[]{:S(2)}) collective-permute-start(bf16[2,2,3,128,128]{4,3,2,1,0:T(8,128)(2,1)S(1)} %pack.15), channel_id=1, source_target_pairs={{0,4},{4,8},{8,12},{12,16},{16,20},{20,24},{24,28},{28,32},{32,36}... | collective-permute-start | bytes 1179656 | tf_op jit(solution)/shard_map/ppermute | solution.py:354
  28.9 34.8 %collective-permute-start.7 = (bf16[2,2,3,128,128]{4,3,2,1,0:T(8,128)(2,1)S(1)}, bf16[2,2,3,128,128]{4,3,2,1,0:T(8,128)(2,1)S(1)}, u32[]{:S(2)}, u32[]{:S(2)}) collective-permute-start(bf16[2,2,3,128,128]{4,3,2,1,0:T(8,128)(2,1)S(1)} %pack.14), channel_id=1, source_target_pairs={{0,4},{4,8},{8,12},{12,16},{16,20},{20,24},{24,28},{28,32},{32,36}... | collective-permute-start | bytes 1179656 | tf_op jit(solution)/shard_map/ppermute | solution.py:354
  37.3 32.9 %collective-permute-start.6 = (bf16[2,2,3,128,128]{4,3,2,1,0:T(8,128)(2,1)S(1)}, bf16[2,2,3,128,128]{4,3,2,1,0:T(8,128)(2,1)S(1)}, u32[]{:S(2)}, u32[]{:S(2)}) collective-permute-start(bf16[2,2,3,128,128]{4,3,2,1,0:T(8,128)(2,1)S(1)} %pack.13), channel_id=1, source_target_pairs={{0,4},{4,8},{8,12},{12,16},{16,20},{20,24},{24,28},{28,32},{32,36}... | collective-permute-start | bytes 1179656 | tf_op jit(solution)/shard_map/ppermute | solution.py:354
  54.0 12.4 %collective-permute-start.10 = (bf16[544,128]{1,0:T(8,128)(2,1)S(1)}, bf16[544,128]{1,0:T(8,128)(2,1)S(1)}, u32[]{:S(2)}, u32[]{:S(2)}) collective-permute-start(bf16[544,128]{1,0:T(8,128)(2,1)S(1)} %ship.1), channel_id=1, source_target_pairs={{252,236},{253,237},{254,238},{255,239}} | collective-permute-start | bytes 417800 | tf_op jit(solution)/shard_map/ppermute | solution.py:384
  54.7 14.5 %collective-permute-start.9 = (bf16[544,128]{1,0:T(8,128)(2,1)S(1)}, bf16[544,128]{1,0:T(8,128)(2,1)S(1)}, u32[]{:S(2)}, u32[]{:S(2)}) collective-permute-start(bf16[544,128]{1,0:T(8,128)(2,1)S(1)} %ship.1), channel_id=1, source_target_pairs={{0,320},{4,324},{8,328},{12,332},{16,336},{20,340},{24,344},{28,34... | collective-permute-start | bytes 417800 | tf_op jit(solution)/shard_map/ppermute | solution.py:383
  61.8 12.4 %collective-permute-start.5 = (bf16[1,2,3,128,128]{4,3,2,1,0:T(8,128)(2,1)S(1)}, bf16[1,2,3,128,128]{4,3,2,1,0:T(8,128)(2,1)S(1)}, u32[]{:S(2)}, u32[]{:S(2)}) collective-permute-start(bf16[1,2,3,128,128]{4,3,2,1,0:T(8,128)(2,1)S(1)} %pack.12), channel_id=1, source_target_pairs={{0,4},{4,8},{8,12},{12,16},{16,20},{20,24},{24,28},{28,32},{32,36}... | collective-permute-start | bytes 589832 | tf_op jit(solution)/shard_map/ppermute | solution.py:354
  63.7 13.7 %collective-permute-start.4 = (bf16[1,2,3,128,128]{4,3,2,1,0:T(8,128)(2,1)S(1)}, bf16[1,2,3,128,128]{4,3,2,1,0:T(8,128)(2,1)S(1)}, u32[]{:S(2)}, u32[]{:S(2)}) collective-permute-start(bf16[1,2,3,128,128]{4,3,2,1,0:T(8,128)(2,1)S(1)} %pack.11.refs_5_), channel_id=1, source_target_pairs={{0,4},{4,8},{8,12},{12,16},{16,20},{20,24},{24,28},{28,32},{32,36}... | collective-permute-start | bytes 589832 | tf_op jit(solution)/shard_map/ppermute | solution.py:354
  66.4 8.7 %collective-permute-start.11 = (bf16[544,128]{1,0:T(8,128)(2,1)S(1)}, bf16[544,128]{1,0:T(8,128)(2,1)S(1)}, u32[]{:S(2)}, u32[]{:S(2)}) collective-permute-start(bf16[544,128]{1,0:T(8,128)(2,1)S(1)} %collective-permute-done.10.refs_9_), channel_id=1, source_target_pairs={{236,316},{237,317},{238,318},{239,319}} | collective-permute-start | bytes 417800 | tf_op jit(solution)/shard_map/ppermute | solution.py:385

commit v6 on v5

--- a/solution.py
+++ b/solution.py
@@ -15,6 +15,7 @@
 BLOCK = 16
 AHEAD = 4
 SENT = 9
+SPARE = 24
 PARAMS = pltpu.CompilerParams(vmem_limit_bytes=12 << 20)
 FIRST = pltpu.CompilerParams(vmem_limit_bytes=56_000_000)
 VMEM = pl.BlockSpec(memory_space=pltpu.VMEM)
@@ -43,7 +44,7 @@
 
 def spread(value, rows, out_ref, p, r):
     frames = value.shape[0] // SIDE
-    rows[...] = value.astype(jnp.float32)
+    rows[pl.ds(0, value.shape[0]), :] = value.astype(jnp.float32)
     for t in range(1, frames):
         out_ref[p, r, t - 1] = rows[pl.ds(t, SIDE, stride=frames), :].astype(jnp.bfloat16)
 
@@ -75,7 +76,7 @@
     lane = lax.broadcasted_iota(jnp.int32, (BLOCK, SIDE), 1)
     sign = 1.0 - 2.0 * (lane % 2).astype(jnp.float32)
     for r in range(2):
-        rows[r] = v_ref[channel, p, r].astype(jnp.float32)
+        rows[r, pl.ds(0, frames * SIDE), :] = v_ref[channel, p, r].astype(jnp.float32)
     for n in range(0, SIDE, BLOCK):
         shaped = [taps_ref[pl.ds(count * n + k, BLOCK, stride=count), :] * sign for k in range(count)]
         for r in range(2):
@@ -195,7 +196,7 @@
 
 def lay_kernel(p0, p3, border, p5, p6, theirs, relayed, out_ref, every, plain):
     half = lax.axis_index("half")
-    peers = out_ref.shape[0] // (2 * SENT)
+    peers = (out_ref.shape[0] - SPARE) // (2 * SENT)
     plain[...] = theirs[...].astype(jnp.float32) + relayed[...].astype(jnp.float32)
     lay_out(plain.at[pl.ds(8, plain.shape[0] - 16)], out_ref, peers, 2 * SENT, SENT)
 
@@ -236,7 +237,7 @@
         row = pl.ds(3 * group * stride + 8, 1)
         same_ref[row, :] = jnp.where(lane < SIDE // 2, same_ref[row, :], value[SIDE - 1 :])
 
-    out_ref[...] = same_ref[...].astype(jnp.bfloat16)
+    out_ref[...] = same_ref[pl.ds(0, out_ref.shape[0]), :].astype(jnp.bfloat16)
 
 
 def tree_kernel(scale, in_ref, out_ref, wide, steps, flat):
@@ -245,7 +246,7 @@
     sources = in_ref.shape[0] // step
     per = sources // (NT // 2)
     lane = lax.broadcasted_iota(jnp.int32, (16, SIDE), 1)
-    wide[...] = in_ref[...].astype(jnp.float32)
+    wide[pl.ds(0, in_ref.shape[0]), :] = in_ref[...].astype(jnp.float32)
     steps[...] = jnp.zeros(steps.shape, jnp.float32)
     for whose in range(2):
         base = 8 * 16 * (half if whose == 0 else 1 - half)
@@ -329,6 +330,7 @@
 
     halo = (2, 2, count - 1, SIDE, SIDE)
     interleaved = (SIDE * frames, SIDE)
+    roomy = (SIDE * frames + 8, SIDE)
     first = call(
         first_pack_kernel,
         "pack_first",
@@ -337,7 +339,7 @@
         bf16,
         [
             pltpu.VMEM((2, 2) + interleaved, bf16),
-            pltpu.VMEM((2, 2) + interleaved, f32),
+            pltpu.VMEM((2, 2) + roomy, f32),
             pltpu.SemaphoreType.DMA((2, 2)),
         ],
         specs=[ANY],
@@ -349,13 +351,13 @@
     def send(place, pols, after):
         shape = (len(pols),) + halo[1:]
         body = bind(pack_kernel, place, pols)
-        value = call(body, "pack", [rows], shape, bf16, [pltpu.VMEM((2,) + interleaved, f32)], after=after)
+        value = call(body, "pack", [rows], shape, bf16, [pltpu.VMEM((2,) + roomy, f32)], after=after)
         packs.append(value)
         near[place].append(lax.ppermute(value, ("half", "tm"), pairs))
 
     constants = [coefficients, fourier, back, cos, sin]
     scratch = [
-        pltpu.VMEM((2,) + interleaved, f32),
+        pltpu.VMEM((2,) + roomy, f32),
         pltpu.VMEM((2 * SIDE, frames * SIDE), bf16),
         pltpu.VMEM((frames * SIDE, 2 * SIDE), bf16),
     ]
@@ -404,7 +406,7 @@
         lay_kernel,
         "lay",
         [power[0], power[3], *power[4:7], theirs, relayed],
-        sent,
+        (sent[0] + SPARE, SIDE),
         f32,
         [pltpu.VMEM((8 + 4 * SIDE + 8, SIDE), f32), pltpu.VMEM(shipped, f32)],
         after=[part],
@@ -413,7 +415,7 @@
         last_kernel,
         "last",
         [rows, *constants, near[last][1], part, begun, power[4], power[6], laid],
-        [(sent, bf16), (sent, f32)],
+        [(sent, bf16), ((sent[0] + SPARE, SIDE), f32)],
         None,
         scratch[1:] + [pltpu.VMEM((8 + SIDE + 8, SIDE), f32)],
         flops // 2,
@@ -428,7 +430,11 @@
         [owned],
         (2, NT, channels * length // (2 * peers)),
         f32,
-        [pltpu.VMEM(sent, f32), pltpu.VMEM((16 * NT, SIDE), f32), pltpu.VMEM((8 * NT, SIDE), f32)],
+        [
+            pltpu.VMEM((sent[0] + 16 * SENT, SIDE), f32),
+            pltpu.VMEM((16 * NT + 16, SIDE), f32),
+            pltpu.VMEM((8 * NT + 8, SIDE), f32),
+        ],
     )
 
 

time: 100 us -> 100 us (level)
  transfers between devices with their start and end apart: 12 -> 12, of which waited for: 8 -> 8; matrix products, arithmetic and copies ran while one was open for 0% -> 0% of each run, Pallas kernels for 9% -> 10%
where the time goes in v6:
time: 100 us
  starting transfers between devices  33.7 us (34%)
  waiting for transfers between devices  32.5 us (32%)
  blocking collectives  20.7 us (21%)
  Pallas kernels  12.8 us (13%)
    ppermute x8, waiting for transfers between devices, send(): near[place].append(lax.ppermute(value, ('half', 'tm'), pairs))  28.1 us
    ppermute x8, starting transfers between devices, send(): near[place].append(lax.ppermute(value, ('half', 'tm'), pairs))  21 us
    all_to_all x1, blocking collectives, per_device(): lax.all_to_all(out, 'tm', split_axis=0, concat_axis=0, tiled=True)  20.7 us
    pallas_call x21, Pallas kernels, call(): pl.pallas_call(ordered, in_specs=(specs or [VMEM] * len(args)) + [ANY] *...  12.8 us
    ppermute x1, starting transfers between devices, per_device(): theirs = lax.ppermute(ship, ('half', 'tm'), straight)  6.95 us
    ppermute x1, starting transfers between devices, per_device(): lax.ppermute(first, ('half', 'tm'), pairs)  4.41 us
    ppermute x1, waiting for transfers between devices, per_device(): lax.ppermute(first, ('half', 'tm'), pairs)  2.39 us
    ppermute x1, waiting for transfers between devices, per_device(): theirs = lax.ppermute(ship, ('half', 'tm'), straight)  2.05 us
  transfers between devices with their start and end apart: 12, of which 8 were waited for; matrix products, arithmetic and copies ran while one was open for 0% of the time, Pallas kernels for 10%

profile of v6, /device:TPU:2, one launch (start us, length us, event | category | flops | bytes accessed | tf_op | source)
XLA Modules:
  0.0 100.0 jit_solution(15842882781266140172)
XLA Ops:
  0.0 1.3 %pack_first.1.refs_1_ = bf16[2,2,3,128,128]{4,3,2,1,0:T(8,128)(2,1)S(1)} custom-call(bf16[8,2,2,512,128]{4,3,2,1,0:T(8,128)(2,1)} %bitcast.12), custom_call_target="tpu_custom_call" | custom-call | flops 1048576 | bytes 1048576 | tf_op jit(solution)/shard_map/pack_first/pallas_call | solution.py:297
  1.3 4.4 %collective-permute-start.3 = (bf16[2,2,3,128,128]{4,3,2,1,0:T(8,128)(2,1)S(1)}, bf16[2,2,3,128,128]{4,3,2,1,0:T(8,128)(2,1)S(1)}, u32[]{:S(2)}, u32[]{:S(2)}) collective-permute-start(bf16[2,2,3,128,128]{4,3,2,1,0:T(8,128)(2,1)S(1)} %pack_first.1.refs_1_), channel_id=1, source_target_pairs={{0,4},{4,8},{8,12},{12,16},{16,20},{20,24},{24,28},{28,32},{32,36}... | collective-permute-start | bytes 1179656 | tf_op jit(solution)/shard_map/ppermute | solution.py:349
  5.7 0.1 pack.10
  5.9 0.0 copy-start.1
  5.9 0.0 copy-start.2
  5.9 0.0 copy-start.3
  5.9 0.0 copy-start.4
  5.9 0.0 copy-start.5
  6.0 4.4 %collective-permute-start.2 = (bf16[2,2,3,128,128]{4,3,2,1,0:T(8,128)(2,1)S(1)}, bf16[2,2,3,128,128]{4,3,2,1,0:T(8,128)(2,1)S(1)}, u32[]{:S(2)}, u32[]{:S(2)}) collective-permute-start(bf16[2,2,3,128,128]{4,3,2,1,0:T(8,128)(2,1)S(1)} %pack.10), channel_id=1, source_target_pairs={{0,4},{4,8},{8,12},{12,16},{16,20},{20,24},{24,28},{28,32},{32,36}... | collective-permute-start | bytes 1179656 | tf_op jit(solution)/shard_map/ppermute | solution.py:356
  10.4 0.1 pack.9
  10.5 4.3 %collective-permute-start.1 = (bf16[2,2,3,128,128]{4,3,2,1,0:T(8,128)(2,1)S(1)}, bf16[2,2,3,128,128]{4,3,2,1,0:T(8,128)(2,1)S(1)}, u32[]{:S(2)}, u32[]{:S(2)}) collective-permute-start(bf16[2,2,3,128,128]{4,3,2,1,0:T(8,128)(2,1)S(1)} %pack.9), channel_id=1, source_target_pairs={{0,4},{4,8},{8,12},{12,16},{16,20},{20,24},{24,28},{28,32},{32,36}... | collective-permute-start | bytes 1179656 | tf_op jit(solution)/shard_map/ppermute | solution.py:356
  14.8 0.1 pack.8
  14.9 1.9 %collective-permute-start = (bf16[2,2,3,128,128]{4,3,2,1,0:T(8,128)(2,1)S(1)}, bf16[2,2,3,128,128]{4,3,2,1,0:T(8,128)(2,1)S(1)}, u32[]{:S(2)}, u32[]{:S(2)}) collective-permute-start(bf16[2,2,3,128,128]{4,3,2,1,0:T(8,128)(2,1)S(1)} %pack.8), channel_id=1, source_target_pairs={{0,4},{4,8},{8,12},{12,16},{16,20},{20,24},{24,28},{28,32},{32,36}... | collective-permute-start | bytes 1179656 | tf_op jit(solution)/shard_map/ppermute | solution.py:356
  16.9 2.4 %collective-permute-done.3.refs_6_ = bf16[2,2,3,128,128]{4,3,2,1,0:T(8,128)(2,1)S(1)} collective-permute-done((bf16[2,2,3,128,128]{4,3,2,1,0:T(8,128)(2,1)S(1)}, bf16[2,2,3,128,128]{4,3,2,1,0:T(8,128)(2,1)S(1)}, u32[]{:S(2)}, u32[]{:S(2)}) %collective-permute-start.3) | collective-permute-done | bytes 393248 | tf_op jit(solution)/shard_map/ppermute | solution.py:349
  19.3 1.1 %chunk.7.refs_7_.refs_1_.refs_0_ = f32[128,128]{1,0:T(8,128)S(1)} custom-call(bf16[8,2,2,512,128]{4,3,2,1,0:T(8,128)(2,1)S(1)} %bitcast.16, f32[512,128]{1,0:T(8,128)S(1)} %bitcast.30, bf16[256,256]{1,0:T(8,128)(2,1)S(1)} %copy-done.3, bf16[256,256]{1,0:T(8,128)(2,1)S(1)} %copy-done.2, f32[128,128]{1,0:T(8,128)S(1)} %copy-done.4, f32[128,128]{1,0:T(8,128)S(1)} %copy-done.5, ...), custom_call_target="tpu_custom_call" | custom-call | flops 314572800 | bytes 1048576 | tf_op jit(solution)/shard_map/chunk/pallas_call | solution.py:297
  20.4 0.1 pack.15
  20.5 1.9 %collective-permute-start.8 = (bf16[2,2,3,128,128]{4,3,2,1,0:T(8,128)(2,1)S(1)}, bf16[2,2,3,128,128]{4,3,2,1,0:T(8,128)(2,1)S(1)}, u32[]{:S(2)}, u32[]{:S(2)}) collective-permute-start(bf16[2,2,3,128,128]{4,3,2,1,0:T(8,128)(2,1)S(1)} %pack.15), channel_id=1, source_target_pairs={{0,4},{4,8},{8,12},{12,16},{16,20},{20,24},{24,28},{28,32},{32,36}... | collective-permute-start | bytes 1179656 | tf_op jit(solution)/shard_map/ppermute | solution.py:356
  22.4 5.3 %collective-permute-done.2.refs_6_ = bf16[2,2,3,128,128]{4,3,2,1,0:T(8,128)(2,1)S(1)} collective-permute-done((bf16[2,2,3,128,128]{4,3,2,1,0:T(8,128)(2,1)S(1)}, bf16[2,2,3,128,128]{4,3,2,1,0:T(8,128)(2,1)S(1)}, u32[]{:S(2)}, u32[]{:S(2)}) %collective-permute-start.2) | collective-permute-done | bytes 393248 | tf_op jit(solution)/shard_map/ppermute | solution.py:356
  27.7 1.1 %chunk.8.refs_7_.refs_1_ = f32[128,128]{1,0:T(8,128)S(1)} custom-call(bf16[8,2,2,512,128]{4,3,2,1,0:T(8,128)(2,1)S(1)} %bitcast.18, f32[512,128]{1,0:T(8,128)S(1)} %bitcast.31, bf16[256,256]{1,0:T(8,128)(2,1)S(1)} %copy-done.3, bf16[256,256]{1,0:T(8,128)(2,1)S(1)} %copy-done.2, f32[128,128]{1,0:T(8,128)S(1)} %copy-done.4, f32[128,128]{1,0:T(8,128)S(1)} %copy-done.5, ...), custom_call_target="tpu_custom_call" | custom-call | flops 314572800 | bytes 1048576 | tf_op jit(solution)/shard_map/chunk/pallas_call | solution.py:297
  28.7 0.1 pack.14
  28.9 1.9 %collective-permute-start.7 = (bf16[2,2,3,128,128]{4,3,2,1,0:T(8,128)(2,1)S(1)}, bf16[2,2,3,128,128]{4,3,2,1,0:T(8,128)(2,1)S(1)}, u32[]{:S(2)}, u32[]{:S(2)}) collective-permute-start(bf16[2,2,3,128,128]{4,3,2,1,0:T(8,128)(2,1)S(1)} %pack.14), channel_id=1, source_target_pairs={{0,4},{4,8},{8,12},{12,16},{16,20},{20,24},{24,28},{28,32},{32,36}... | collective-permute-start | bytes 1179656 | tf_op jit(solution)/shard_map/ppermute | solution.py:356
  30.8 5.3 %collective-permute-done.1.refs_6_ = bf16[2,2,3,128,128]{4,3,2,1,0:T(8,128)(2,1)S(1)} collective-permute-done((bf16[2,2,3,128,128]{4,3,2,1,0:T(8,128)(2,1)S(1)}, bf16[2,2,3,128,128]{4,3,2,1,0:T(8,128)(2,1)S(1)}, u32[]{:S(2)}, u32[]{:S(2)}) %collective-permute-start.1) | collective-permute-done | bytes 393248 | tf_op jit(solution)/shard_map/ppermute | solution.py:356
  36.1 1.1 %chunk.9.refs_7_.refs_1_.refs_2_ = f32[128,128]{1,0:T(8,128)S(1)} custom-call(bf16[8,2,2,512,128]{4,3,2,1,0:T(8,128)(2,1)S(1)} %bitcast.20, f32[512,128]{1,0:T(8,128)S(1)} %bitcast.32, bf16[256,256]{1,0:T(8,128)(2,1)S(1)} %copy-done.3, bf16[256,256]{1,0:T(8,128)(2,1)S(1)} %copy-done.2, f32[128,128]{1,0:T(8,128)S(1)} %copy-done.4, f32[128,128]{1,0:T(8,128)S(1)} %copy-done.5, ...), custom_call_target="tpu_custom_call" | custom-call | flops 314572800 | bytes 1048576 | tf_op jit(solution)/shard_map/chunk/pallas_call | solution.py:297
  37.2 0.1 pack.13
  37.3 1.9 %collective-permute-start.6 = (bf16[2,2,3,128,128]{4,3,2,1,0:T(8,128)(2,1)S(1)}, bf16[2,2,3,128,128]{4,3,2,1,0:T(8,128)(2,1)S(1)}, u32[]{:S(2)}, u32[]{:S(2)}) collective-permute-start(bf16[2,2,3,128,128]{4,3,2,1,0:T(8,128)(2,1)S(1)} %pack.13), channel_id=1, source_target_pairs={{0,4},{4,8},{8,12},{12,16},{16,20},{20,24},{24,28},{28,32},{32,36}... | collective-permute-start | bytes 1179656 | tf_op jit(solution)/shard_map/ppermute | solution.py:356
  39.2 5.3 %collective-permute-done.refs_6_ = bf16[2,2,3,128,128]{4,3,2,1,0:T(8,128)(2,1)S(1)} collective-permute-done((bf16[2,2,3,128,128]{4,3,2,1,0:T(8,128)(2,1)S(1)}, bf16[2,2,3,128,128]{4,3,2,1,0:T(8,128)(2,1)S(1)}, u32[]{:S(2)}, u32[]{:S(2)}) %collective-permute-start) | collective-permute-done | bytes 393248 | tf_op jit(solution)/shard_map/ppermute | solution.py:356
  44.5 1.1 %chunk.10.refs_1_.refs_7_.refs_3_ = f32[128,128]{1,0:T(8,128)S(1)} custom-call(bf16[8,2,2,512,128]{4,3,2,1,0:T(8,128)(2,1)S(1)} %bitcast.22, f32[512,128]{1,0:T(8,128)S(1)} %bitcast.33, bf16[256,256]{1,0:T(8,128)(2,1)S(1)} %copy-done.3, bf16[256,256]{1,0:T(8,128)(2,1)S(1)} %copy-done.2, f32[128,128]{1,0:T(8,128)S(1)} %copy-done.4, f32[128,128]{1,0:T(8,128)S(1)} %copy-done.5, ...), custom_call_target="tpu_custom_call" | custom-call | flops 314572800 | bytes 1048576 | tf_op jit(solution)/shard_map/chunk/pallas_call | solution.py:297
  45.6 0.1 pack.11.refs_5_
  45.7 7.3 %collective-permute-done.8.refs_6_ = bf16[2,2,3,128,128]{4,3,2,1,0:T(8,128)(2,1)S(1)} collective-permute-done((bf16[2,2,3,128,128]{4,3,2,1,0:T(8,128)(2,1)S(1)}, bf16[2,2,3,128,128]{4,3,2,1,0:T(8,128)(2,1)S(1)}, u32[]{:S(2)}, u32[]{:S(2)}) %collective-permute-start.8) | collective-permute-done | bytes 393248 | tf_op jit(solution)/shard_map/ppermute | solution.py:356
  53.0 1.1 %chunk.11.refs_4_.refs_7_.refs_2_.refs_9_ = f32[128,128]{1,0:T(8,128)S(1)} custom-call(bf16[8,2,2,512,128]{4,3,2,1,0:T(8,128)(2,1)S(1)} %bitcast.24, f32[512,128]{1,0:T(8,128)S(1)} %bitcast.34, bf16[256,256]{1,0:T(8,128)(2,1)S(1)} %copy-done.3, bf16[256,256]{1,0:T(8,128)(2,1)S(1)} %copy-done.2, f32[128,128]{1,0:T(8,128)S(1)} %copy-done.4, ...), custom_call_target="tpu_custom_call" | custom-call | flops 314572800 | bytes 1048576 | tf_op jit(solution)/shard_map/chunk/pallas_call | solution.py:297
  54.1 0.7 collective-permute-start.10
  54.7 6.9 %collective-permute-start.9 = (bf16[544,128]{1,0:T(8,128)(2,1)S(1)}, bf16[544,128]{1,0:T(8,128)(2,1)S(1)}, u32[]{:S(2)}, u32[]{:S(2)}) collective-permute-start(bf16[544,128]{1,0:T(8,128)(2,1)S(1)} %ship.1), channel_id=1, source_target_pairs={{0,320},{4,324},{8,328},{12,332},{16,336},{20,340},{24,344},{28,34... | collective-permute-start | bytes 417800 | tf_op jit(solution)/shard_map/ppermute | solution.py:385
  61.7 0.1 pack.12
  61.8 1.9 %collective-permute-start.5 = (bf16[1,2,3,128,128]{4,3,2,1,0:T(8,128)(2,1)S(1)}, bf16[1,2,3,128,128]{4,3,2,1,0:T(8,128)(2,1)S(1)}, u32[]{:S(2)}, u32[]{:S(2)}) collective-permute-start(bf16[1,2,3,128,128]{4,3,2,1,0:T(8,128)(2,1)S(1)} %pack.12), channel_id=1, source_target_pairs={{0,4},{4,8},{8,12},{12,16},{16,20},{20,24},{24,28},{28,32},{32,36}... | collective-permute-start | bytes 589832 | tf_op jit(solution)/shard_map/ppermute | solution.py:356
  63.7 2.7 %collective-permute-start.4 = (bf16[1,2,3,128,128]{4,3,2,1,0:T(8,128)(2,1)S(1)}, bf16[1,2,3,128,128]{4,3,2,1,0:T(8,128)(2,1)S(1)}, u32[]{:S(2)}, u32[]{:S(2)}) collective-permute-start(bf16[1,2,3,128,128]{4,3,2,1,0:T(8,128)(2,1)S(1)} %pack.11.refs_5_), channel_id=1, source_target_pairs={{0,4},{4,8},{8,12},{12,16},{16,20},{20,24},{24,28},{28,32},{32,36}... | collective-permute-start | bytes 589832 | tf_op jit(solution)/shard_map/ppermute | solution.py:356
  66.4 0.0 collective-permute-done.10.refs_9_
  66.5 0.7 collective-permute-start.11
  67.1 2.1 %collective-permute-done.9.refs_8_.refs_5_ = bf16[544,128]{1,0:T(8,128)(2,1)S(1)} collective-permute-done((bf16[544,128]{1,0:T(8,128)(2,1)S(1)}, bf16[544,128]{1,0:T(8,128)(2,1)S(1)}, u32[]{:S(2)}, u32[]{:S(2)}) %collective-permute-start.9) | collective-permute-done | bytes 139296 | tf_op jit(solution)/shard_map/ppermute | solution.py:385
  69.2 1.1 %chunk.12.refs_7_.refs_3_ = f32[128,128]{1,0:T(8,128)S(1)} custom-call(bf16[8,2,2,512,128]{4,3,2,1,0:T(8,128)(2,1)S(1)} %bitcast.26, f32[512,128]{1,0:T(8,128)S(1)} %bitcast.35, bf16[256,256]{1,0:T(8,128)(2,1)S(1)} %copy-done.3, bf16[256,256]{1,0:T(8,128)(2,1)S(1)} %copy-done.2, f32[128,128]{1,0:T(8,128)S(1)} %copy-done.4, f32[128,128]{1,0:T(8,128)S(1)} %copy-done.5, ...), custom_call_target="tpu_custom_call" | custom-call | flops 314572800 | bytes 1048576 | tf_op jit(solution)/shard_map/chunk/pallas_call | solution.py:297
  70.3 0.0 collective-permute-done.6.refs_6_
  70.3 1.1 %chunk.13.refs_7_.refs_4_.refs_10_ = f32[128,128]{1,0:T(8,128)S(1)} custom-call(bf16[8,2,2,512,128]{4,3,2,1,0:T(8,128)(2,1)S(1)} %bitcast.27, f32[512,128]{1,0:T(8,128)S(1)} %bitcast.36, bf16[256,256]{1,0:T(8,128)(2,1)S(1)} %copy-done.3, bf16[256,256]{1,0:T(8,128)(2,1)S(1)} %copy-done.2, f32[128,128]{1,0:T(8,128)S(1)} %copy-done.4, ...), custom_call_target="tpu_custom_call" | custom-call | flops 314572800 | bytes 1048576 | tf_op jit(solution)/shard_map/chunk/pallas_call | solution.py:297
  71.3 2.9 %collective-permute-done.5.refs_6_ = bf16[1,2,3,128,128]{4,3,2,1,0:T(8,128)(2,1)S(1)} collective-permute-done((bf16[1,2,3,128,128]{4,3,2,1,0:T(8,128)(2,1)S(1)}, bf16[1,2,3,128,128]{4,3,2,1,0:T(8,128)(2,1)S(1)}, u32[]{:S(2)}, u32[]{:S(2)}) %collective-permute-start.5) | collective-permute-done | bytes 196640 | tf_op jit(solution)/shard_map/ppermute | solution.py:356
  74.2 0.9 chunk_early.1
  75.1 0.2 lay.1.refs_11_
  75.3 2.1 %collective-permute-done.4.refs_6_ = bf16[1,2,3,128,128]{4,3,2,1,0:T(8,128)(2,1)S(1)} collective-permute-done((bf16[1,2,3,128,128]{4,3,2,1,0:T(8,128)(2,1)S(1)}, bf16[1,2,3,128,128]{4,3,2,1,0:T(8,128)(2,1)S(1)}, u32[]{:S(2)}, u32[]{:S(2)}) %collective-permute-start.4) | collective-permute-done | bytes 196640 | tf_op jit(solution)/shard_map/ppermute | solution.py:356
  77.4 0.6 last.1
  78.0 20.7 %all_to_all.5 = bf16[64,9,2,128]{3,2,1,0:T(2,128)(2,1)S(1)} all-to-all(bf16[64,9,2,128]{3,2,1,0:T(2,128)(2,1)S(1)} %bitcast.40), channel_id=1, replica_groups=mesh['half'=2,'tm'=64,'chan'=4] {'tm'}, dimensions={0} | all-to-all | bytes 589824 | tf_op jit(solution)/shard_map/all_to_all | solution.py:425
  98.7 1.3 %tree.1 = f32[2,16,1024]{2,1,0:T(8,128)} custom-call(bf16[1152,128]{1,0:T(8,128)(2,1)S(1)} %bitcast.39), custom_call_target="tpu_custom_call" | custom-call | flops 1048576 | bytes 1048576 | tf_op jit(solution)/shard_map/tree/pallas_call | solution.py:297
  (10 shorter events, 0.0 us)
Async XLA Ops:
  0.0 5.7 %copy-start = (bf16[8,2,2,4,16384]{4,3,2,1,0:T(4,128)(2,1)S(1)}, bf16[8,2,2,4,16384]{4,3,2,1,0:T(4,128)(2,1)}, u32[]{:S(2)}) copy-start(bf16[8,2,2,4,16384]{4,3,2,1,0:T(4,128)(2,1)} %param.6) | copy-start | bytes 12582916
  1.3 17.9 %collective-permute-start.3 = (bf16[2,2,3,128,128]{4,3,2,1,0:T(8,128)(2,1)S(1)}, bf16[2,2,3,128,128]{4,3,2,1,0:T(8,128)(2,1)S(1)}, u32[]{:S(2)}, u32[]{:S(2)}) collective-permute-start(bf16[2,2,3,128,128]{4,3,2,1,0:T(8,128)(2,1)S(1)} %pack_first.1.refs_1_), channel_id=1, source_target_pairs={{0,4},{4,8},{8,12},{12,16},{16,20},{20,24},{24,28},{28,32},{32,36}... | collective-permute-start | bytes 1179656 | tf_op jit(solution)/shard_map/ppermute | solution.py:349
  5.9 13.4 %copy-start.1 = (f32[4,16384]{1,0:T(4,128)S(1)}, f32[4,16384]{1,0:T(4,128)}, u32[]{:S(2)}) copy-start(f32[4,16384]{1,0:T(4,128)} %param.7) | copy-start | bytes 786436
  5.9 13.4 %copy-start.2 = (bf16[256,256]{1,0:T(8,128)(2,1)S(1)}, bf16[256,256]{1,0:T(8,128)(2,1)}, u32[]{:S(2)}) copy-start(bf16[256,256]{1,0:T(8,128)(2,1)} %constant.8.clone.refs_3_) | copy-start | bytes 393220
  5.9 13.3 %copy-start.3 = (bf16[256,256]{1,0:T(8,128)(2,1)S(1)}, bf16[256,256]{1,0:T(8,128)(2,1)}, u32[]{:S(2)}) copy-start(bf16[256,256]{1,0:T(8,128)(2,1)} %constant.9.clone.refs_2_) | copy-start | bytes 393220
  5.9 13.3 %copy-start.4 = (f32[128,128]{1,0:T(8,128)S(1)}, f32[128,128]{1,0:T(8,128)}, u32[]{:S(2)}) copy-start(f32[128,128]{1,0:T(8,128)} %constant.10.clone.refs_4_) | copy-start | bytes 196612
  5.9 13.3 %copy-start.5 = (f32[128,128]{1,0:T(8,128)S(1)}, f32[128,128]{1,0:T(8,128)}, u32[]{:S(2)}) copy-start(f32[128,128]{1,0:T(8,128)} %constant.11.clone.refs_5_) | copy-start | bytes 196612
  6.0 21.7 %collective-permute-start.2 = (bf16[2,2,3,128,128]{4,3,2,1,0:T(8,128)(2,1)S(1)}, bf16[2,2,3,128,128]{4,3,2,1,0:T(8,128)(2,1)S(1)}, u32[]{:S(2)}, u32[]{:S(2)}) collective-permute-start(bf16[2,2,3,128,128]{4,3,2,1,0:T(8,128)(2,1)S(1)} %pack.10), channel_id=1, source_target_pairs={{0,4},{4,8},{8,12},{12,16},{16,20},{20,24},{24,28},{28,32},{32,36}... | collective-permute-start | bytes 1179656 | tf_op jit(solution)/shard_map/ppermute | solution.py:356
  10.5 25.6 %collective-permute-start.1 = (bf16[2,2,3,128,128]{4,3,2,1,0:T(8,128)(2,1)S(1)}, bf16[2,2,3,128,128]{4,3,2,1,0:T(8,128)(2,1)S(1)}, u32[]{:S(2)}, u32[]{:S(2)}) collective-permute-start(bf16[2,2,3,128,128]{4,3,2,1,0:T(8,128)(2,1)S(1)} %pack.9), channel_id=1, source_target_pairs={{0,4},{4,8},{8,12},{12,16},{16,20},{20,24},{24,28},{28,32},{32,36}... | collective-permute-start | bytes 1179656 | tf_op jit(solution)/shard_map/ppermute | solution.py:356
  14.9 29.6 %collective-permute-start = (bf16[2,2,3,128,128]{4,3,2,1,0:T(8,128)(2,1)S(1)}, bf16[2,2,3,128,128]{4,3,2,1,0:T(8,128)(2,1)S(1)}, u32[]{:S(2)}, u32[]{:S(2)}) collective-permute-start(bf16[2,2,3,128,128]{4,3,2,1,0:T(8,128)(2,1)S(1)} %pack.8), channel_id=1, source_target_pairs={{0,4},{4,8},{8,12},{12,16},{16,20},{20,24},{24,28},{28,32},{32,36}... | collective-permute-start | bytes 1179656 | tf_op jit(solution)/shard_map/ppermute | solution.py:356
  20.5 32.5 %collective-permute-start.8 = (bf16[2,2,3,128,128]{4,3,2,1,0:T(8,128)(2,1)S(1)}, bf16[2,2,3,128,128]{4,3,2,1,0:T(8,128)(2,1)S(1)}, u32[]{:S(2)}, u32[]{:S(2)}) collective-permute-start(bf16[2,2,3,128,128]{4,3,2,1,0:T(8,128)(2,1)S(1)} %pack.15), channel_id=1, source_target_pairs={{0,4},{4,8},{8,12},{12,16},{16,20},{20,24},{24,28},{28,32},{32,36}... | collective-permute-start | bytes 1179656 | tf_op jit(solution)/shard_map/ppermute | solution.py:356
  28.9 34.8 %collective-permute-start.7 = (bf16[2,2,3,128,128]{4,3,2,1,0:T(8,128)(2,1)S(1)}, bf16[2,2,3,128,128]{4,3,2,1,0:T(8,128)(2,1)S(1)}, u32[]{:S(2)}, u32[]{:S(2)}) collective-permute-start(bf16[2,2,3,128,128]{4,3,2,1,0:T(8,128)(2,1)S(1)} %pack.14), channel_id=1, source_target_pairs={{0,4},{4,8},{8,12},{12,16},{16,20},{20,24},{24,28},{28,32},{32,36}... | collective-permute-start | bytes 1179656 | tf_op jit(solution)/shard_map/ppermute | solution.py:356
  37.3 32.9 %collective-permute-start.6 = (bf16[2,2,3,128,128]{4,3,2,1,0:T(8,128)(2,1)S(1)}, bf16[2,2,3,128,128]{4,3,2,1,0:T(8,128)(2,1)S(1)}, u32[]{:S(2)}, u32[]{:S(2)}) collective-permute-start(bf16[2,2,3,128,128]{4,3,2,1,0:T(8,128)(2,1)S(1)} %pack.13), channel_id=1, source_target_pairs={{0,4},{4,8},{8,12},{12,16},{16,20},{20,24},{24,28},{28,32},{32,36}... | collective-permute-start | bytes 1179656 | tf_op jit(solution)/shard_map/ppermute | solution.py:356
  54.1 12.4 %collective-permute-start.10 = (bf16[544,128]{1,0:T(8,128)(2,1)S(1)}, bf16[544,128]{1,0:T(8,128)(2,1)S(1)}, u32[]{:S(2)}, u32[]{:S(2)}) collective-permute-start(bf16[544,128]{1,0:T(8,128)(2,1)S(1)} %ship.1), channel_id=1, source_target_pairs={{252,236},{253,237},{254,238},{255,239}} | collective-permute-start | bytes 417800 | tf_op jit(solution)/shard_map/ppermute | solution.py:386
  54.7 14.5 %collective-permute-start.9 = (bf16[544,128]{1,0:T(8,128)(2,1)S(1)}, bf16[544,128]{1,0:T(8,128)(2,1)S(1)}, u32[]{:S(2)}, u32[]{:S(2)}) collective-permute-start(bf16[544,128]{1,0:T(8,128)(2,1)S(1)} %ship.1), channel_id=1, source_target_pairs={{0,320},{4,324},{8,328},{12,332},{16,336},{20,340},{24,344},{28,34... | collective-permute-start | bytes 417800 | tf_op jit(solution)/shard_map/ppermute | solution.py:385
  61.8 12.4 %collective-permute-start.5 = (bf16[1,2,3,128,128]{4,3,2,1,0:T(8,128)(2,1)S(1)}, bf16[1,2,3,128,128]{4,3,2,1,0:T(8,128)(2,1)S(1)}, u32[]{:S(2)}, u32[]{:S(2)}) collective-permute-start(bf16[1,2,3,128,128]{4,3,2,1,0:T(8,128)(2,1)S(1)} %pack.12), channel_id=1, source_target_pairs={{0,4},{4,8},{8,12},{12,16},{16,20},{20,24},{24,28},{28,32},{32,36}... | collective-permute-start | bytes 589832 | tf_op jit(solution)/shard_map/ppermute | solution.py:356
  63.7 13.7 %collective-permute-start.4 = (bf16[1,2,3,128,128]{4,3,2,1,0:T(8,128)(2,1)S(1)}, bf16[1,2,3,128,128]{4,3,2,1,0:T(8,128)(2,1)S(1)}, u32[]{:S(2)}, u32[]{:S(2)}) collective-permute-start(bf16[1,2,3,128,128]{4,3,2,1,0:T(8,128)(2,1)S(1)} %pack.11.refs_5_), channel_id=1, source_target_pairs={{0,4},{4,8},{8,12},{12,16},{16,20},{20,24},{24,28},{28,32},{32,36}... | collective-permute-start | bytes 589832 | tf_op jit(solution)/shard_map/ppermute | solution.py:356
  66.5 8.7 %collective-permute-start.11 = (bf16[544,128]{1,0:T(8,128)(2,1)S(1)}, bf16[544,128]{1,0:T(8,128)(2,1)S(1)}, u32[]{:S(2)}, u32[]{:S(2)}) collective-permute-start(bf16[544,128]{1,0:T(8,128)(2,1)S(1)} %collective-permute-done.10.refs_9_), channel_id=1, source_target_pairs={{236,316},{237,317},{238,318},{239,319}} | collective-permute-start | bytes 417800 | tf_op jit(solution)/shard_map/ppermute | solution.py:387

commit v7 on v6

--- a/solution.py
+++ b/solution.py
@@ -16,6 +16,7 @@
 AHEAD = 4
 SENT = 9
 SPARE = 24
+ROOM = 24
 PARAMS = pltpu.CompilerParams(vmem_limit_bytes=12 << 20)
 FIRST = pltpu.CompilerParams(vmem_limit_bytes=56_000_000)
 VMEM = pl.BlockSpec(memory_space=pltpu.VMEM)
@@ -245,47 +246,53 @@
     step = 2 * SENT
     sources = in_ref.shape[0] // step
     per = sources // (NT // 2)
-    lane = lax.broadcasted_iota(jnp.int32, (16, SIDE), 1)
+    lane = lax.broadcasted_iota(jnp.int32, (8, SIDE), 1)
     wide[pl.ds(0, in_ref.shape[0]), :] = in_ref[...].astype(jnp.float32)
-    steps[...] = jnp.zeros(steps.shape, jnp.float32)
     for whose in range(2):
-        base = 8 * 16 * (half if whose == 0 else 1 - half)
+        base = 8 * ROOM * (half if whose == 0 else 1 - half)
         for j in range(SENT):
             value = wide[pl.ds(whose * SENT + j, 8, stride=step * per), :]
             for i in range(1, per):
                 value = value + wide[pl.ds(step * i + whose * SENT + j, 8, stride=step * per), :]
-            for row in (j,) if j < 8 else (8, 15):
+            for row in (8 + j,) if j < 8 else (7, 16):
                 if whose == 0:
-                    steps[pl.ds(base + row, 8, stride=16), :] = value
+                    steps[pl.ds(base + row, 8, stride=ROOM), :] = value
                 else:
-                    steps[pl.ds(base + 6 * 16 + row, 2, stride=16), :] = value[:2]
-                    steps[pl.ds(base + row, 6, stride=16), :] = value[2:]
+                    steps[pl.ds(base + 6 * ROOM + row, 2, stride=ROOM), :] = value[:2]
+                    steps[pl.ds(base + row, 6, stride=ROOM), :] = value[2:]
 
     def moved(value, move, sense):
         if move == 0:
             return value
-        if sense > 0:
-            here = pltpu.roll(value, SIDE - move, 1)
-            return jnp.where(lane < SIDE - move, here, pltpu.roll(here, 15, 0))
-        here = pltpu.roll(value, move, 1)
-        return jnp.where(lane >= move, here, pltpu.roll(here, 1, 0))
-
-    for which, sense in enumerate((1, -1)):
-        level = [[steps[pl.ds(16 * s, 16), :]] for s in range(NT)]
-        length = 1
-        while len(level) > 1:
-            level = [
-                [
-                    level[j][d // 2] + moved(level[j + 1][d // 2], d - d // 2, sense)
-                    for d in range(2 * length)
-                ]
-                for j in range(0, len(level), 2)
-            ]
-            length *= 2
+        own, beside = value
+        by = SIDE - move if sense > 0 else move
+        mixed = jnp.where(lane < move if sense > 0 else lane >= SIDE - move, beside, own)
+        return pltpu.roll(mixed, by, 1), pltpu.roll(beside, by, 1)
+
+    senses = (1, -1)
+    levels = [
+        [[(steps[pl.ds(ROOM * s + 8, 8), :], steps[pl.ds(ROOM * s + 8 + sense, 8), :])] for s in range(NT)]
+        for sense in senses
+    ]
+    length = 1
+    while length < NT:
+        nexts = [[], []]
+        for j in range(0, len(levels[0]), 2):
+            for level, following, sense in zip(levels, nexts, senses):
+                following.append(
+                    [
+                        tuple(p + q for p, q in zip(level[j][d // 2], moved(level[j + 1][d // 2], d - d // 2, sense)))
+                        for d in range(2 * length)
+                    ]
+                )
+        levels = nexts
+        length *= 2
+    for which in range(2):
         for d in range(NT):
-            flat[pl.ds(8 * d, 8), :] = level[0][d][:8]
+            flat[which, pl.ds(8 * d, 8), :] = levels[which][0][d][0]
+    for which in range(2):
         for r in range(8):
-            out_ref[which, :, pl.ds(r * SIDE, SIDE)] = flat[pl.ds(r, NT, stride=8), :] * scale
+            out_ref[which, :, pl.ds(r * SIDE, SIDE)] = flat[which, pl.ds(r, NT, stride=8), :] * scale
 
 
 def call(body, name, args, shape, dtype, scratch, flops=1 << 20, after=(), specs=None, params=PARAMS, alias=None):
@@ -432,8 +439,8 @@
         f32,
         [
             pltpu.VMEM((sent[0] + 16 * SENT, SIDE), f32),
-            pltpu.VMEM((16 * NT + 16, SIDE), f32),
-            pltpu.VMEM((8 * NT + 8, SIDE), f32),
+            pltpu.VMEM((ROOM * NT + ROOM, SIDE), f32),
+            pltpu.VMEM((2, 8 * NT + 8, SIDE), f32),
         ],
     )
 

time: 100 us -> 100 us (level)
  no operation moved by 1% of the time
where the time goes in v7:
time: 100 us; the launch traced here: 99.9 us
  starting transfers between devices  33.7 us (34%)
  waiting for transfers between devices  32.5 us (32%)
  blocking collectives  20.7 us (21%)
  Pallas kernels  12.7 us (13%)
    ppermute x8, waiting for transfers between devices, send(): near[place].append(lax.ppermute(value, ('half', 'tm'), pairs))  28.1 us
    ppermute x8, starting transfers between devices, send(): near[place].append(lax.ppermute(value, ('half', 'tm'), pairs))  21 us
    all_to_all x1, blocking collectives, per_device(): lax.all_to_all(out, 'tm', split_axis=0, concat_axis=0, tiled=True)  20.7 us
    pallas_call x21, Pallas kernels, call(): pl.pallas_call(ordered, in_specs=(specs or [VMEM] * len(args)) + [ANY] *...  12.7 us
    ppermute x1, starting transfers between devices, per_device(): theirs = lax.ppermute(ship, ('half', 'tm'), straight)  6.95 us
    ppermute x1, starting transfers between devices, per_device(): lax.ppermute(first, ('half', 'tm'), pairs)  4.41 us
    ppermute x1, waiting for transfers between devices, per_device(): lax.ppermute(first, ('half', 'tm'), pairs)  2.39 us
    ppermute x1, waiting for transfers between devices, per_device(): theirs = lax.ppermute(ship, ('half', 'tm'), straight)  2.05 us
  transfers between devices with their start and end apart: 12, of which 8 were waited for; matrix products, arithmetic and copies ran while one was open for 0% of the time, Pallas kernels for 10%

profile of v7, /device:TPU:2, one launch (start us, length us, event | category | flops | bytes accessed | tf_op | source)
XLA Modules:
  0.0 99.9 jit_solution(2467511716350249683)
XLA Ops:
  0.0 1.3 %pack_first.1.refs_1_ = bf16[2,2,3,128,128]{4,3,2,1,0:T(8,128)(2,1)S(1)} custom-call(bf16[8,2,2,512,128]{4,3,2,1,0:T(8,128)(2,1)} %bitcast.12), custom_call_target="tpu_custom_call" | custom-call | flops 1048576 | bytes 1048576 | tf_op jit(solution)/shard_map/pack_first/pallas_call | solution.py:304
  1.3 4.4 %collective-permute-start.3 = (bf16[2,2,3,128,128]{4,3,2,1,0:T(8,128)(2,1)S(1)}, bf16[2,2,3,128,128]{4,3,2,1,0:T(8,128)(2,1)S(1)}, u32[]{:S(2)}, u32[]{:S(2)}) collective-permute-start(bf16[2,2,3,128,128]{4,3,2,1,0:T(8,128)(2,1)S(1)} %pack_first.1.refs_1_), channel_id=1, source_target_pairs={{0,4},{4,8},{8,12},{12,16},{16,20},{20,24},{24,28},{28,32},{32,36}... | collective-permute-start | bytes 1179656 | tf_op jit(solution)/shard_map/ppermute | solution.py:356
  5.7 0.1 pack.10
  5.9 0.0 copy-start.1
  5.9 0.0 copy-start.2
  5.9 0.0 copy-start.3
  5.9 0.0 copy-start.4
  5.9 0.0 copy-start.5
  6.0 4.4 %collective-permute-start.2 = (bf16[2,2,3,128,128]{4,3,2,1,0:T(8,128)(2,1)S(1)}, bf16[2,2,3,128,128]{4,3,2,1,0:T(8,128)(2,1)S(1)}, u32[]{:S(2)}, u32[]{:S(2)}) collective-permute-start(bf16[2,2,3,128,128]{4,3,2,1,0:T(8,128)(2,1)S(1)} %pack.10), channel_id=1, source_target_pairs={{0,4},{4,8},{8,12},{12,16},{16,20},{20,24},{24,28},{28,32},{32,36}... | collective-permute-start | bytes 1179656 | tf_op jit(solution)/shard_map/ppermute | solution.py:363
  10.4 0.1 pack.9
  10.5 4.3 %collective-permute-start.1 = (bf16[2,2,3,128,128]{4,3,2,1,0:T(8,128)(2,1)S(1)}, bf16[2,2,3,128,128]{4,3,2,1,0:T(8,128)(2,1)S(1)}, u32[]{:S(2)}, u32[]{:S(2)}) collective-permute-start(bf16[2,2,3,128,128]{4,3,2,1,0:T(8,128)(2,1)S(1)} %pack.9), channel_id=1, source_target_pairs={{0,4},{4,8},{8,12},{12,16},{16,20},{20,24},{24,28},{28,32},{32,36}... | collective-permute-start | bytes 1179656 | tf_op jit(solution)/shard_map/ppermute | solution.py:363
  14.8 0.1 pack.8
  14.9 1.9 %collective-permute-start = (bf16[2,2,3,128,128]{4,3,2,1,0:T(8,128)(2,1)S(1)}, bf16[2,2,3,128,128]{4,3,2,1,0:T(8,128)(2,1)S(1)}, u32[]{:S(2)}, u32[]{:S(2)}) collective-permute-start(bf16[2,2,3,128,128]{4,3,2,1,0:T(8,128)(2,1)S(1)} %pack.8), channel_id=1, source_target_pairs={{0,4},{4,8},{8,12},{12,16},{16,20},{20,24},{24,28},{28,32},{32,36}... | collective-permute-start | bytes 1179656 | tf_op jit(solution)/shard_map/ppermute | solution.py:363
  16.9 2.4 %collective-permute-done.3.refs_6_ = bf16[2,2,3,128,128]{4,3,2,1,0:T(8,128)(2,1)S(1)} collective-permute-done((bf16[2,2,3,128,128]{4,3,2,1,0:T(8,128)(2,1)S(1)}, bf16[2,2,3,128,128]{4,3,2,1,0:T(8,128)(2,1)S(1)}, u32[]{:S(2)}, u32[]{:S(2)}) %collective-permute-start.3) | collective-permute-done | bytes 393248 | tf_op jit(solution)/shard_map/ppermute | solution.py:356
  19.3 1.1 %chunk.7.refs_7_.refs_1_.refs_0_ = f32[128,128]{1,0:T(8,128)S(1)} custom-call(bf16[8,2,2,512,128]{4,3,2,1,0:T(8,128)(2,1)S(1)} %bitcast.16, f32[512,128]{1,0:T(8,128)S(1)} %bitcast.30, bf16[256,256]{1,0:T(8,128)(2,1)S(1)} %copy-done.3, bf16[256,256]{1,0:T(8,128)(2,1)S(1)} %copy-done.2, f32[128,128]{1,0:T(8,128)S(1)} %copy-done.4, f32[128,128]{1,0:T(8,128)S(1)} %copy-done.5, ...), custom_call_target="tpu_custom_call" | custom-call | flops 314572800 | bytes 1048576 | tf_op jit(solution)/shard_map/chunk/pallas_call | solution.py:304
  20.4 0.1 pack.15
  20.5 1.9 %collective-permute-start.8 = (bf16[2,2,3,128,128]{4,3,2,1,0:T(8,128)(2,1)S(1)}, bf16[2,2,3,128,128]{4,3,2,1,0:T(8,128)(2,1)S(1)}, u32[]{:S(2)}, u32[]{:S(2)}) collective-permute-start(bf16[2,2,3,128,128]{4,3,2,1,0:T(8,128)(2,1)S(1)} %pack.15), channel_id=1, source_target_pairs={{0,4},{4,8},{8,12},{12,16},{16,20},{20,24},{24,28},{28,32},{32,36}... | collective-permute-start | bytes 1179656 | tf_op jit(solution)/shard_map/ppermute | solution.py:363
  22.4 5.3 %collective-permute-done.2.refs_6_ = bf16[2,2,3,128,128]{4,3,2,1,0:T(8,128)(2,1)S(1)} collective-permute-done((bf16[2,2,3,128,128]{4,3,2,1,0:T(8,128)(2,1)S(1)}, bf16[2,2,3,128,128]{4,3,2,1,0:T(8,128)(2,1)S(1)}, u32[]{:S(2)}, u32[]{:S(2)}) %collective-permute-start.2) | collective-permute-done | bytes 393248 | tf_op jit(solution)/shard_map/ppermute | solution.py:363
  27.7 1.1 %chunk.8.refs_7_.refs_1_ = f32[128,128]{1,0:T(8,128)S(1)} custom-call(bf16[8,2,2,512,128]{4,3,2,1,0:T(8,128)(2,1)S(1)} %bitcast.18, f32[512,128]{1,0:T(8,128)S(1)} %bitcast.31, bf16[256,256]{1,0:T(8,128)(2,1)S(1)} %copy-done.3, bf16[256,256]{1,0:T(8,128)(2,1)S(1)} %copy-done.2, f32[128,128]{1,0:T(8,128)S(1)} %copy-done.4, f32[128,128]{1,0:T(8,128)S(1)} %copy-done.5, ...), custom_call_target="tpu_custom_call" | custom-call | flops 314572800 | bytes 1048576 | tf_op jit(solution)/shard_map/chunk/pallas_call | solution.py:304
  28.7 0.1 pack.14
  28.9 1.9 %collective-permute-start.7 = (bf16[2,2,3,128,128]{4,3,2,1,0:T(8,128)(2,1)S(1)}, bf16[2,2,3,128,128]{4,3,2,1,0:T(8,128)(2,1)S(1)}, u32[]{:S(2)}, u32[]{:S(2)}) collective-permute-start(bf16[2,2,3,128,128]{4,3,2,1,0:T(8,128)(2,1)S(1)} %pack.14), channel_id=1, source_target_pairs={{0,4},{4,8},{8,12},{12,16},{16,20},{20,24},{24,28},{28,32},{32,36}... | collective-permute-start | bytes 1179656 | tf_op jit(solution)/shard_map/ppermute | solution.py:363
  30.8 5.3 %collective-permute-done.1.refs_6_ = bf16[2,2,3,128,128]{4,3,2,1,0:T(8,128)(2,1)S(1)} collective-permute-done((bf16[2,2,3,128,128]{4,3,2,1,0:T(8,128)(2,1)S(1)}, bf16[2,2,3,128,128]{4,3,2,1,0:T(8,128)(2,1)S(1)}, u32[]{:S(2)}, u32[]{:S(2)}) %collective-permute-start.1) | collective-permute-done | bytes 393248 | tf_op jit(solution)/shard_map/ppermute | solution.py:363
  36.1 1.1 %chunk.9.refs_7_.refs_1_.refs_2_ = f32[128,128]{1,0:T(8,128)S(1)} custom-call(bf16[8,2,2,512,128]{4,3,2,1,0:T(8,128)(2,1)S(1)} %bitcast.20, f32[512,128]{1,0:T(8,128)S(1)} %bitcast.32, bf16[256,256]{1,0:T(8,128)(2,1)S(1)} %copy-done.3, bf16[256,256]{1,0:T(8,128)(2,1)S(1)} %copy-done.2, f32[128,128]{1,0:T(8,128)S(1)} %copy-done.4, f32[128,128]{1,0:T(8,128)S(1)} %copy-done.5, ...), custom_call_target="tpu_custom_call" | custom-call | flops 314572800 | bytes 1048576 | tf_op jit(solution)/shard_map/chunk/pallas_call | solution.py:304
  37.2 0.1 pack.13
  37.3 1.9 %collective-permute-start.6 = (bf16[2,2,3,128,128]{4,3,2,1,0:T(8,128)(2,1)S(1)}, bf16[2,2,3,128,128]{4,3,2,1,0:T(8,128)(2,1)S(1)}, u32[]{:S(2)}, u32[]{:S(2)}) collective-permute-start(bf16[2,2,3,128,128]{4,3,2,1,0:T(8,128)(2,1)S(1)} %pack.13), channel_id=1, source_target_pairs={{0,4},{4,8},{8,12},{12,16},{16,20},{20,24},{24,28},{28,32},{32,36}... | collective-permute-start | bytes 1179656 | tf_op jit(solution)/shard_map/ppermute | solution.py:363
  39.2 5.3 %collective-permute-done.refs_6_ = bf16[2,2,3,128,128]{4,3,2,1,0:T(8,128)(2,1)S(1)} collective-permute-done((bf16[2,2,3,128,128]{4,3,2,1,0:T(8,128)(2,1)S(1)}, bf16[2,2,3,128,128]{4,3,2,1,0:T(8,128)(2,1)S(1)}, u32[]{:S(2)}, u32[]{:S(2)}) %collective-permute-start) | collective-permute-done | bytes 393248 | tf_op jit(solution)/shard_map/ppermute | solution.py:363
  44.5 1.1 %chunk.10.refs_1_.refs_7_.refs_3_ = f32[128,128]{1,0:T(8,128)S(1)} custom-call(bf16[8,2,2,512,128]{4,3,2,1,0:T(8,128)(2,1)S(1)} %bitcast.22, f32[512,128]{1,0:T(8,128)S(1)} %bitcast.33, bf16[256,256]{1,0:T(8,128)(2,1)S(1)} %copy-done.3, bf16[256,256]{1,0:T(8,128)(2,1)S(1)} %copy-done.2, f32[128,128]{1,0:T(8,128)S(1)} %copy-done.4, f32[128,128]{1,0:T(8,128)S(1)} %copy-done.5, ...), custom_call_target="tpu_custom_call" | custom-call | flops 314572800 | bytes 1048576 | tf_op jit(solution)/shard_map/chunk/pallas_call | solution.py:304
  45.6 0.1 pack.11.refs_5_
  45.7 7.3 %collective-permute-done.8.refs_6_ = bf16[2,2,3,128,128]{4,3,2,1,0:T(8,128)(2,1)S(1)} collective-permute-done((bf16[2,2,3,128,128]{4,3,2,1,0:T(8,128)(2,1)S(1)}, bf16[2,2,3,128,128]{4,3,2,1,0:T(8,128)(2,1)S(1)}, u32[]{:S(2)}, u32[]{:S(2)}) %collective-permute-start.8) | collective-permute-done | bytes 393248 | tf_op jit(solution)/shard_map/ppermute | solution.py:363
  53.0 1.1 %chunk.11.refs_4_.refs_7_.refs_2_.refs_9_ = f32[128,128]{1,0:T(8,128)S(1)} custom-call(bf16[8,2,2,512,128]{4,3,2,1,0:T(8,128)(2,1)S(1)} %bitcast.24, f32[512,128]{1,0:T(8,128)S(1)} %bitcast.34, bf16[256,256]{1,0:T(8,128)(2,1)S(1)} %copy-done.3, bf16[256,256]{1,0:T(8,128)(2,1)S(1)} %copy-done.2, f32[128,128]{1,0:T(8,128)S(1)} %copy-done.4, ...), custom_call_target="tpu_custom_call" | custom-call | flops 314572800 | bytes 1048576 | tf_op jit(solution)/shard_map/chunk/pallas_call | solution.py:304
  54.1 0.7 collective-permute-start.10
  54.7 6.9 %collective-permute-start.9 = (bf16[544,128]{1,0:T(8,128)(2,1)S(1)}, bf16[544,128]{1,0:T(8,128)(2,1)S(1)}, u32[]{:S(2)}, u32[]{:S(2)}) collective-permute-start(bf16[544,128]{1,0:T(8,128)(2,1)S(1)} %ship.1), channel_id=1, source_target_pairs={{0,320},{4,324},{8,328},{12,332},{16,336},{20,340},{24,344},{28,34... | collective-permute-start | bytes 417800 | tf_op jit(solution)/shard_map/ppermute | solution.py:392
  61.7 0.1 pack.12
  61.8 1.9 %collective-permute-start.5 = (bf16[1,2,3,128,128]{4,3,2,1,0:T(8,128)(2,1)S(1)}, bf16[1,2,3,128,128]{4,3,2,1,0:T(8,128)(2,1)S(1)}, u32[]{:S(2)}, u32[]{:S(2)}) collective-permute-start(bf16[1,2,3,128,128]{4,3,2,1,0:T(8,128)(2,1)S(1)} %pack.12), channel_id=1, source_target_pairs={{0,4},{4,8},{8,12},{12,16},{16,20},{20,24},{24,28},{28,32},{32,36}... | collective-permute-start | bytes 589832 | tf_op jit(solution)/shard_map/ppermute | solution.py:363
  63.7 2.7 %collective-permute-start.4 = (bf16[1,2,3,128,128]{4,3,2,1,0:T(8,128)(2,1)S(1)}, bf16[1,2,3,128,128]{4,3,2,1,0:T(8,128)(2,1)S(1)}, u32[]{:S(2)}, u32[]{:S(2)}) collective-permute-start(bf16[1,2,3,128,128]{4,3,2,1,0:T(8,128)(2,1)S(1)} %pack.11.refs_5_), channel_id=1, source_target_pairs={{0,4},{4,8},{8,12},{12,16},{16,20},{20,24},{24,28},{28,32},{32,36}... | collective-permute-start | bytes 589832 | tf_op jit(solution)/shard_map/ppermute | solution.py:363
  66.4 0.0 collective-permute-done.10.refs_9_
  66.5 0.7 collective-permute-start.11
  67.1 2.1 %collective-permute-done.9.refs_8_.refs_5_ = bf16[544,128]{1,0:T(8,128)(2,1)S(1)} collective-permute-done((bf16[544,128]{1,0:T(8,128)(2,1)S(1)}, bf16[544,128]{1,0:T(8,128)(2,1)S(1)}, u32[]{:S(2)}, u32[]{:S(2)}) %collective-permute-start.9) | collective-permute-done | bytes 139296 | tf_op jit(solution)/shard_map/ppermute | solution.py:392
  69.2 1.1 %chunk.12.refs_7_.refs_3_ = f32[128,128]{1,0:T(8,128)S(1)} custom-call(bf16[8,2,2,512,128]{4,3,2,1,0:T(8,128)(2,1)S(1)} %bitcast.26, f32[512,128]{1,0:T(8,128)S(1)} %bitcast.35, bf16[256,256]{1,0:T(8,128)(2,1)S(1)} %copy-done.3, bf16[256,256]{1,0:T(8,128)(2,1)S(1)} %copy-done.2, f32[128,128]{1,0:T(8,128)S(1)} %copy-done.4, f32[128,128]{1,0:T(8,128)S(1)} %copy-done.5, ...), custom_call_target="tpu_custom_call" | custom-call | flops 314572800 | bytes 1048576 | tf_op jit(solution)/shard_map/chunk/pallas_call | solution.py:304
  70.3 0.0 collective-permute-done.6.refs_6_
  70.3 1.1 %chunk.13.refs_7_.refs_4_.refs_10_ = f32[128,128]{1,0:T(8,128)S(1)} custom-call(bf16[8,2,2,512,128]{4,3,2,1,0:T(8,128)(2,1)S(1)} %bitcast.27, f32[512,128]{1,0:T(8,128)S(1)} %bitcast.36, bf16[256,256]{1,0:T(8,128)(2,1)S(1)} %copy-done.3, bf16[256,256]{1,0:T(8,128)(2,1)S(1)} %copy-done.2, f32[128,128]{1,0:T(8,128)S(1)} %copy-done.4, ...), custom_call_target="tpu_custom_call" | custom-call | flops 314572800 | bytes 1048576 | tf_op jit(solution)/shard_map/chunk/pallas_call | solution.py:304
  71.3 2.9 %collective-permute-done.5.refs_6_ = bf16[1,2,3,128,128]{4,3,2,1,0:T(8,128)(2,1)S(1)} collective-permute-done((bf16[1,2,3,128,128]{4,3,2,1,0:T(8,128)(2,1)S(1)}, bf16[1,2,3,128,128]{4,3,2,1,0:T(8,128)(2,1)S(1)}, u32[]{:S(2)}, u32[]{:S(2)}) %collective-permute-start.5) | collective-permute-done | bytes 196640 | tf_op jit(solution)/shard_map/ppermute | solution.py:363
  74.2 0.9 chunk_early.1
  75.1 0.2 lay.1.refs_11_
  75.3 2.1 %collective-permute-done.4.refs_6_ = bf16[1,2,3,128,128]{4,3,2,1,0:T(8,128)(2,1)S(1)} collective-permute-done((bf16[1,2,3,128,128]{4,3,2,1,0:T(8,128)(2,1)S(1)}, bf16[1,2,3,128,128]{4,3,2,1,0:T(8,128)(2,1)S(1)}, u32[]{:S(2)}, u32[]{:S(2)}) %collective-permute-start.4) | collective-permute-done | bytes 196640 | tf_op jit(solution)/shard_map/ppermute | solution.py:363
  77.4 0.6 last.1
  78.0 20.7 %all_to_all.5 = bf16[64,9,2,128]{3,2,1,0:T(2,128)(2,1)S(1)} all-to-all(bf16[64,9,2,128]{3,2,1,0:T(2,128)(2,1)S(1)} %bitcast.40), channel_id=1, replica_groups=mesh['half'=2,'tm'=64,'chan'=4] {'tm'}, dimensions={0} | all-to-all | bytes 589824 | tf_op jit(solution)/shard_map/all_to_all | solution.py:432
  98.7 1.2 %tree.1 = f32[2,16,1024]{2,1,0:T(8,128)} custom-call(bf16[1152,128]{1,0:T(8,128)(2,1)S(1)} %bitcast.39), custom_call_target="tpu_custom_call" | custom-call | flops 1048576 | bytes 1048576 | tf_op jit(solution)/shard_map/tree/pallas_call | solution.py:304
  (10 shorter events, 0.0 us)
Async XLA Ops:
  0.0 5.7 %copy-start = (bf16[8,2,2,4,16384]{4,3,2,1,0:T(4,128)(2,1)S(1)}, bf16[8,2,2,4,16384]{4,3,2,1,0:T(4,128)(2,1)}, u32[]{:S(2)}) copy-start(bf16[8,2,2,4,16384]{4,3,2,1,0:T(4,128)(2,1)} %param.6) | copy-start | bytes 12582916
  1.3 17.9 %collective-permute-start.3 = (bf16[2,2,3,128,128]{4,3,2,1,0:T(8,128)(2,1)S(1)}, bf16[2,2,3,128,128]{4,3,2,1,0:T(8,128)(2,1)S(1)}, u32[]{:S(2)}, u32[]{:S(2)}) collective-permute-start(bf16[2,2,3,128,128]{4,3,2,1,0:T(8,128)(2,1)S(1)} %pack_first.1.refs_1_), channel_id=1, source_target_pairs={{0,4},{4,8},{8,12},{12,16},{16,20},{20,24},{24,28},{28,32},{32,36}... | collective-permute-start | bytes 1179656 | tf_op jit(solution)/shard_map/ppermute | solution.py:356
  5.9 13.4 %copy-start.1 = (f32[4,16384]{1,0:T(4,128)S(1)}, f32[4,16384]{1,0:T(4,128)}, u32[]{:S(2)}) copy-start(f32[4,16384]{1,0:T(4,128)} %param.7) | copy-start | bytes 786436
  5.9 13.4 %copy-start.2 = (bf16[256,256]{1,0:T(8,128)(2,1)S(1)}, bf16[256,256]{1,0:T(8,128)(2,1)}, u32[]{:S(2)}) copy-start(bf16[256,256]{1,0:T(8,128)(2,1)} %constant.8.clone.refs_3_) | copy-start | bytes 393220
  5.9 13.3 %copy-start.3 = (bf16[256,256]{1,0:T(8,128)(2,1)S(1)}, bf16[256,256]{1,0:T(8,128)(2,1)}, u32[]{:S(2)}) copy-start(bf16[256,256]{1,0:T(8,128)(2,1)} %constant.9.clone.refs_2_) | copy-start | bytes 393220
  5.9 13.3 %copy-start.4 = (f32[128,128]{1,0:T(8,128)S(1)}, f32[128,128]{1,0:T(8,128)}, u32[]{:S(2)}) copy-start(f32[128,128]{1,0:T(8,128)} %constant.10.clone.refs_4_) | copy-start | bytes 196612
  5.9 13.3 %copy-start.5 = (f32[128,128]{1,0:T(8,128)S(1)}, f32[128,128]{1,0:T(8,128)}, u32[]{:S(2)}) copy-start(f32[128,128]{1,0:T(8,128)} %constant.11.clone.refs_5_) | copy-start | bytes 196612
  6.0 21.7 %collective-permute-start.2 = (bf16[2,2,3,128,128]{4,3,2,1,0:T(8,128)(2,1)S(1)}, bf16[2,2,3,128,128]{4,3,2,1,0:T(8,128)(2,1)S(1)}, u32[]{:S(2)}, u32[]{:S(2)}) collective-permute-start(bf16[2,2,3,128,128]{4,3,2,1,0:T(8,128)(2,1)S(1)} %pack.10), channel_id=1, source_target_pairs={{0,4},{4,8},{8,12},{12,16},{16,20},{20,24},{24,28},{28,32},{32,36}... | collective-permute-start | bytes 1179656 | tf_op jit(solution)/shard_map/ppermute | solution.py:363
  10.5 25.6 %collective-permute-start.1 = (bf16[2,2,3,128,128]{4,3,2,1,0:T(8,128)(2,1)S(1)}, bf16[2,2,3,128,128]{4,3,2,1,0:T(8,128)(2,1)S(1)}, u32[]{:S(2)}, u32[]{:S(2)}) collective-permute-start(bf16[2,2,3,128,128]{4,3,2,1,0:T(8,128)(2,1)S(1)} %pack.9), channel_id=1, source_target_pairs={{0,4},{4,8},{8,12},{12,16},{16,20},{20,24},{24,28},{28,32},{32,36}... | collective-permute-start | bytes 1179656 | tf_op jit(solution)/shard_map/ppermute | solution.py:363
  14.9 29.6 %collective-permute-start = (bf16[2,2,3,128,128]{4,3,2,1,0:T(8,128)(2,1)S(1)}, bf16[2,2,3,128,128]{4,3,2,1,0:T(8,128)(2,1)S(1)}, u32[]{:S(2)}, u32[]{:S(2)}) collective-permute-start(bf16[2,2,3,128,128]{4,3,2,1,0:T(8,128)(2,1)S(1)} %pack.8), channel_id=1, source_target_pairs={{0,4},{4,8},{8,12},{12,16},{16,20},{20,24},{24,28},{28,32},{32,36}... | collective-permute-start | bytes 1179656 | tf_op jit(solution)/shard_map/ppermute | solution.py:363
  20.5 32.5 %collective-permute-start.8 = (bf16[2,2,3,128,128]{4,3,2,1,0:T(8,128)(2,1)S(1)}, bf16[2,2,3,128,128]{4,3,2,1,0:T(8,128)(2,1)S(1)}, u32[]{:S(2)}, u32[]{:S(2)}) collective-permute-start(bf16[2,2,3,128,128]{4,3,2,1,0:T(8,128)(2,1)S(1)} %pack.15), channel_id=1, source_target_pairs={{0,4},{4,8},{8,12},{12,16},{16,20},{20,24},{24,28},{28,32},{32,36}... | collective-permute-start | bytes 1179656 | tf_op jit(solution)/shard_map/ppermute | solution.py:363
  28.9 34.8 %collective-permute-start.7 = (bf16[2,2,3,128,128]{4,3,2,1,0:T(8,128)(2,1)S(1)}, bf16[2,2,3,128,128]{4,3,2,1,0:T(8,128)(2,1)S(1)}, u32[]{:S(2)}, u32[]{:S(2)}) collective-permute-start(bf16[2,2,3,128,128]{4,3,2,1,0:T(8,128)(2,1)S(1)} %pack.14), channel_id=1, source_target_pairs={{0,4},{4,8},{8,12},{12,16},{16,20},{20,24},{24,28},{28,32},{32,36}... | collective-permute-start | bytes 1179656 | tf_op jit(solution)/shard_map/ppermute | solution.py:363
  37.3 32.9 %collective-permute-start.6 = (bf16[2,2,3,128,128]{4,3,2,1,0:T(8,128)(2,1)S(1)}, bf16[2,2,3,128,128]{4,3,2,1,0:T(8,128)(2,1)S(1)}, u32[]{:S(2)}, u32[]{:S(2)}) collective-permute-start(bf16[2,2,3,128,128]{4,3,2,1,0:T(8,128)(2,1)S(1)} %pack.13), channel_id=1, source_target_pairs={{0,4},{4,8},{8,12},{12,16},{16,20},{20,24},{24,28},{28,32},{32,36}... | collective-permute-start | bytes 1179656 | tf_op jit(solution)/shard_map/ppermute | solution.py:363
  54.1 12.4 %collective-permute-start.10 = (bf16[544,128]{1,0:T(8,128)(2,1)S(1)}, bf16[544,128]{1,0:T(8,128)(2,1)S(1)}, u32[]{:S(2)}, u32[]{:S(2)}) collective-permute-start(bf16[544,128]{1,0:T(8,128)(2,1)S(1)} %ship.1), channel_id=1, source_target_pairs={{252,236},{253,237},{254,238},{255,239}} | collective-permute-start | bytes 417800 | tf_op jit(solution)/shard_map/ppermute | solution.py:393
  54.7 14.5 %collective-permute-start.9 = (bf16[544,128]{1,0:T(8,128)(2,1)S(1)}, bf16[544,128]{1,0:T(8,128)(2,1)S(1)}, u32[]{:S(2)}, u32[]{:S(2)}) collective-permute-start(bf16[544,128]{1,0:T(8,128)(2,1)S(1)} %ship.1), channel_id=1, source_target_pairs={{0,320},{4,324},{8,328},{12,332},{16,336},{20,340},{24,344},{28,34... | collective-permute-start | bytes 417800 | tf_op jit(solution)/shard_map/ppermute | solution.py:392
  61.8 12.4 %collective-permute-start.5 = (bf16[1,2,3,128,128]{4,3,2,1,0:T(8,128)(2,1)S(1)}, bf16[1,2,3,128,128]{4,3,2,1,0:T(8,128)(2,1)S(1)}, u32[]{:S(2)}, u32[]{:S(2)}) collective-permute-start(bf16[1,2,3,128,128]{4,3,2,1,0:T(8,128)(2,1)S(1)} %pack.12), channel_id=1, source_target_pairs={{0,4},{4,8},{8,12},{12,16},{16,20},{20,24},{24,28},{28,32},{32,36}... | collective-permute-start | bytes 589832 | tf_op jit(solution)/shard_map/ppermute | solution.py:363
  63.7 13.7 %collective-permute-start.4 = (bf16[1,2,3,128,128]{4,3,2,1,0:T(8,128)(2,1)S(1)}, bf16[1,2,3,128,128]{4,3,2,1,0:T(8,128)(2,1)S(1)}, u32[]{:S(2)}, u32[]{:S(2)}) collective-permute-start(bf16[1,2,3,128,128]{4,3,2,1,0:T(8,128)(2,1)S(1)} %pack.11.refs_5_), channel_id=1, source_target_pairs={{0,4},{4,8},{8,12},{12,16},{16,20},{20,24},{24,28},{28,32},{32,36}... | collective-permute-start | bytes 589832 | tf_op jit(solution)/shard_map/ppermute | solution.py:363
  66.5 8.7 %collective-permute-start.11 = (bf16[544,128]{1,0:T(8,128)(2,1)S(1)}, bf16[544,128]{1,0:T(8,128)(2,1)S(1)}, u32[]{:S(2)}, u32[]{:S(2)}) collective-permute-start(bf16[544,128]{1,0:T(8,128)(2,1)S(1)} %collective-permute-done.10.refs_9_), channel_id=1, source_target_pairs={{236,316},{237,317},{238,318},{239,319}} | collective-permute-start | bytes 417800 | tf_op jit(solution)/shard_map/ppermute | solution.py:394

commit v8 on v7

--- a/solution.py
+++ b/solution.py
@@ -221,6 +221,8 @@
     ins, (late, part, sums_ref, border, p6, laid), out_ref, same_ref = refs[:6], refs[6:12], refs[12], refs[13]
     wide, tall, every = refs[14:]
     half = lax.axis_index("half")
+    settled = SIDE // 8 * 2 * SENT * 2 - 16
+    out_ref[pl.ds(0, settled), :] = same_ref[pl.ds(0, settled), :].astype(jnp.bfloat16)
     value = (part[...] + late_power(ins, late, sums_ref, wide, tall)).T
     every[pl.ds(8, SIDE), :] = value
     zero = jnp.zeros((8, SIDE), jnp.float32)
@@ -238,7 +240,8 @@
         row = pl.ds(3 * group * stride + 8, 1)
         same_ref[row, :] = jnp.where(lane < SIDE // 2, same_ref[row, :], value[SIDE - 1 :])
 
-    out_ref[...] = same_ref[pl.ds(0, out_ref.shape[0]), :].astype(jnp.bfloat16)
+    rest = pl.ds(settled, out_ref.shape[0] - settled)
+    out_ref[rest, :] = same_ref[rest, :].astype(jnp.bfloat16)
 
 
 def tree_kernel(scale, in_ref, out_ref, wide, steps, flat):

time: 100 us -> 100 us (level)
  no operation moved by 1% of the time
where the time goes in v8:
time: 100 us; the launch traced here: 99.9 us
  starting transfers between devices  33.7 us (34%)
  waiting for transfers between devices  32.5 us (32%)
  blocking collectives  20.7 us (21%)
  Pallas kernels  12.7 us (13%)
    ppermute x8, waiting for transfers between devices, send(): near[place].append(lax.ppermute(value, ('half', 'tm'), pairs))  28.1 us
    ppermute x8, starting transfers between devices, send(): near[place].append(lax.ppermute(value, ('half', 'tm'), pairs))  21 us
    all_to_all x1, blocking collectives, per_device(): lax.all_to_all(out, 'tm', split_axis=0, concat_axis=0, tiled=True)  20.7 us
    pallas_call x21, Pallas kernels, call(): pl.pallas_call(ordered, in_specs=(specs or [VMEM] * len(args)) + [ANY] *...  12.7 us
    ppermute x1, starting transfers between devices, per_device(): theirs = lax.ppermute(ship, ('half', 'tm'), straight)  6.95 us
    ppermute x1, starting transfers between devices, per_device(): lax.ppermute(first, ('half', 'tm'), pairs)  4.41 us
    ppermute x1, waiting for transfers between devices, per_device(): lax.ppermute(first, ('half', 'tm'), pairs)  2.39 us
    ppermute x1, waiting for transfers between devices, per_device(): theirs = lax.ppermute(ship, ('half', 'tm'), straight)  2.05 us
  transfers between devices with their start and end apart: 12, of which 8 were waited for; matrix products, arithmetic and copies ran while one was open for 0% of the time, Pallas kernels for 10%

profile of v8, /device:TPU:2, one launch (start us, length us, event | category | flops | bytes accessed | tf_op | source)
XLA Modules:
  0.0 99.9 jit_solution(3510147954138136803)
XLA Ops:
  0.0 1.3 %pack_first.1.refs_1_ = bf16[2,2,3,128,128]{4,3,2,1,0:T(8,128)(2,1)S(1)} custom-call(bf16[8,2,2,512,128]{4,3,2,1,0:T(8,128)(2,1)} %bitcast.12), custom_call_target="tpu_custom_call" | custom-call | flops 1048576 | bytes 1048576 | tf_op jit(solution)/shard_map/pack_first/pallas_call | solution.py:307
  1.3 4.4 %collective-permute-start.3 = (bf16[2,2,3,128,128]{4,3,2,1,0:T(8,128)(2,1)S(1)}, bf16[2,2,3,128,128]{4,3,2,1,0:T(8,128)(2,1)S(1)}, u32[]{:S(2)}, u32[]{:S(2)}) collective-permute-start(bf16[2,2,3,128,128]{4,3,2,1,0:T(8,128)(2,1)S(1)} %pack_first.1.refs_1_), channel_id=1, source_target_pairs={{0,4},{4,8},{8,12},{12,16},{16,20},{20,24},{24,28},{28,32},{32,36}... | collective-permute-start | bytes 1179656 | tf_op jit(solution)/shard_map/ppermute | solution.py:359
  5.7 0.1 pack.10
  5.9 0.0 copy-start.1
  5.9 0.0 copy-start.2
  5.9 0.0 copy-start.3
  5.9 0.0 copy-start.4
  5.9 0.0 copy-start.5
  6.0 4.4 %collective-permute-start.2 = (bf16[2,2,3,128,128]{4,3,2,1,0:T(8,128)(2,1)S(1)}, bf16[2,2,3,128,128]{4,3,2,1,0:T(8,128)(2,1)S(1)}, u32[]{:S(2)}, u32[]{:S(2)}) collective-permute-start(bf16[2,2,3,128,128]{4,3,2,1,0:T(8,128)(2,1)S(1)} %pack.10), channel_id=1, source_target_pairs={{0,4},{4,8},{8,12},{12,16},{16,20},{20,24},{24,28},{28,32},{32,36}... | collective-permute-start | bytes 1179656 | tf_op jit(solution)/shard_map/ppermute | solution.py:366
  10.4 0.1 pack.9
  10.5 4.3 %collective-permute-start.1 = (bf16[2,2,3,128,128]{4,3,2,1,0:T(8,128)(2,1)S(1)}, bf16[2,2,3,128,128]{4,3,2,1,0:T(8,128)(2,1)S(1)}, u32[]{:S(2)}, u32[]{:S(2)}) collective-permute-start(bf16[2,2,3,128,128]{4,3,2,1,0:T(8,128)(2,1)S(1)} %pack.9), channel_id=1, source_target_pairs={{0,4},{4,8},{8,12},{12,16},{16,20},{20,24},{24,28},{28,32},{32,36}... | collective-permute-start | bytes 1179656 | tf_op jit(solution)/shard_map/ppermute | solution.py:366
  14.8 0.1 pack.8
  14.9 1.9 %collective-permute-start = (bf16[2,2,3,128,128]{4,3,2,1,0:T(8,128)(2,1)S(1)}, bf16[2,2,3,128,128]{4,3,2,1,0:T(8,128)(2,1)S(1)}, u32[]{:S(2)}, u32[]{:S(2)}) collective-permute-start(bf16[2,2,3,128,128]{4,3,2,1,0:T(8,128)(2,1)S(1)} %pack.8), channel_id=1, source_target_pairs={{0,4},{4,8},{8,12},{12,16},{16,20},{20,24},{24,28},{28,32},{32,36}... | collective-permute-start | bytes 1179656 | tf_op jit(solution)/shard_map/ppermute | solution.py:366
  16.9 2.4 %collective-permute-done.3.refs_6_ = bf16[2,2,3,128,128]{4,3,2,1,0:T(8,128)(2,1)S(1)} collective-permute-done((bf16[2,2,3,128,128]{4,3,2,1,0:T(8,128)(2,1)S(1)}, bf16[2,2,3,128,128]{4,3,2,1,0:T(8,128)(2,1)S(1)}, u32[]{:S(2)}, u32[]{:S(2)}) %collective-permute-start.3) | collective-permute-done | bytes 393248 | tf_op jit(solution)/shard_map/ppermute | solution.py:359
  19.3 1.1 %chunk.7.refs_7_.refs_1_.refs_0_ = f32[128,128]{1,0:T(8,128)S(1)} custom-call(bf16[8,2,2,512,128]{4,3,2,1,0:T(8,128)(2,1)S(1)} %bitcast.16, f32[512,128]{1,0:T(8,128)S(1)} %bitcast.30, bf16[256,256]{1,0:T(8,128)(2,1)S(1)} %copy-done.3, bf16[256,256]{1,0:T(8,128)(2,1)S(1)} %copy-done.2, f32[128,128]{1,0:T(8,128)S(1)} %copy-done.4, f32[128,128]{1,0:T(8,128)S(1)} %copy-done.5, ...), custom_call_target="tpu_custom_call" | custom-call | flops 314572800 | bytes 1048576 | tf_op jit(solution)/shard_map/chunk/pallas_call | solution.py:307
  20.4 0.1 pack.15
  20.5 1.9 %collective-permute-start.8 = (bf16[2,2,3,128,128]{4,3,2,1,0:T(8,128)(2,1)S(1)}, bf16[2,2,3,128,128]{4,3,2,1,0:T(8,128)(2,1)S(1)}, u32[]{:S(2)}, u32[]{:S(2)}) collective-permute-start(bf16[2,2,3,128,128]{4,3,2,1,0:T(8,128)(2,1)S(1)} %pack.15), channel_id=1, source_target_pairs={{0,4},{4,8},{8,12},{12,16},{16,20},{20,24},{24,28},{28,32},{32,36}... | collective-permute-start | bytes 1179656 | tf_op jit(solution)/shard_map/ppermute | solution.py:366
  22.4 5.3 %collective-permute-done.2.refs_6_ = bf16[2,2,3,128,128]{4,3,2,1,0:T(8,128)(2,1)S(1)} collective-permute-done((bf16[2,2,3,128,128]{4,3,2,1,0:T(8,128)(2,1)S(1)}, bf16[2,2,3,128,128]{4,3,2,1,0:T(8,128)(2,1)S(1)}, u32[]{:S(2)}, u32[]{:S(2)}) %collective-permute-start.2) | collective-permute-done | bytes 393248 | tf_op jit(solution)/shard_map/ppermute | solution.py:366
  27.7 1.1 %chunk.8.refs_7_.refs_1_ = f32[128,128]{1,0:T(8,128)S(1)} custom-call(bf16[8,2,2,512,128]{4,3,2,1,0:T(8,128)(2,1)S(1)} %bitcast.18, f32[512,128]{1,0:T(8,128)S(1)} %bitcast.31, bf16[256,256]{1,0:T(8,128)(2,1)S(1)} %copy-done.3, bf16[256,256]{1,0:T(8,128)(2,1)S(1)} %copy-done.2, f32[128,128]{1,0:T(8,128)S(1)} %copy-done.4, f32[128,128]{1,0:T(8,128)S(1)} %copy-done.5, ...), custom_call_target="tpu_custom_call" | custom-call | flops 314572800 | bytes 1048576 | tf_op jit(solution)/shard_map/chunk/pallas_call | solution.py:307
  28.7 0.1 pack.14
  28.9 1.9 %collective-permute-start.7 = (bf16[2,2,3,128,128]{4,3,2,1,0:T(8,128)(2,1)S(1)}, bf16[2,2,3,128,128]{4,3,2,1,0:T(8,128)(2,1)S(1)}, u32[]{:S(2)}, u32[]{:S(2)}) collective-permute-start(bf16[2,2,3,128,128]{4,3,2,1,0:T(8,128)(2,1)S(1)} %pack.14), channel_id=1, source_target_pairs={{0,4},{4,8},{8,12},{12,16},{16,20},{20,24},{24,28},{28,32},{32,36}... | collective-permute-start | bytes 1179656 | tf_op jit(solution)/shard_map/ppermute | solution.py:366
  30.8 5.3 %collective-permute-done.1.refs_6_ = bf16[2,2,3,128,128]{4,3,2,1,0:T(8,128)(2,1)S(1)} collective-permute-done((bf16[2,2,3,128,128]{4,3,2,1,0:T(8,128)(2,1)S(1)}, bf16[2,2,3,128,128]{4,3,2,1,0:T(8,128)(2,1)S(1)}, u32[]{:S(2)}, u32[]{:S(2)}) %collective-permute-start.1) | collective-permute-done | bytes 393248 | tf_op jit(solution)/shard_map/ppermute | solution.py:366
  36.1 1.1 %chunk.9.refs_7_.refs_1_.refs_2_ = f32[128,128]{1,0:T(8,128)S(1)} custom-call(bf16[8,2,2,512,128]{4,3,2,1,0:T(8,128)(2,1)S(1)} %bitcast.20, f32[512,128]{1,0:T(8,128)S(1)} %bitcast.32, bf16[256,256]{1,0:T(8,128)(2,1)S(1)} %copy-done.3, bf16[256,256]{1,0:T(8,128)(2,1)S(1)} %copy-done.2, f32[128,128]{1,0:T(8,128)S(1)} %copy-done.4, f32[128,128]{1,0:T(8,128)S(1)} %copy-done.5, ...), custom_call_target="tpu_custom_call" | custom-call | flops 314572800 | bytes 1048576 | tf_op jit(solution)/shard_map/chunk/pallas_call | solution.py:307
  37.2 0.1 pack.13
  37.3 1.9 %collective-permute-start.6 = (bf16[2,2,3,128,128]{4,3,2,1,0:T(8,128)(2,1)S(1)}, bf16[2,2,3,128,128]{4,3,2,1,0:T(8,128)(2,1)S(1)}, u32[]{:S(2)}, u32[]{:S(2)}) collective-permute-start(bf16[2,2,3,128,128]{4,3,2,1,0:T(8,128)(2,1)S(1)} %pack.13), channel_id=1, source_target_pairs={{0,4},{4,8},{8,12},{12,16},{16,20},{20,24},{24,28},{28,32},{32,36}... | collective-permute-start | bytes 1179656 | tf_op jit(solution)/shard_map/ppermute | solution.py:366
  39.2 5.3 %collective-permute-done.refs_6_ = bf16[2,2,3,128,128]{4,3,2,1,0:T(8,128)(2,1)S(1)} collective-permute-done((bf16[2,2,3,128,128]{4,3,2,1,0:T(8,128)(2,1)S(1)}, bf16[2,2,3,128,128]{4,3,2,1,0:T(8,128)(2,1)S(1)}, u32[]{:S(2)}, u32[]{:S(2)}) %collective-permute-start) | collective-permute-done | bytes 393248 | tf_op jit(solution)/shard_map/ppermute | solution.py:366
  44.5 1.1 %chunk.10.refs_1_.refs_7_.refs_3_ = f32[128,128]{1,0:T(8,128)S(1)} custom-call(bf16[8,2,2,512,128]{4,3,2,1,0:T(8,128)(2,1)S(1)} %bitcast.22, f32[512,128]{1,0:T(8,128)S(1)} %bitcast.33, bf16[256,256]{1,0:T(8,128)(2,1)S(1)} %copy-done.3, bf16[256,256]{1,0:T(8,128)(2,1)S(1)} %copy-done.2, f32[128,128]{1,0:T(8,128)S(1)} %copy-done.4, f32[128,128]{1,0:T(8,128)S(1)} %copy-done.5, ...), custom_call_target="tpu_custom_call" | custom-call | flops 314572800 | bytes 1048576 | tf_op jit(solution)/shard_map/chunk/pallas_call | solution.py:307
  45.6 0.1 pack.11.refs_5_
  45.7 7.3 %collective-permute-done.8.refs_6_ = bf16[2,2,3,128,128]{4,3,2,1,0:T(8,128)(2,1)S(1)} collective-permute-done((bf16[2,2,3,128,128]{4,3,2,1,0:T(8,128)(2,1)S(1)}, bf16[2,2,3,128,128]{4,3,2,1,0:T(8,128)(2,1)S(1)}, u32[]{:S(2)}, u32[]{:S(2)}) %collective-permute-start.8) | collective-permute-done | bytes 393248 | tf_op jit(solution)/shard_map/ppermute | solution.py:366
  53.0 1.1 %chunk.11.refs_4_.refs_7_.refs_2_.refs_9_ = f32[128,128]{1,0:T(8,128)S(1)} custom-call(bf16[8,2,2,512,128]{4,3,2,1,0:T(8,128)(2,1)S(1)} %bitcast.24, f32[512,128]{1,0:T(8,128)S(1)} %bitcast.34, bf16[256,256]{1,0:T(8,128)(2,1)S(1)} %copy-done.3, bf16[256,256]{1,0:T(8,128)(2,1)S(1)} %copy-done.2, f32[128,128]{1,0:T(8,128)S(1)} %copy-done.4, ...), custom_call_target="tpu_custom_call" | custom-call | flops 314572800 | bytes 1048576 | tf_op jit(solution)/shard_map/chunk/pallas_call | solution.py:307
  54.1 0.7 collective-permute-start.10
  54.7 6.9 %collective-permute-start.9 = (bf16[544,128]{1,0:T(8,128)(2,1)S(1)}, bf16[544,128]{1,0:T(8,128)(2,1)S(1)}, u32[]{:S(2)}, u32[]{:S(2)}) collective-permute-start(bf16[544,128]{1,0:T(8,128)(2,1)S(1)} %ship.1), channel_id=1, source_target_pairs={{0,320},{4,324},{8,328},{12,332},{16,336},{20,340},{24,344},{28,34... | collective-permute-start | bytes 417800 | tf_op jit(solution)/shard_map/ppermute | solution.py:395
  61.7 0.1 pack.12
  61.8 1.9 %collective-permute-start.5 = (bf16[1,2,3,128,128]{4,3,2,1,0:T(8,128)(2,1)S(1)}, bf16[1,2,3,128,128]{4,3,2,1,0:T(8,128)(2,1)S(1)}, u32[]{:S(2)}, u32[]{:S(2)}) collective-permute-start(bf16[1,2,3,128,128]{4,3,2,1,0:T(8,128)(2,1)S(1)} %pack.12), channel_id=1, source_target_pairs={{0,4},{4,8},{8,12},{12,16},{16,20},{20,24},{24,28},{28,32},{32,36}... | collective-permute-start | bytes 589832 | tf_op jit(solution)/shard_map/ppermute | solution.py:366
  63.7 2.7 %collective-permute-start.4 = (bf16[1,2,3,128,128]{4,3,2,1,0:T(8,128)(2,1)S(1)}, bf16[1,2,3,128,128]{4,3,2,1,0:T(8,128)(2,1)S(1)}, u32[]{:S(2)}, u32[]{:S(2)}) collective-permute-start(bf16[1,2,3,128,128]{4,3,2,1,0:T(8,128)(2,1)S(1)} %pack.11.refs_5_), channel_id=1, source_target_pairs={{0,4},{4,8},{8,12},{12,16},{16,20},{20,24},{24,28},{28,32},{32,36}... | collective-permute-start | bytes 589832 | tf_op jit(solution)/shard_map/ppermute | solution.py:366
  66.4 0.0 collective-permute-done.10.refs_9_
  66.5 0.7 collective-permute-start.11
  67.1 2.1 %collective-permute-done.9.refs_8_.refs_5_ = bf16[544,128]{1,0:T(8,128)(2,1)S(1)} collective-permute-done((bf16[544,128]{1,0:T(8,128)(2,1)S(1)}, bf16[544,128]{1,0:T(8,128)(2,1)S(1)}, u32[]{:S(2)}, u32[]{:S(2)}) %collective-permute-start.9) | collective-permute-done | bytes 139296 | tf_op jit(solution)/shard_map/ppermute | solution.py:395
  69.2 1.1 %chunk.12.refs_7_.refs_3_ = f32[128,128]{1,0:T(8,128)S(1)} custom-call(bf16[8,2,2,512,128]{4,3,2,1,0:T(8,128)(2,1)S(1)} %bitcast.26, f32[512,128]{1,0:T(8,128)S(1)} %bitcast.35, bf16[256,256]{1,0:T(8,128)(2,1)S(1)} %copy-done.3, bf16[256,256]{1,0:T(8,128)(2,1)S(1)} %copy-done.2, f32[128,128]{1,0:T(8,128)S(1)} %copy-done.4, f32[128,128]{1,0:T(8,128)S(1)} %copy-done.5, ...), custom_call_target="tpu_custom_call" | custom-call | flops 314572800 | bytes 1048576 | tf_op jit(solution)/shard_map/chunk/pallas_call | solution.py:307
  70.3 0.0 collective-permute-done.6.refs_6_
  70.3 1.1 %chunk.13.refs_7_.refs_4_.refs_10_ = f32[128,128]{1,0:T(8,128)S(1)} custom-call(bf16[8,2,2,512,128]{4,3,2,1,0:T(8,128)(2,1)S(1)} %bitcast.27, f32[512,128]{1,0:T(8,128)S(1)} %bitcast.36, bf16[256,256]{1,0:T(8,128)(2,1)S(1)} %copy-done.3, bf16[256,256]{1,0:T(8,128)(2,1)S(1)} %copy-done.2, f32[128,128]{1,0:T(8,128)S(1)} %copy-done.4, ...), custom_call_target="tpu_custom_call" | custom-call | flops 314572800 | bytes 1048576 | tf_op jit(solution)/shard_map/chunk/pallas_call | solution.py:307
  71.3 2.9 %collective-permute-done.5.refs_6_ = bf16[1,2,3,128,128]{4,3,2,1,0:T(8,128)(2,1)S(1)} collective-permute-done((bf16[1,2,3,128,128]{4,3,2,1,0:T(8,128)(2,1)S(1)}, bf16[1,2,3,128,128]{4,3,2,1,0:T(8,128)(2,1)S(1)}, u32[]{:S(2)}, u32[]{:S(2)}) %collective-permute-start.5) | collective-permute-done | bytes 196640 | tf_op jit(solution)/shard_map/ppermute | solution.py:366
  74.2 0.9 chunk_early.1
  75.1 0.2 lay.1.refs_11_
  75.3 2.1 %collective-permute-done.4.refs_6_ = bf16[1,2,3,128,128]{4,3,2,1,0:T(8,128)(2,1)S(1)} collective-permute-done((bf16[1,2,3,128,128]{4,3,2,1,0:T(8,128)(2,1)S(1)}, bf16[1,2,3,128,128]{4,3,2,1,0:T(8,128)(2,1)S(1)}, u32[]{:S(2)}, u32[]{:S(2)}) %collective-permute-start.4) | collective-permute-done | bytes 196640 | tf_op jit(solution)/shard_map/ppermute | solution.py:366
  77.4 0.6 last.1
  78.0 20.7 %all_to_all.5 = bf16[64,9,2,128]{3,2,1,0:T(2,128)(2,1)S(1)} all-to-all(bf16[64,9,2,128]{3,2,1,0:T(2,128)(2,1)S(1)} %bitcast.40), channel_id=1, replica_groups=mesh['half'=2,'tm'=64,'chan'=4] {'tm'}, dimensions={0} | all-to-all | bytes 589824 | tf_op jit(solution)/shard_map/all_to_all | solution.py:435
  98.7 1.2 %tree.1 = f32[2,16,1024]{2,1,0:T(8,128)} custom-call(bf16[1152,128]{1,0:T(8,128)(2,1)S(1)} %bitcast.39), custom_call_target="tpu_custom_call" | custom-call | flops 1048576 | bytes 1048576 | tf_op jit(solution)/shard_map/tree/pallas_call | solution.py:307
  (10 shorter events, 0.0 us)
Async XLA Ops:
  0.0 5.7 %copy-start = (bf16[8,2,2,4,16384]{4,3,2,1,0:T(4,128)(2,1)S(1)}, bf16[8,2,2,4,16384]{4,3,2,1,0:T(4,128)(2,1)}, u32[]{:S(2)}) copy-start(bf16[8,2,2,4,16384]{4,3,2,1,0:T(4,128)(2,1)} %param.6) | copy-start | bytes 12582916
  1.3 17.9 %collective-permute-start.3 = (bf16[2,2,3,128,128]{4,3,2,1,0:T(8,128)(2,1)S(1)}, bf16[2,2,3,128,128]{4,3,2,1,0:T(8,128)(2,1)S(1)}, u32[]{:S(2)}, u32[]{:S(2)}) collective-permute-start(bf16[2,2,3,128,128]{4,3,2,1,0:T(8,128)(2,1)S(1)} %pack_first.1.refs_1_), channel_id=1, source_target_pairs={{0,4},{4,8},{8,12},{12,16},{16,20},{20,24},{24,28},{28,32},{32,36}... | collective-permute-start | bytes 1179656 | tf_op jit(solution)/shard_map/ppermute | solution.py:359
  5.9 13.4 %copy-start.1 = (f32[4,16384]{1,0:T(4,128)S(1)}, f32[4,16384]{1,0:T(4,128)}, u32[]{:S(2)}) copy-start(f32[4,16384]{1,0:T(4,128)} %param.7) | copy-start | bytes 786436
  5.9 13.4 %copy-start.2 = (bf16[256,256]{1,0:T(8,128)(2,1)S(1)}, bf16[256,256]{1,0:T(8,128)(2,1)}, u32[]{:S(2)}) copy-start(bf16[256,256]{1,0:T(8,128)(2,1)} %constant.8.clone.refs_3_) | copy-start | bytes 393220
  5.9 13.3 %copy-start.3 = (bf16[256,256]{1,0:T(8,128)(2,1)S(1)}, bf16[256,256]{1,0:T(8,128)(2,1)}, u32[]{:S(2)}) copy-start(bf16[256,256]{1,0:T(8,128)(2,1)} %constant.9.clone.refs_2_) | copy-start | bytes 393220
  5.9 13.3 %copy-start.4 = (f32[128,128]{1,0:T(8,128)S(1)}, f32[128,128]{1,0:T(8,128)}, u32[]{:S(2)}) copy-start(f32[128,128]{1,0:T(8,128)} %constant.10.clone.refs_4_) | copy-start | bytes 196612
  5.9 13.3 %copy-start.5 = (f32[128,128]{1,0:T(8,128)S(1)}, f32[128,128]{1,0:T(8,128)}, u32[]{:S(2)}) copy-start(f32[128,128]{1,0:T(8,128)} %constant.11.clone.refs_5_) | copy-start | bytes 196612
  6.0 21.7 %collective-permute-start.2 = (bf16[2,2,3,128,128]{4,3,2,1,0:T(8,128)(2,1)S(1)}, bf16[2,2,3,128,128]{4,3,2,1,0:T(8,128)(2,1)S(1)}, u32[]{:S(2)}, u32[]{:S(2)}) collective-permute-start(bf16[2,2,3,128,128]{4,3,2,1,0:T(8,128)(2,1)S(1)} %pack.10), channel_id=1, source_target_pairs={{0,4},{4,8},{8,12},{12,16},{16,20},{20,24},{24,28},{28,32},{32,36}... | collective-permute-start | bytes 1179656 | tf_op jit(solution)/shard_map/ppermute | solution.py:366
  10.5 25.6 %collective-permute-start.1 = (bf16[2,2,3,128,128]{4,3,2,1,0:T(8,128)(2,1)S(1)}, bf16[2,2,3,128,128]{4,3,2,1,0:T(8,128)(2,1)S(1)}, u32[]{:S(2)}, u32[]{:S(2)}) collective-permute-start(bf16[2,2,3,128,128]{4,3,2,1,0:T(8,128)(2,1)S(1)} %pack.9), channel_id=1, source_target_pairs={{0,4},{4,8},{8,12},{12,16},{16,20},{20,24},{24,28},{28,32},{32,36}... | collective-permute-start | bytes 1179656 | tf_op jit(solution)/shard_map/ppermute | solution.py:366
  14.9 29.6 %collective-permute-start = (bf16[2,2,3,128,128]{4,3,2,1,0:T(8,128)(2,1)S(1)}, bf16[2,2,3,128,128]{4,3,2,1,0:T(8,128)(2,1)S(1)}, u32[]{:S(2)}, u32[]{:S(2)}) collective-permute-start(bf16[2,2,3,128,128]{4,3,2,1,0:T(8,128)(2,1)S(1)} %pack.8), channel_id=1, source_target_pairs={{0,4},{4,8},{8,12},{12,16},{16,20},{20,24},{24,28},{28,32},{32,36}... | collective-permute-start | bytes 1179656 | tf_op jit(solution)/shard_map/ppermute | solution.py:366
  20.5 32.5 %collective-permute-start.8 = (bf16[2,2,3,128,128]{4,3,2,1,0:T(8,128)(2,1)S(1)}, bf16[2,2,3,128,128]{4,3,2,1,0:T(8,128)(2,1)S(1)}, u32[]{:S(2)}, u32[]{:S(2)}) collective-permute-start(bf16[2,2,3,128,128]{4,3,2,1,0:T(8,128)(2,1)S(1)} %pack.15), channel_id=1, source_target_pairs={{0,4},{4,8},{8,12},{12,16},{16,20},{20,24},{24,28},{28,32},{32,36}... | collective-permute-start | bytes 1179656 | tf_op jit(solution)/shard_map/ppermute | solution.py:366
  28.9 34.8 %collective-permute-start.7 = (bf16[2,2,3,128,128]{4,3,2,1,0:T(8,128)(2,1)S(1)}, bf16[2,2,3,128,128]{4,3,2,1,0:T(8,128)(2,1)S(1)}, u32[]{:S(2)}, u32[]{:S(2)}) collective-permute-start(bf16[2,2,3,128,128]{4,3,2,1,0:T(8,128)(2,1)S(1)} %pack.14), channel_id=1, source_target_pairs={{0,4},{4,8},{8,12},{12,16},{16,20},{20,24},{24,28},{28,32},{32,36}... | collective-permute-start | bytes 1179656 | tf_op jit(solution)/shard_map/ppermute | solution.py:366
  37.3 32.9 %collective-permute-start.6 = (bf16[2,2,3,128,128]{4,3,2,1,0:T(8,128)(2,1)S(1)}, bf16[2,2,3,128,128]{4,3,2,1,0:T(8,128)(2,1)S(1)}, u32[]{:S(2)}, u32[]{:S(2)}) collective-permute-start(bf16[2,2,3,128,128]{4,3,2,1,0:T(8,128)(2,1)S(1)} %pack.13), channel_id=1, source_target_pairs={{0,4},{4,8},{8,12},{12,16},{16,20},{20,24},{24,28},{28,32},{32,36}... | collective-permute-start | bytes 1179656 | tf_op jit(solution)/shard_map/ppermute | solution.py:366
  54.1 12.4 %collective-permute-start.10 = (bf16[544,128]{1,0:T(8,128)(2,1)S(1)}, bf16[544,128]{1,0:T(8,128)(2,1)S(1)}, u32[]{:S(2)}, u32[]{:S(2)}) collective-permute-start(bf16[544,128]{1,0:T(8,128)(2,1)S(1)} %ship.1), channel_id=1, source_target_pairs={{252,236},{253,237},{254,238},{255,239}} | collective-permute-start | bytes 417800 | tf_op jit(solution)/shard_map/ppermute | solution.py:396
  54.7 14.5 %collective-permute-start.9 = (bf16[544,128]{1,0:T(8,128)(2,1)S(1)}, bf16[544,128]{1,0:T(8,128)(2,1)S(1)}, u32[]{:S(2)}, u32[]{:S(2)}) collective-permute-start(bf16[544,128]{1,0:T(8,128)(2,1)S(1)} %ship.1), channel_id=1, source_target_pairs={{0,320},{4,324},{8,328},{12,332},{16,336},{20,340},{24,344},{28,34... | collective-permute-start | bytes 417800 | tf_op jit(solution)/shard_map/ppermute | solution.py:395
  61.8 12.4 %collective-permute-start.5 = (bf16[1,2,3,128,128]{4,3,2,1,0:T(8,128)(2,1)S(1)}, bf16[1,2,3,128,128]{4,3,2,1,0:T(8,128)(2,1)S(1)}, u32[]{:S(2)}, u32[]{:S(2)}) collective-permute-start(bf16[1,2,3,128,128]{4,3,2,1,0:T(8,128)(2,1)S(1)} %pack.12), channel_id=1, source_target_pairs={{0,4},{4,8},{8,12},{12,16},{16,20},{20,24},{24,28},{28,32},{32,36}... | collective-permute-start | bytes 589832 | tf_op jit(solution)/shard_map/ppermute | solution.py:366
  63.7 13.7 %collective-permute-start.4 = (bf16[1,2,3,128,128]{4,3,2,1,0:T(8,128)(2,1)S(1)}, bf16[1,2,3,128,128]{4,3,2,1,0:T(8,128)(2,1)S(1)}, u32[]{:S(2)}, u32[]{:S(2)}) collective-permute-start(bf16[1,2,3,128,128]{4,3,2,1,0:T(8,128)(2,1)S(1)} %pack.11.refs_5_), channel_id=1, source_target_pairs={{0,4},{4,8},{8,12},{12,16},{16,20},{20,24},{24,28},{28,32},{32,36}... | collective-permute-start | bytes 589832 | tf_op jit(solution)/shard_map/ppermute | solution.py:366
  66.5 8.7 %collective-permute-start.11 = (bf16[544,128]{1,0:T(8,128)(2,1)S(1)}, bf16[544,128]{1,0:T(8,128)(2,1)S(1)}, u32[]{:S(2)}, u32[]{:S(2)}) collective-permute-start(bf16[544,128]{1,0:T(8,128)(2,1)S(1)} %collective-permute-done.10.refs_9_), channel_id=1, source_target_pairs={{236,316},{237,317},{238,318},{239,319}} | collective-permute-start | bytes 417800 | tf_op jit(solution)/shard_map/ppermute | solution.py:397
